TPU v7x, 128 devices: a whole 4x4x4 slice. The times are simulated.
128 devices in a mesh: lon: 16 (over y, z_lo, core), lat: 8 (over z_hi, x).
Axes of the slice: x: 4, y: 4, z: 4 (z_hi: 2, z_lo: 2; z = z_hi * 2 + z_lo), core: 2. Of those that a mesh axis runs over, the one named last changes fastest.
Arguments:
- tokens: bfloat16 [288, 384, 4, 512], P('lat', 'lon'), may hold values from -6 to 6
- norm1_gain: float32 [512], replicated, may hold values from 0.1 to 1.9
- norm1_bias: float32 [512], replicated, may hold values from -3 to 3
- qkv_weight: bfloat16 [512, 1536], replicated
- rel_bias: float32 [8, 759], replicated, may hold values from -4 to 4
- key_mask: int32 [288, 384], replicated, may hold values from 0 to 1, as said below
- proj_weight: bfloat16 [512, 512], replicated, may hold values from -0.25 to 0.25
- norm2_gain: float32 [512], replicated, may hold values from 0.1 to 1.9
- norm2_bias: float32 [512], replicated, may hold values from -3 to 3
- fc1_weight: bfloat16 [512, 2048], replicated, may hold values from -0.25 to 0.25
- fc2_weight: bfloat16 [2048, 512], replicated, may hold values from -0.125 to 0.125
Outputs:
- block_out: bfloat16 [288, 384, 4, 512], P('lat', 'lon')
Inputs may be any that keep to these rules, and one draw needn't show every extreme that they name: `key_mask`: whole rows next to each pole are 0, and scattered cells elsewhere.
All inputs are finite; a program needn't handle non-finite values.
Results may differ from a plain program's by a relative error of at most 0.0059.
Values may be sent and summed in bfloat16 or wider, within the bound.
No kernel may reach another device: no remote copies, remote signals or barrier semaphores. Data moves between devices by JAX's collectives and lax.ppermute only.
A program may use at most 192 MiB of HBM per device.

v0:
```python
import functools
import math

import jax
import jax.numpy as jnp
import numpy as np
from jax import lax
from jax.experimental import pallas as pl
from jax.experimental.pallas import tpu as pltpu
from jax.sharding import PartitionSpec as P

C = 512
FF = 2048
HEADS = 8
HEAD_DIM = 64
WLEV = 2
WLAT = 6
WLON = 12
LEV = 4
SLAT = 3
SLON = 6
WIN = WLAT * WLON * WLEV
HALF = WIN // 2
QUART = WIN // 4
EPS = 1e-5
LOG2E = math.log2(math.e)
NEG = -jnp.inf
BF = jnp.bfloat16
F32 = jnp.float32
PAIRS = ((1, 2), (3, 0))
VMEM_LIMIT = 56 * 1024 * 1024
ERF = (0.7978281359956358, 0.036468790964347284, -0.00012486163691975404,
       -3.0581006276508824e-05, 1.1190821930105387e-06)


def order_columns():
    first = [(p, 6 * h + q, r) for h in range(2) for r in range(2) for p in range(6) for q in range(6)]
    second = [(3 * h + p, q, r) for h in range(2) for r in range(2) for p in range(3) for q in range(12)]
    return first, second


def lane_pqr(u, which):
    half, r, cell = u // HALF, (u // QUART) % 2, u % QUART
    if which == 0:
        return cell // 6, 6 * half + cell % 6, r
    return 3 * half + cell // 12, cell % 12, r


def prep_kernel(place_ref, table_ref, mask_ref, bias1_ref, bias2_ref, valid_ref, rows_ref, *, shape):
    lat, lon, lats = place_ref[0], place_ref[1], shape[0] // shape[2]
    table = table_ref[...] * LOG2E
    out_refs = (bias1_ref, bias2_ref)
    for which, order in enumerate(order_columns()):
        for t, (p, q, r) in enumerate(order):
            start = p * 69 + q * 3 + r
            rows_ref[8 * t : 8 * t + 8, :] = table[:, start : start + 384]
        rows = rows_ref[...]
        high = rows.astype(BF)
        low = (rows - high.astype(F32)).astype(BF)
        k = lax.broadcasted_iota(jnp.int32, (384, WIN), 0)
        p, q, r = lane_pqr(lax.broadcasted_iota(jnp.int32, (384, WIN), 1), which)
        pick = (k == 379 - (p * 69 + q * 3 + r)).astype(F32).astype(BF)
        full = jnp.dot(high, pick, preferred_element_type=F32) + jnp.dot(low, pick, preferred_element_type=F32)
        full = jnp.transpose(full.reshape(WIN, HEADS, WIN), (1, 0, 2))
        t = lax.broadcasted_iota(jnp.int32, (WIN, WIN), 0)
        u = lax.broadcasted_iota(jnp.int32, (WIN, WIN), 1)
        same = (t // QUART) % 2 == (u // QUART) % 2
        for h in range(HEADS):
            out_refs[which][h, 0] = full[h]
            out_refs[which][h, 1] = jnp.where(same, full[h], NEG)
    nlat, nlon, tile_rows, tile_cols = shape
    row = lax.broadcasted_iota(jnp.int32, (48, nlat), 0)
    col = lax.broadcasted_iota(jnp.int32, (48, nlat), 1)
    want = lax.rem(lat * tile_rows - SLAT + row + nlat, nlat)
    pick_rows = (want == col).astype(F32).astype(BF)
    mask = (mask_ref[...] > 0).astype(F32).astype(BF)
    picked = jnp.dot(pick_rows, mask, preferred_element_type=F32).astype(BF)
    for which in range(2):
        row = lax.broadcasted_iota(jnp.int32, (nlon, 3 * WIN), 0)
        lane = lax.broadcasted_iota(jnp.int32, (nlon, 3 * WIN), 1)
        _, q, _ = lane_pqr(lane % WIN, which)
        want = lax.rem(lon * tile_cols - SLON + 12 * (lane // WIN) + q + nlon, nlon)
        pick_cols = (want == row).astype(F32).astype(BF)
        spread = jnp.dot(picked, pick_cols, preferred_element_type=F32)
        row = lax.broadcasted_iota(jnp.int32, (48, 3 * WIN), 0)
        lane = lax.broadcasted_iota(jnp.int32, (48, 3 * WIN), 1)
        p, _, _ = lane_pqr(lane % WIN, which)
        lane1 = lax.broadcasted_iota(jnp.int32, (1, 3 * WIN), 1)
        for window in (range(1, 6) if which == 0 else (0, 6)):
            value = jnp.sum(jnp.where(row == 6 * window + p, spread, 0.0), axis=0, keepdims=True)
            ok = value > 0.5
            if window == 0:
                ok = ok & ((lat > 0) | (lane1 % WIN >= HALF))
            if window == 6:
                ok = ok & ((lat < lats - 1) | (lane1 % WIN < HALF))
            value = jnp.where(ok, 0.0, NEG)
            for k in range(3):
                valid_ref[3 * window + k] = value[:, k * WIN : (k + 1) * WIN]


def layer_norm(values, gain, offset):
    average = jnp.mean(values, axis=-1, keepdims=True)
    centred = values - average
    spread = jnp.mean(centred * centred, axis=-1, keepdims=True)
    return centred * lax.rsqrt(spread + EPS) * gain + offset


def by_level(block):
    cells = block.astype(F32).reshape(QUART, LEV, C)
    return jnp.transpose(cells, (1, 0, 2))


def from_level(rows, shape):
    return jnp.transpose(rows, (1, 0, 2)).reshape(shape).astype(BF)


def attend(q, k, v, bias_of, block_mask):
    n = q.shape[0]
    head_of = lax.broadcasted_iota(jnp.int32, (1, 256), 1) // HEAD_DIM
    parts = []
    for g in range(2):
        lanes = slice(256 * g, 256 * g + 256)
        qg = q[:, lanes]
        stacked = jnp.concatenate([jnp.where(head_of == j, qg, 0.0) for j in range(4)], axis=0).astype(BF)
        scores = lax.dot_general(stacked, k[:, lanes], (((1,), (1,)), ((), ())), preferred_element_type=F32)
        probs, scale = [], []
        for j in range(4):
            s = scores[j * n : (j + 1) * n] + (bias_of(4 * g + j) + block_mask)
            powered = jnp.exp2(s - jnp.max(s, axis=-1, keepdims=True))
            scale.append(1.0 / jnp.sum(powered, axis=-1, keepdims=True))
            probs.append(powered)
        probs = jnp.concatenate(probs, axis=0).astype(BF)
        out = jnp.dot(probs, v[:, lanes], preferred_element_type=F32)
        context = out[:n] * scale[0]
        for j in range(1, 4):
            context = jnp.where(head_of == j, out[j * n : (j + 1) * n] * scale[j], context)
        parts.append(context)
    return jnp.concatenate(parts, axis=1)


def feed(middle, gain, offset, fc1_ref, fc2_ref):
    normed = layer_norm(middle, gain, offset).astype(BF)
    total = None
    for j in range(4):
        v = jnp.dot(normed, fc1_ref[:, 512 * j : 512 * j + 512], preferred_element_type=F32)
        y = v * v
        poly = ERF[4] * y + ERF[3]
        for c in ERF[2::-1]:
            poly = poly * y + c
        hidden = (v + v * jnp.tanh(v * poly)).astype(BF)
        part = jnp.dot(hidden, fc2_ref[512 * j : 512 * j + 512, :], preferred_element_type=F32)
        total = part if total is None else total + part
    return middle + 0.5 * total


def key_block_mask(valid, first, n):
    t = lax.broadcasted_iota(jnp.int32, (n, WIN), 0) + first
    u = lax.broadcasted_iota(jnp.int32, (n, WIN), 1)
    return jnp.where(t == u, 0.0, jnp.broadcast_to(valid, (n, WIN)))


def inner_kernel(tok_ref, g1_ref, b1_ref, qkv_ref, bias_ref, valid_ref, proj_ref, g2_ref, b2_ref,
                 fc1_ref, fc2_ref, out_ref, xs_ref, q_ref, kv_ref, ctx_ref):
    i = pl.program_id(0)
    x = tok_ref[...]
    for h in range(2):
        levels = by_level(x[:, 6 * h : 6 * h + 6])
        for pair in range(2):
            for r in range(2):
                at = WIN * pair + HALF * h + QUART * r
                xs_ref[at : at + QUART, :] = levels[PAIRS[pair][r]]
    normed = layer_norm(xs_ref[...], g1_ref[...], b1_ref[...]).astype(BF)
    q_ref[...] = jnp.dot(normed, qkv_ref[:, :C], preferred_element_type=F32) * (HEAD_DIM ** -0.5 * LOG2E)
    kv_ref[...] = jnp.dot(normed, qkv_ref[:, C:], preferred_element_type=F32).astype(BF)
    block_mask = key_block_mask(valid_ref[3 * (i + 1) + 1], 0, WIN)
    for pair in range(2):
        rows = slice(WIN * pair, WIN * pair + WIN)
        context = attend(q_ref[rows, :], kv_ref[rows, :C], kv_ref[rows, C:],
                         lambda h: bias_ref[h, pair], block_mask)
        ctx_ref[rows, :] = context.astype(BF)
    moved = jnp.dot(ctx_ref[...], proj_ref[...], preferred_element_type=F32).astype(BF)
    middle = xs_ref[...] + moved.astype(F32)
    xs_ref[...] = feed(middle, g2_ref[...], b2_ref[...], fc1_ref, fc2_ref)
    for h in range(2):
        levels = [None] * LEV
        for pair in range(2):
            for r in range(2):
                at = WIN * pair + HALF * h + QUART * r
                levels[PAIRS[pair][r]] = xs_ref[at : at + QUART, :]
        out_ref[:, 6 * h : 6 * h + 6] = from_level(jnp.stack(levels), (6, 6, LEV, C))


def half_windows(windows, refs, bias_ref, results):
    g1, b1, qkv_ref, proj_ref, g2, b2, fc1_ref, fc2_ref, xs_ref, q_ref, kv_ref, own_ref = refs
    count = len(windows)
    total = 2 * WIN * count
    for w, (own, halo, own_first, _) in enumerate(windows):
        for block, here in ((own, own_first), (halo, not own_first)):
            levels = by_level(block)
            for pair in range(2):
                for r in range(2):
                    at = 2 * WIN * w + WIN * pair + (0 if here else HALF) + QUART * r
                    xs_ref[at : at + QUART, :] = levels[PAIRS[pair][r]]

    def own_rows(array):
        pieces = []
        for w in range(count):
            for pair in range(2):
                at = 2 * WIN * w + WIN * pair + (0 if windows[w][2] else HALF)
                pieces.append(array[at : at + HALF])
        return jnp.concatenate(pieces, axis=0)

    normed = layer_norm(xs_ref[:total, :], g1, b1)
    q_ref[: total // 2, :] = jnp.dot(own_rows(normed).astype(BF), qkv_ref[:, :C], preferred_element_type=F32) * (
        HEAD_DIM ** -0.5 * LOG2E)
    kv_ref[:total, :] = jnp.dot(normed.astype(BF), qkv_ref[:, C:], preferred_element_type=F32).astype(BF)
    contexts = []
    for w in range(count):
        first = 0 if windows[w][2] else HALF
        block_mask = key_block_mask(windows[w][3], first, HALF)
        for pair in range(2):
            at = 2 * WIN * w + WIN * pair
            mine = HALF * (2 * w + pair)
            contexts.append(attend(q_ref[mine : mine + HALF, :], kv_ref[at : at + WIN, :C], kv_ref[at : at + WIN, C:],
                                   lambda h: bias_ref[h, pair, first : first + HALF, :], block_mask))
    context = jnp.concatenate(contexts, axis=0).astype(BF)
    moved = jnp.dot(context, proj_ref[...], preferred_element_type=F32).astype(BF)
    middle = own_rows(xs_ref) + moved.astype(F32)
    own_ref[: total // 2, :] = feed(middle, g2, b2, fc1_ref, fc2_ref)
    for w in range(count):
        levels = [None] * LEV
        for pair in range(2):
            for r in range(2):
                at = HALF * (2 * w + pair) + QUART * r
                levels[PAIRS[pair][r]] = own_ref[at : at + QUART, :]
        results(w, jnp.stack(levels))


def edge_kernel(part_ref, tok_ref, west_ref, east_ref, north_ref, south_ref, nw_ref, ne_ref, sw_ref, se_ref,
                g1_ref, b1_ref, qkv_ref, bias1_ref, bias2_ref, valid_ref, proj_ref, g2_ref, b2_ref,
                fc1_ref, fc2_ref, out_ref, xs_ref, q_ref, kv_ref, own_ref, sides_ref, strip_ref, side_sem, strip_sem):
    del part_ref
    rows, cols = tok_ref.shape[:2]
    refs = (g1_ref[...], b1_ref[...], qkv_ref, proj_ref, g2_ref[...], b2_ref[...], fc1_ref, fc2_ref,
            xs_ref, q_ref, kv_ref, own_ref)

    def side_copies(i, slot):
        at = pl.ds(SLAT + WLAT * i, WLAT)
        return [pltpu.make_async_copy(sides_ref.at[slot, side], out_ref.at[at, pl.ds(where, SLON)],
                                      side_sem.at[slot, side])
                for side, where in ((0, 0), (1, cols - SLON))]

    def sides(i, carry):
        slot = lax.rem(i, 2)
        at = pl.ds(SLAT + WLAT * i, WLAT)
        windows = (
            (tok_ref[at, 0:SLON], west_ref[at], False, valid_ref[3 * (i + 1)]),
            (tok_ref[at, cols - SLON : cols], east_ref[at], True, valid_ref[3 * (i + 1) + 2]),
        )

        @pl.when(i >= 2)
        def _():
            for copy in side_copies(i - 2, slot):
                copy.wait()

        def results(w, levels):
            sides_ref[slot, w] = from_level(levels, (WLAT, SLON, LEV, C))

        half_windows(windows, refs, bias1_ref, results)
        for copy in side_copies(i, slot):
            copy.start()
        return carry

    steps = (rows - WLAT) // WLAT
    lax.fori_loop(0, steps, sides, 0)

    copies = []
    for which in range(2):
        if which == 0:
            own_rows, own_first, mid, left, right = slice(0, SLAT), False, north_ref, nw_ref, ne_ref
        else:
            own_rows, own_first, mid, left, right = slice(rows - SLAT, rows), True, south_ref, sw_ref, se_ref
        own = jnp.concatenate([west_ref[own_rows], tok_ref[own_rows], east_ref[own_rows]], axis=1)
        halo = jnp.concatenate([left[...], mid[...], right[...]], axis=1)
        windows = tuple(
            (own[:, WLON * k : WLON * k + WLON], halo[:, WLON * k : WLON * k + WLON], own_first,
             valid_ref[18 * which + k]) for k in range(3))

        def results(w, levels):
            block = from_level(levels, (SLAT, WLON, LEV, C))
            if w == 0:
                strip_ref[which, :, 0:SLON] = block[:, SLON:]
            elif w == 1:
                strip_ref[which, :, SLON : SLON + WLON] = block
            else:
                strip_ref[which, :, SLON + WLON :] = block[:, :SLON]

        half_windows(windows, refs, bias2_ref, results)
        copy = pltpu.make_async_copy(strip_ref.at[which], out_ref.at[own_rows], strip_sem.at[which])
        copy.start()
        copies.append(copy)
    for i in (steps - 2, steps - 1):
        for copy in side_copies(i, i % 2):
            copy.wait()
    for copy in copies:
        copy.wait()


def passed_along(block, axes, distance):
    sizes = [lax.axis_size(a) for a in axes]
    route = []
    for i in np.ndindex(*sizes):
        j = tuple((a - d) % s for a, d, s in zip(i, distance, sizes))
        route.append((int(np.ravel_multi_index(j, sizes)), int(np.ravel_multi_index(i, sizes))))
    return lax.ppermute(block, axes if len(axes) > 1 else axes[0], route)


def per_device(tokens, norm1_gain, norm1_bias, qkv_weight, rel_bias, key_mask, proj_weight,
               norm2_gain, norm2_bias, fc1_weight, fc2_weight):
    rows, cols = tokens.shape[:2]
    west = passed_along(tokens[:, cols - SLON :], ("lon",), (1,))
    east = passed_along(tokens[:, :SLON], ("lon",), (-1,))
    north = passed_along(tokens[rows - SLAT :], ("lat",), (1,))
    south = passed_along(tokens[:SLAT], ("lat",), (-1,))
    both = ("lon", "lat")
    nw = passed_along(tokens[rows - SLAT :, cols - SLON :], both, (1, 1))
    ne = passed_along(tokens[rows - SLAT :, :SLON], both, (-1, 1))
    sw = passed_along(tokens[:SLAT, cols - SLON :], both, (1, -1))
    se = passed_along(tokens[:SLAT, :SLON], both, (-1, -1))

    vmem = pl.BlockSpec(memory_space=pltpu.VMEM)
    params = pltpu.CompilerParams(vmem_limit_bytes=VMEM_LIMIT)
    shape = (*key_mask.shape, rows, cols)
    place = jnp.stack([lax.axis_index("lat"), lax.axis_index("lon")]).astype(jnp.int32)
    table = jnp.pad(rel_bias, ((0, 0), (0, 9)))
    bias1, bias2, valid = pl.pallas_call(
        functools.partial(prep_kernel, shape=shape),
        out_shape=[jax.ShapeDtypeStruct((HEADS, 2, WIN, WIN), F32)] * 2 + [jax.ShapeDtypeStruct((21, 1, WIN), F32)],
        in_specs=[pl.BlockSpec(memory_space=pltpu.SMEM), vmem, vmem],
        out_specs=[vmem] * 3,
        scratch_shapes=[pltpu.VMEM((8 * WIN, 384), F32)],
        compiler_params=params,
        cost_estimate=pl.CostEstimate(flops=10**9, bytes_accessed=5 * 10**6, transcendentals=0),
        name="prep",
    )(place, table, key_mask)

    g1, b1 = norm1_gain.reshape(1, C), norm1_bias.reshape(1, C)
    g2, b2 = norm2_gain.reshape(1, C), norm2_bias.reshape(1, C)
    fixed = lambda *s: pl.BlockSpec(s, lambda i: (0,) * len(s), pipeline_mode=pl.Buffered(1))
    part = pl.pallas_call(
        inner_kernel,
        grid=((rows - WLAT) // WLAT,),
        out_shape=jax.ShapeDtypeStruct(tokens.shape, BF),
        in_specs=[
            pl.BlockSpec((pl.Element(WLAT), pl.Element(WLON), pl.Element(LEV), pl.Element(C)),
                         lambda i: (SLAT + WLAT * i, SLON, 0, 0)),
            fixed(1, C), fixed(1, C), fixed(C, 3 * C), fixed(HEADS, 2, WIN, WIN), fixed(21, 1, WIN), fixed(C, C),
            fixed(1, C), fixed(1, C), fixed(C, FF), fixed(FF, C),
        ],
        out_specs=pl.BlockSpec((pl.Element(WLAT), pl.Element(WLON), pl.Element(LEV), pl.Element(C)),
                               lambda i: (SLAT + WLAT * i, SLON, 0, 0)),
        scratch_shapes=[pltpu.VMEM((2 * WIN, C), F32), pltpu.VMEM((2 * WIN, C), F32),
                        pltpu.VMEM((2 * WIN, 2 * C), BF), pltpu.VMEM((2 * WIN, C), BF)],
        compiler_params=params,
        cost_estimate=pl.CostEstimate(flops=12 * 10**9, bytes_accessed=12 * 10**6, transcendentals=0),
        name="inner",
    )(tokens, g1, b1, qkv_weight, bias1, valid, proj_weight, g2, b2, fc1_weight, fc2_weight)

    any_space = pl.BlockSpec(memory_space=pl.ANY)
    most = 6 * WIN
    return pl.pallas_call(
        edge_kernel,
        out_shape=jax.ShapeDtypeStruct(tokens.shape, BF),
        in_specs=[any_space] + [vmem] * 20,
        out_specs=any_space,
        scratch_shapes=[pltpu.VMEM((most, C), F32), pltpu.VMEM((most // 2, C), F32), pltpu.VMEM((most, 2 * C), BF),
                        pltpu.VMEM((most // 2, C), F32), pltpu.VMEM((2, 2, WLAT, SLON, LEV, C), BF),
                        pltpu.VMEM((2, SLAT, cols, LEV, C), BF),
                        pltpu.SemaphoreType.DMA((2, 2)), pltpu.SemaphoreType.DMA((2,))],
        input_output_aliases={0: 0},
        compiler_params=params,
        cost_estimate=pl.CostEstimate(flops=16 * 10**9, bytes_accessed=16 * 10**6, transcendentals=0),
        name="edge",
    )(part, tokens, west, east, north, south, nw, ne, sw, se, g1, b1, qkv_weight, bias1, bias2, valid,
      proj_weight, g2, b2, fc1_weight, fc2_weight)


def solution(mesh):
    return jax.shard_map(
        per_device,
        mesh=mesh,
        in_specs=(P("lat", "lon", None, None),) + (P(),) * 10,
        out_specs=P("lat", "lon", None, None),
        check_vma=False,
    )
```

profile of v0, /device:TPU:0, one launch (start us, length us, event | category | flops | bytes accessed | tf_op | source)
XLA Modules:
  0.0 106.1 jit_solution(18335791140363923985)
XLA Ops:
  0.0 0.0 copy-start
  0.0 1.1 %fusion = (bf16[3,6,4,512]{3,2,1,0:T(4,128)(2,1)S(1)}, bf16[3,6,4,512]{3,2,1,0:T(4,128)(2,1)S(1)}, bf16[3,6,4,512]{3,2,1,0:T(4,128)(2,1)S(1)}, bf16[3,6,4,512]{3,2,1,0:T(4,128)(2,1)S(1)}) fusion(bf16[36,24,4,512]{3,2,1,0:T(4,128)(2,1)} %tok_ref.3), kind=kLoop, calls=%fused_computation.1 | loop fusion | bytes 589824 | tf_op jit(solution)/shard_map/slice | solution.py:329
  1.1 8.3 %collective-permute-start.7 = (bf16[3,6,4,512]{3,2,1,0:T(4,128)(2,1)S(1)}, bf16[3,6,4,512]{3,2,1,0:T(4,128)(2,1)S(1)}, u32[]{:S(2)}, u32[]{:S(2)}) collective-permute-start(bf16[3,6,4,512]{3,2,1,0:T(4,128)(2,1)S(1)} %get-tuple-element.11), channel_id=1, source_target_pairs={{9,0},{10,1},{11,2},{12,3},{13,4},{14,5},{15,6},{8,7},{17,8},{18,9... | collective-permute-start | bytes 221192 | tf_op jit(solution)/shard_map/ppermute | solution.py:315
  9.4 0.0 collective-permute-start.6
  9.4 4.8 %collective-permute-start.5 = (bf16[3,6,4,512]{3,2,1,0:T(4,128)(2,1)S(1)}, bf16[3,6,4,512]{3,2,1,0:T(4,128)(2,1)S(1)}, u32[]{:S(2)}, u32[]{:S(2)}) collective-permute-start(bf16[3,6,4,512]{3,2,1,0:T(4,128)(2,1)S(1)} %get-tuple-element.13), channel_id=1, source_target_pairs={{15,0},{8,1},{9,2},{10,3},{11,4},{12,5},{13,6},{14,7},{23,8},{16,9... | collective-permute-start | bytes 221192 | tf_op jit(solution)/shard_map/ppermute | solution.py:315
  14.1 0.0 collective-permute-start.4
  14.1 1.3 %fusion.1 = (bf16[3,24,4,512]{3,2,1,0:T(4,128)(2,1)S(1)}, bf16[3,24,4,512]{3,2,1,0:T(4,128)(2,1)S(1)}) fusion(bf16[36,24,4,512]{3,2,1,0:T(4,128)(2,1)} %tok_ref.3), kind=kLoop, calls=%fused_computation.2 | loop fusion | bytes 1179648 | tf_op jit(solution)/shard_map/slice | solution.py:324
  15.4 3.0 %collective-permute-start.3 = (bf16[3,24,4,512]{3,2,1,0:T(4,128)(2,1)S(1)}, bf16[3,24,4,512]{3,2,1,0:T(4,128)(2,1)S(1)}, u32[]{:S(2)}, u32[]{:S(2)}) collective-permute-start(bf16[3,24,4,512]{3,2,1,0:T(4,128)(2,1)S(1)} %get-tuple-element.15), channel_id=1, source_target_pairs={{1,0},{2,1},{3,2},{4,3},{5,4},{6,5},{7,6},{0,7},{9,8},{10,9},{11,1... | collective-permute-start | bytes 884744 | tf_op jit(solution)/shard_map/ppermute | solution.py:315
  18.4 2.0 %fusion.2 = (bf16[36,6,4,512]{3,2,1,0:T(4,128)(2,1)S(1)}, bf16[36,6,4,512]{3,2,1,0:T(4,128)(2,1)S(1)}) fusion(bf16[36,24,4,512]{3,2,1,0:T(4,128)(2,1)} %tok_ref.3), kind=kLoop, calls=%fused_computation.3 | loop fusion | bytes 3538944 | tf_op jit(solution)/shard_map/slice | solution.py:322
  20.5 0.6 pad_add_fusion.place_ref
  21.0 0.0 copy-done
  21.0 0.6 pad.4.table_ref
  21.6 5.3 %prep.1 = (f32[8,2,144,144]{3,2,1,0:T(8,128)}, f32[8,2,144,144]{3,2,1,0:T(8,128)}, f32[21,1,144]{2,1,0:T(1,128)}) custom-call(s32[2]{0:T(128)} %pad_add_fusion.place_ref, f32[8,768]{1,0:T(8,128)} %pad.4.table_ref, s32[288,384]{1,0:T(8,128)} %mask_ref.1), custom_call_target="tpu_custom_call" | custom-call | flops 1000000000 | bytes 5000000 | tf_op jit(solution)/shard_map/prep/pallas_call | solution.py:336
  26.9 0.0 collective-permute-done.7.se_ref
  26.9 0.0 copy-start.5
  26.9 0.0 collective-permute-start.2
  26.9 0.0 collective-permute-done.6.sw_ref
  26.9 0.0 copy-start.6
  27.0 4.9 %collective-permute-start.1 = (bf16[36,6,4,512]{3,2,1,0:T(4,128)(2,1)S(1)}, bf16[36,6,4,512]{3,2,1,0:T(4,128)(2,1)S(1)}, u32[]{:S(2)}, u32[]{:S(2)}) collective-permute-start(bf16[36,6,4,512]{3,2,1,0:T(4,128)(2,1)S(1)} %get-tuple-element.17), channel_id=1, source_target_pairs={{8,0},{16,8},{24,16},{32,24},{40,32},{48,40},{56,48},{64,56},{72,6... | collective-permute-start | bytes 2654216 | tf_op jit(solution)/shard_map/ppermute | solution.py:315
  31.8 0.0 collective-permute-done.5.ne_ref
  31.8 0.0 copy-start.7
  31.8 0.0 collective-permute-start
  31.8 27.1 %inner.1.part_ref = bf16[36,24,4,512]{3,2,1,0:T(4,128)(2,1)} custom-call(bf16[36,24,4,512]{3,2,1,0:T(4,128)(2,1)} %tok_ref.3, f32[1,512]{1,0:T(1,128)} %bitcast.6, f32[1,512]{1,0:T(1,128)} %bitcast.8, bf16[512,1536]{1,0:T(8,128)(2,1)} %qkv_ref.3, f32[8,2,144,144]{3,2,1,0:T(8,128)} %get-tuple-element.8.bias_ref.bias1_ref, ...), custom_call_target="tpu_custom_call" | custom-call | flops 12000000000 | bytes 12000000 | tf_op jit(solution)/shard_map/inner/pallas_call | solution.py:350
  58.9 0.0 copy-done.5
  58.9 0.0 copy-done.6
  58.9 0.0 copy-done.7
  58.9 0.0 collective-permute-done.4.nw_ref
  58.9 0.0 copy-start.8
  59.0 0.0 collective-permute-done.3.south_ref
  59.0 0.0 copy-start.3
  59.0 0.0 collective-permute-done.2.north_ref
  59.0 0.0 copy-start.4
  59.0 0.0 collective-permute-done.1.east_ref
  59.0 0.0 copy-start.1
  59.0 0.0 collective-permute-done.west_ref
  59.0 0.0 copy-start.2
  59.0 0.5 copy-done.8
  59.6 0.1 copy-done.3
  59.7 0.1 copy-done.4
  59.8 0.3 copy-done.1
  60.1 0.3 copy-done.2
  60.4 45.5 %edge.1 = bf16[36,24,4,512]{3,2,1,0:T(4,128)(2,1)} custom-call(bf16[36,24,4,512]{3,2,1,0:T(4,128)(2,1)} %inner.1.part_ref, bf16[36,24,4,512]{3,2,1,0:T(4,128)(2,1)} %tok_ref.3, bf16[36,6,4,512]{3,2,1,0:T(4,128)(2,1)} %copy-done.2, bf16[36,6,4,512]{3,2,1,0:T(4,128)(2,1)} %copy-done.1, ...), custom_call_target="tpu_custom_call", output_to_operand_aliasing={{}: (0, {})} | custom-call | flops 16000000000 | bytes 16000000 | tf_op jit(solution)/shard_map/edge/pallas_call | solution.py:371
Async XLA Ops:
  0.0 21.0 %copy-start = (f32[8,759]{1,0:T(8,128)S(1)}, f32[8,759]{1,0:T(8,128)}, u32[]{:S(2)}) copy-start(f32[8,759]{1,0:T(8,128)} %param.15) | copy-start | bytes 72868
  1.1 25.8 %collective-permute-start.7 = (bf16[3,6,4,512]{3,2,1,0:T(4,128)(2,1)S(1)}, bf16[3,6,4,512]{3,2,1,0:T(4,128)(2,1)S(1)}, u32[]{:S(2)}, u32[]{:S(2)}) collective-permute-start(bf16[3,6,4,512]{3,2,1,0:T(4,128)(2,1)S(1)} %get-tuple-element.11), channel_id=1, source_target_pairs={{9,0},{10,1},{11,2},{12,3},{13,4},{14,5},{15,6},{8,7},{17,8},{18,9... | collective-permute-start | bytes 221192 | tf_op jit(solution)/shard_map/ppermute | solution.py:315
  9.4 17.5 %collective-permute-start.6 = (bf16[3,6,4,512]{3,2,1,0:T(4,128)(2,1)S(1)}, bf16[3,6,4,512]{3,2,1,0:T(4,128)(2,1)S(1)}, u32[]{:S(2)}, u32[]{:S(2)}) collective-permute-start(bf16[3,6,4,512]{3,2,1,0:T(4,128)(2,1)S(1)} %get-tuple-element.12), channel_id=1, source_target_pairs={{121,0},{122,1},{123,2},{124,3},{125,4},{126,5},{127,6},{120,7},{1... | collective-permute-start | bytes 221192 | tf_op jit(solution)/shard_map/ppermute | solution.py:315
  9.4 22.4 %collective-permute-start.5 = (bf16[3,6,4,512]{3,2,1,0:T(4,128)(2,1)S(1)}, bf16[3,6,4,512]{3,2,1,0:T(4,128)(2,1)S(1)}, u32[]{:S(2)}, u32[]{:S(2)}) collective-permute-start(bf16[3,6,4,512]{3,2,1,0:T(4,128)(2,1)S(1)} %get-tuple-element.13), channel_id=1, source_target_pairs={{15,0},{8,1},{9,2},{10,3},{11,4},{12,5},{13,6},{14,7},{23,8},{16,9... | collective-permute-start | bytes 221192 | tf_op jit(solution)/shard_map/ppermute | solution.py:315
  14.1 44.8 %collective-permute-start.4 = (bf16[3,6,4,512]{3,2,1,0:T(4,128)(2,1)S(1)}, bf16[3,6,4,512]{3,2,1,0:T(4,128)(2,1)S(1)}, u32[]{:S(2)}, u32[]{:S(2)}) collective-permute-start(bf16[3,6,4,512]{3,2,1,0:T(4,128)(2,1)S(1)} %get-tuple-element.14), channel_id=1, source_target_pairs={{127,0},{120,1},{121,2},{122,3},{123,4},{124,5},{125,6},{126,7},{7... | collective-permute-start | bytes 221192 | tf_op jit(solution)/shard_map/ppermute | solution.py:315
  15.4 43.6 %collective-permute-start.3 = (bf16[3,24,4,512]{3,2,1,0:T(4,128)(2,1)S(1)}, bf16[3,24,4,512]{3,2,1,0:T(4,128)(2,1)S(1)}, u32[]{:S(2)}, u32[]{:S(2)}) collective-permute-start(bf16[3,24,4,512]{3,2,1,0:T(4,128)(2,1)S(1)} %get-tuple-element.15), channel_id=1, source_target_pairs={{1,0},{2,1},{3,2},{4,3},{5,4},{6,5},{7,6},{0,7},{9,8},{10,9},{11,1... | collective-permute-start | bytes 884744 | tf_op jit(solution)/shard_map/ppermute | solution.py:315
  26.9 32.0 %copy-start.5 = (bf16[3,6,4,512]{3,2,1,0:T(4,128)(2,1)}, bf16[3,6,4,512]{3,2,1,0:T(4,128)(2,1)S(1)}, u32[]{:S(2)}) copy-start(bf16[3,6,4,512]{3,2,1,0:T(4,128)(2,1)S(1)} %collective-permute-done.7.se_ref) | copy-start | bytes 221188
  26.9 32.1 %collective-permute-start.2 = (bf16[3,24,4,512]{3,2,1,0:T(4,128)(2,1)S(1)}, bf16[3,24,4,512]{3,2,1,0:T(4,128)(2,1)S(1)}, u32[]{:S(2)}, u32[]{:S(2)}) collective-permute-start(bf16[3,24,4,512]{3,2,1,0:T(4,128)(2,1)S(1)} %get-tuple-element.16), channel_id=1, source_target_pairs={{7,0},{0,1},{1,2},{2,3},{3,4},{4,5},{5,6},{6,7},{15,8},{8,9},{9,10... | collective-permute-start | bytes 884744 | tf_op jit(solution)/shard_map/ppermute | solution.py:315
  26.9 32.0 %copy-start.6 = (bf16[3,6,4,512]{3,2,1,0:T(4,128)(2,1)}, bf16[3,6,4,512]{3,2,1,0:T(4,128)(2,1)S(1)}, u32[]{:S(2)}) copy-start(bf16[3,6,4,512]{3,2,1,0:T(4,128)(2,1)S(1)} %collective-permute-done.6.sw_ref) | copy-start | bytes 221188
  27.0 32.0 %collective-permute-start.1 = (bf16[36,6,4,512]{3,2,1,0:T(4,128)(2,1)S(1)}, bf16[36,6,4,512]{3,2,1,0:T(4,128)(2,1)S(1)}, u32[]{:S(2)}, u32[]{:S(2)}) collective-permute-start(bf16[36,6,4,512]{3,2,1,0:T(4,128)(2,1)S(1)} %get-tuple-element.17), channel_id=1, source_target_pairs={{8,0},{16,8},{24,16},{32,24},{40,32},{48,40},{56,48},{64,56},{72,6... | collective-permute-start | bytes 2654216 | tf_op jit(solution)/shard_map/ppermute | solution.py:315
  31.8 27.1 %copy-start.7 = (bf16[3,6,4,512]{3,2,1,0:T(4,128)(2,1)}, bf16[3,6,4,512]{3,2,1,0:T(4,128)(2,1)S(1)}, u32[]{:S(2)}) copy-start(bf16[3,6,4,512]{3,2,1,0:T(4,128)(2,1)S(1)} %collective-permute-done.5.ne_ref) | copy-start | bytes 221188
  31.8 27.2 %collective-permute-start = (bf16[36,6,4,512]{3,2,1,0:T(4,128)(2,1)S(1)}, bf16[36,6,4,512]{3,2,1,0:T(4,128)(2,1)S(1)}, u32[]{:S(2)}, u32[]{:S(2)}) collective-permute-start(bf16[36,6,4,512]{3,2,1,0:T(4,128)(2,1)S(1)} %get-tuple-element.18), channel_id=1, source_target_pairs={{120,0},{0,8},{8,16},{16,24},{24,32},{32,40},{40,48},{48,56},{56,6... | collective-permute-start | bytes 2654216 | tf_op jit(solution)/shard_map/ppermute | solution.py:315
  58.9 0.6 copy-start.8
  59.0 0.8 copy-start.3
  59.0 0.8 copy-start.4
  59.0 1.1 %copy-start.1 = (bf16[36,6,4,512]{3,2,1,0:T(4,128)(2,1)}, bf16[36,6,4,512]{3,2,1,0:T(4,128)(2,1)S(1)}, u32[]{:S(2)}) copy-start(bf16[36,6,4,512]{3,2,1,0:T(4,128)(2,1)S(1)} %collective-permute-done.1.east_ref) | copy-start | bytes 2654212
  59.0 1.4 %copy-start.2 = (bf16[36,6,4,512]{3,2,1,0:T(4,128)(2,1)}, bf16[36,6,4,512]{3,2,1,0:T(4,128)(2,1)S(1)}, u32[]{:S(2)}) copy-start(bf16[36,6,4,512]{3,2,1,0:T(4,128)(2,1)S(1)} %collective-permute-done.west_ref) | copy-start | bytes 2654212
where the time goes:
time: 106 us
  Pallas kernels  77.9 us (73%)
  starting transfers between devices  20.9 us (20%)
  local copies, waits for them, and re-layouts  6.41 us (6%)
    pallas_call x1, Pallas kernels, per_device(): pl.pallas_call(edge_kernel, out_shape=jax.ShapeDtypeStruct(tokens.shape,...  45.5 us
    pallas_call x1, Pallas kernels, per_device(): pl.pallas_call(inner_kernel, grid=((rows - WLAT) // WLAT,), out_shape=jax...  27.1 us
    ppermute x8, starting transfers between devices, passed_along(): return lax.ppermute(block, axes if len(axes) > 1 else axes[0], route)  20.9 us
    pallas_call x1, Pallas kernels, per_device(): pl.pallas_call(functools.partial(prep_kernel, shape=shape), out_shape=[ja...  5.28 us
  transfers between devices with their start and end apart: 8, of which 0 were waited for; matrix products, arithmetic and copies ran while one was open for 4% of the time, Pallas kernels for 30%

commit v1 on v0

v1 whole, which is shorter than its diff:
```python
import functools
import math

import jax
import jax.numpy as jnp
import numpy as np
from jax import lax
from jax.experimental import pallas as pl
from jax.experimental.pallas import tpu as pltpu
from jax.sharding import PartitionSpec as P

C = 512
FF = 2048
HEADS = 8
HEAD_DIM = 64
WLEV = 2
WLAT = 6
WLON = 12
LEV = 4
SLAT = 3
SLON = 6
WIN = WLAT * WLON * WLEV
HALF = WIN // 2
QUART = WIN // 4
EPS = 1e-5
LOG2E = math.log2(math.e)
NEG = -jnp.inf
BF = jnp.bfloat16
F32 = jnp.float32
PAIRS = ((1, 2), (3, 0))
VMEM_LIMIT = 56 * 1024 * 1024


def order_columns():
    first = [(p, 6 * h + q, r) for h in range(2) for r in range(2) for p in range(6) for q in range(6)]
    second = [(3 * h + p, q, r) for h in range(2) for r in range(2) for p in range(3) for q in range(12)]
    return first, second


def lane_pqr(u, which):
    half, r, cell = u // HALF, (u // QUART) % 2, u % QUART
    if which == 0:
        return cell // 6, 6 * half + cell % 6, r
    return 3 * half + cell // 12, cell % 12, r


def prep_kernel(place_ref, table_ref, mask_ref, bias1_ref, bias2_ref, valid_ref, rows_ref, *, shape):
    lat, lon, lats = place_ref[0], place_ref[1], shape[0] // shape[2]
    table = table_ref[...] * LOG2E
    out_refs = (bias1_ref, bias2_ref)
    for which, order in enumerate(order_columns()):
        for t, (p, q, r) in enumerate(order):
            start = p * 69 + q * 3 + r
            rows_ref[8 * t : 8 * t + 8, :] = table[:, start : start + 384]
        rows = rows_ref[...]
        high = rows.astype(BF)
        low = (rows - high.astype(F32)).astype(BF)
        k = lax.broadcasted_iota(jnp.int32, (384, WIN), 0)
        p, q, r = lane_pqr(lax.broadcasted_iota(jnp.int32, (384, WIN), 1), which)
        pick = (k == 379 - (p * 69 + q * 3 + r)).astype(F32).astype(BF)
        full = jnp.dot(high, pick, preferred_element_type=F32) + jnp.dot(low, pick, preferred_element_type=F32)
        full = jnp.transpose(full.reshape(WIN, HEADS, WIN), (1, 0, 2))
        out_refs[which][...] = full
    nlat, nlon, tile_rows, tile_cols = shape
    row = lax.broadcasted_iota(jnp.int32, (48, nlat), 0)
    col = lax.broadcasted_iota(jnp.int32, (48, nlat), 1)
    want = lax.rem(lat * tile_rows - SLAT + row + nlat, nlat)
    pick_rows = (want == col).astype(F32).astype(BF)
    mask = (mask_ref[...] > 0).astype(F32).astype(BF)
    picked = jnp.dot(pick_rows, mask, preferred_element_type=F32).astype(BF)
    for which in range(2):
        row = lax.broadcasted_iota(jnp.int32, (nlon, 3 * WIN), 0)
        lane = lax.broadcasted_iota(jnp.int32, (nlon, 3 * WIN), 1)
        _, q, _ = lane_pqr(lane % WIN, which)
        want = lax.rem(lon * tile_cols - SLON + 12 * (lane // WIN) + q + nlon, nlon)
        pick_cols = (want == row).astype(F32).astype(BF)
        spread = jnp.dot(picked, pick_cols, preferred_element_type=F32)
        row = lax.broadcasted_iota(jnp.int32, (48, 3 * WIN), 0)
        lane = lax.broadcasted_iota(jnp.int32, (48, 3 * WIN), 1)
        p, _, _ = lane_pqr(lane % WIN, which)
        lane1 = lax.broadcasted_iota(jnp.int32, (1, 3 * WIN), 1)
        for window in (range(1, 6) if which == 0 else (0, 6)):
            value = jnp.sum(jnp.where(row == 6 * window + p, spread, 0.0), axis=0, keepdims=True)
            ok = value > 0.5
            if window == 0:
                ok = ok & ((lat > 0) | (lane1 % WIN >= HALF))
            if window == 6:
                ok = ok & ((lat < lats - 1) | (lane1 % WIN < HALF))
            value = jnp.where(ok, 0.0, NEG)
            for k in range(3):
                valid_ref[3 * window + k] = value[:, k * WIN : (k + 1) * WIN]


def layer_norm(values, gain, offset):
    average = jnp.mean(values, axis=-1, keepdims=True)
    centred = values - average
    spread = jnp.mean(centred * centred, axis=-1, keepdims=True)
    return centred * lax.rsqrt(spread + EPS) * gain + offset


def by_level(block):
    cells = block.astype(F32).reshape(QUART, LEV, C)
    return jnp.transpose(cells, (1, 0, 2))


def from_level(rows, shape):
    return jnp.transpose(rows, (1, 0, 2)).reshape(shape).astype(BF)


def attend(q, k, v, bias_of, block_mask):
    n = q.shape[0]
    head_of = lax.broadcasted_iota(jnp.int32, (1, 256), 1) // HEAD_DIM
    parts = []
    for g in range(2):
        lanes = slice(256 * g, 256 * g + 256)
        qg = q[:, lanes]
        stacked = jnp.concatenate([jnp.where(head_of == j, qg, 0.0) for j in range(4)], axis=0).astype(BF)
        scores = lax.dot_general(stacked, k[:, lanes], (((1,), (1,)), ((), ())), preferred_element_type=F32)
        probs, scale = [], []
        for j in range(4):
            s = scores[j * n : (j + 1) * n] + (bias_of(4 * g + j) + block_mask)
            powered = jnp.exp2(s - jnp.max(s, axis=-1, keepdims=True))
            scale.append(1.0 / jnp.sum(powered, axis=-1, keepdims=True))
            probs.append(powered)
        probs = jnp.concatenate(probs, axis=0).astype(BF)
        out = jnp.dot(probs, v[:, lanes], preferred_element_type=F32)
        context = out[:n] * scale[0]
        for j in range(1, 4):
            context = jnp.where(head_of == j, out[j * n : (j + 1) * n] * scale[j], context)
        parts.append(context)
    return jnp.concatenate(parts, axis=1)


def feed(middle, gain, offset, fc1_ref, fc2_ref):
    normed = layer_norm(middle, gain, offset).astype(BF)
    total = None
    for j in range(4):
        v = jnp.dot(normed, fc1_ref[:, 512 * j : 512 * j + 512], preferred_element_type=F32)
        hidden = (v + v * lax.erf(v * (0.5 ** 0.5))).astype(BF)
        part = jnp.dot(hidden, fc2_ref[512 * j : 512 * j + 512, :], preferred_element_type=F32)
        total = part if total is None else total + part
    return middle + 0.5 * total


def block_masks(valid, first, n):
    t = lax.broadcasted_iota(jnp.int32, (n, WIN), 0) + first
    u = lax.broadcasted_iota(jnp.int32, (n, WIN), 1)
    joint = jnp.where(t == u, 0.0, jnp.broadcast_to(valid, (n, WIN)))
    same = (t // QUART) % 2 == (u // QUART) % 2
    return joint, jnp.where(same, joint, NEG)


def put_levels(levels, into_ref, at, step):
    for pair in range(2):
        rows = jnp.concatenate([levels[level] for level in PAIRS[pair]], axis=0)
        into_ref[pl.ds(pl.multiple_of(at + step * pair, 8), HALF), :] = rows


def take_levels(from_ref, at, step):
    levels = [None] * LEV
    for pair in range(2):
        rows = from_ref[pl.ds(pl.multiple_of(at + step * pair, 8), HALF), :]
        for r in range(2):
            levels[PAIRS[pair][r]] = rows[QUART * r : QUART * r + QUART]
    return jnp.stack(levels)


def rest_of_block(rows, ctx_ref, xs_ref, proj_ref, g2_ref, b2_ref, fc1_ref, fc2_ref):
    moved = jnp.dot(ctx_ref[rows, :], proj_ref[...], preferred_element_type=F32).astype(BF)
    middle = xs_ref[rows, :] + moved.astype(F32)
    xs_ref[rows, :] = feed(middle, g2_ref[...], b2_ref[...], fc1_ref, fc2_ref)


def start_copies(pairs, sem):
    copies = [pltpu.make_async_copy(src, dst, sem.at[n]) for n, (src, dst) in enumerate(pairs)]
    for copy in copies:
        copy.start()
    return copies


Q_SCALE = HEAD_DIM ** -0.5 * LOG2E


def inner_kernel(tok_hbm, qkv_hbm, bias_hbm, proj_hbm, fc1_hbm, fc2_hbm, g1_ref, b1_ref, valid_ref, g2_ref, b2_ref,
                 out_hbm, tok_ref, qkv_ref, bias_ref, proj_ref, fc1_ref, fc2_ref, out_ref, xs_ref, norm_ref, q_ref,
                 kv_ref, ctx_ref, sem, out_sem):
    steps = tok_ref.shape[0] // WLAT
    inner = (pl.ds(SLAT, WLAT * steps), pl.ds(SLON, WLON))
    copies = start_copies([(tok_hbm.at[inner], tok_ref), (qkv_hbm, qkv_ref), (bias_hbm, bias_ref),
                           (proj_hbm, proj_ref), (fc1_hbm, fc1_ref), (fc2_hbm, fc2_ref)], sem)
    big = 2 * WIN
    part = big * steps // 2

    copies[0].wait()

    def load(i, carry):
        at = pl.multiple_of(big * i, big)
        x = tok_ref[pl.ds(WLAT * i, WLAT)]
        for h in range(2):
            put_levels(by_level(x[:, 6 * h : 6 * h + 6]), xs_ref, at + HALF * h, WIN)
        norm_ref[pl.ds(at, big), :] = layer_norm(xs_ref[pl.ds(at, big), :], g1_ref[...], b1_ref[...]).astype(BF)
        return carry

    lax.fori_loop(0, steps, load, 0)
    copies[1].wait()

    def project(i, carry):
        rows = pl.ds(pl.multiple_of(part * i, 16), part)
        normed = norm_ref[rows, :]
        q_ref[rows, :] = jnp.dot(normed, qkv_ref[:, :C], preferred_element_type=F32) * Q_SCALE
        kv_ref[rows, :] = jnp.dot(normed, qkv_ref[:, C:], preferred_element_type=F32).astype(BF)
        return carry

    lax.fori_loop(0, 2, project, 0)
    copies[2].wait()

    def attention(i, carry):
        masks = block_masks(valid_ref[3 * (i + 1) + 1], 0, WIN)
        for pair in range(2):
            rows = pl.ds(pl.multiple_of(big * i + WIN * pair, WIN), WIN)
            ctx_ref[rows, :] = attend(q_ref[rows, :], kv_ref[rows, :C], kv_ref[rows, C:],
                                      lambda h: bias_ref[h], masks[pair]).astype(BF)
        return carry

    lax.fori_loop(0, steps, attention, 0)
    for copy in copies[3:]:
        copy.wait()

    def rest(i, carry):
        rest_of_block(pl.ds(pl.multiple_of(part * i, 16), part), ctx_ref, xs_ref, proj_ref, g2_ref, b2_ref,
                      fc1_ref, fc2_ref)
        return carry

    lax.fori_loop(0, 2, rest, 0)

    def store(i, carry):
        for h in range(2):
            levels = take_levels(xs_ref, pl.multiple_of(big * i, big) + HALF * h, WIN)
            out_ref[pl.ds(WLAT * i, WLAT), 6 * h : 6 * h + 6] = from_level(levels, (WLAT, 6, LEV, C))
        return carry

    lax.fori_loop(0, steps, store, 0)
    out = pltpu.make_async_copy(out_ref, out_hbm.at[inner], out_sem)
    out.start()
    out.wait()


def edge_kernel(part_hbm, tok_hbm, west_hbm, east_hbm, north_hbm, south_hbm, qkv_hbm, bias1_hbm, bias2_hbm, proj_hbm,
                fc1_hbm, fc2_hbm, g1_ref, b1_ref, valid_ref, g2_ref, b2_ref, out_hbm,
                own_ref, strip_ref, west_ref, east_ref, north_ref, south_ref, qkv_ref, bias1_ref, bias2_ref, proj_ref,
                fc1_ref, fc2_ref, xs_ref, q_ref, kv_ref, ctx_ref, mid_ref, sem, out_sem):
    del part_hbm
    rows, cols = tok_hbm.shape[:2]
    steps = (rows - WLAT) // WLAT
    side_at = ((pl.ds(SLAT, WLAT * steps), pl.ds(0, SLON)), (pl.ds(SLAT, WLAT * steps), pl.ds(cols - SLON, SLON)))
    strip_at = (pl.ds(0, SLAT), pl.ds(rows - SLAT, SLAT))
    places = [(own_ref.at[side], side_at[side]) for side in range(2)]
    places += [(strip_ref.at[which], strip_at[which]) for which in range(2)]
    copies = start_copies([(tok_hbm.at[at], here) for here, at in places[:2]] + [
        (west_hbm, west_ref), (east_hbm, east_ref), (qkv_hbm, qkv_ref), (bias1_hbm, bias1_ref)] + [
        (tok_hbm.at[at], here) for here, at in places[2:]] + [
        (north_hbm, north_ref), (south_hbm, south_ref), (bias2_hbm, bias2_ref), (proj_hbm, proj_ref),
        (fc1_hbm, fc1_ref), (fc2_hbm, fc2_ref)], sem)
    big = 2 * WIN

    def normed_rows(ref, first, count):
        return layer_norm(ref[first : first + count, :], g1_ref[...], b1_ref[...])

    for copy in copies[:6]:
        copy.wait()

    def sides(i, carry):
        at = pl.multiple_of(big * i, big)
        own_rows, halo_rows = pl.ds(WLAT * i, WLAT), pl.ds(2 * SLAT + WLAT * i, WLAT)
        for side, halo_ref in ((0, west_ref), (1, east_ref)):
            own = by_level(own_ref[side, own_rows])
            put_levels(own, xs_ref, big * side + (HALF if side == 0 else 0), WIN)
            put_levels(by_level(halo_ref[halo_rows]), xs_ref, big * side + (0 if side == 0 else HALF), WIN)
            put_levels(own, mid_ref, at + WIN * side, HALF)
        normed = normed_rows(xs_ref, 0, 2 * big)
        kv_ref[: 2 * big, :] = jnp.dot(normed.astype(BF), qkv_ref[:, C:], preferred_element_type=F32).astype(BF)
        own = jnp.concatenate([normed[HALF:WIN], normed[WIN + HALF : big], normed[big : big + HALF],
                               normed[big + WIN : big + WIN + HALF]], axis=0)
        q_ref[...] = jnp.dot(own.astype(BF), qkv_ref[:, :C], preferred_element_type=F32) * Q_SCALE
        contexts = []
        for side in range(2):
            first = HALF if side == 0 else 0
            masks = block_masks(valid_ref[3 * (i + 1) + 2 * side], first, HALF)
            for pair in range(2):
                mine, keys = WIN * side + HALF * pair, big * side + WIN * pair
                contexts.append(attend(q_ref[mine : mine + HALF, :], kv_ref[keys : keys + WIN, :C],
                                       kv_ref[keys : keys + WIN, C:],
                                       lambda h: bias1_ref[h, first : first + HALF, :], masks[pair]))
        ctx_ref[pl.ds(at, big), :] = jnp.concatenate(contexts, axis=0).astype(BF)
        return carry

    lax.fori_loop(0, steps, sides, 0)
    for copy in copies[6:11]:
        copy.wait()

    for which in range(2):
        at = big * (steps + which)
        first = HALF if which == 0 else 0
        inside = slice(SLAT, 2 * SLAT) if which == 0 else slice(rows, rows + SLAT)
        outside = slice(0, SLAT) if which == 0 else slice(rows + SLAT, rows + 2 * SLAT)
        near_ref = (north_ref, south_ref)[which]
        own = jnp.concatenate([west_ref[inside], strip_ref[which], east_ref[inside]], axis=1)
        halo = jnp.concatenate([west_ref[outside], near_ref[...], east_ref[outside]], axis=1)
        for k in range(3):
            window = slice(WLON * k, WLON * k + WLON)
            put_levels(by_level(own[:, window]), xs_ref, big * k + first, WIN)
            put_levels(by_level(halo[:, window]), xs_ref, big * k + HALF - first, WIN)
            if k == 1:
                put_levels(by_level(own[:, window]), mid_ref, at, HALF)
        corner = jnp.concatenate([strip_ref[which, :, cols - SLON :], strip_ref[which, :, :SLON]], axis=1)
        put_levels(by_level(corner), mid_ref, at + WIN, HALF)
        kv_ref[...] = jnp.dot(normed_rows(xs_ref, 0, 3 * big).astype(BF), qkv_ref[:, C:],
                              preferred_element_type=F32).astype(BF)
        q_ref[...] = jnp.dot(normed_rows(mid_ref, at, big).astype(BF), qkv_ref[:, :C],
                             preferred_element_type=F32) * Q_SCALE
        contexts = {}
        for k in range(3):
            masks = block_masks(valid_ref[18 * which + k], first, HALF)
            for pair in range(2):
                mine, keys = (0 if k == 1 else WIN) + HALF * pair, big * k + WIN * pair
                contexts[k, pair] = attend(q_ref[mine : mine + HALF, :], kv_ref[keys : keys + WIN, :C],
                                           kv_ref[keys : keys + WIN, C:],
                                           lambda h: bias2_ref[h, first : first + HALF, :], masks[pair])
        east_cell = lax.broadcasted_iota(jnp.int32, (HALF, 1), 0) % WLON < SLON
        ctx_ref[at : at + big, :] = jnp.concatenate(
            [contexts[1, 0], contexts[1, 1]] + [jnp.where(east_cell, contexts[2, pair], contexts[0, pair])
                                                for pair in range(2)], axis=0).astype(BF)
    for copy in copies[11:]:
        copy.wait()
    part = big * (steps + 2) // 3

    def rest(i, carry):
        rest_of_block(pl.ds(pl.multiple_of(part * i, 16), part), ctx_ref, mid_ref, proj_ref, g2_ref, b2_ref,
                      fc1_ref, fc2_ref)
        return carry

    lax.fori_loop(0, 3, rest, 0)

    def store(i, carry):
        at = pl.multiple_of(big * i, big)
        for side in range(2):
            block = from_level(take_levels(mid_ref, at + WIN * side, HALF), (WLAT, SLON, LEV, C))
            own_ref[side, pl.ds(WLAT * i, WLAT)] = block
        return carry

    lax.fori_loop(0, steps, store, 0)
    for which in range(2):
        at = big * (steps + which)
        strip_ref[which, :, SLON : SLON + WLON] = from_level(take_levels(mid_ref, at, HALF), (SLAT, WLON, LEV, C))
        block = from_level(take_levels(mid_ref, at + WIN, HALF), (SLAT, WLON, LEV, C))
        strip_ref[which, :, cols - SLON :] = block[:, :SLON]
        strip_ref[which, :, :SLON] = block[:, SLON:]
    outs = start_copies([(here, out_hbm.at[at]) for here, at in places], out_sem)
    for copy in outs:
        copy.wait()


def passed_along(block, axis, distance):
    size = lax.axis_size(axis)
    return lax.ppermute(block, axis, [((i - distance) % size, i) for i in range(size)])


def per_device(tokens, norm1_gain, norm1_bias, qkv_weight, rel_bias, key_mask, proj_weight,
               norm2_gain, norm2_bias, fc1_weight, fc2_weight):
    rows, cols = tokens.shape[:2]
    north = passed_along(tokens[rows - SLAT :], "lat", 1)
    south = passed_along(tokens[:SLAT], "lat", -1)

    vmem = pl.BlockSpec(memory_space=pltpu.VMEM)
    any_space = pl.BlockSpec(memory_space=pl.ANY)
    params = pltpu.CompilerParams(vmem_limit_bytes=VMEM_LIMIT)
    shape = (*key_mask.shape, rows, cols)
    place = jnp.stack([lax.axis_index("lat"), lax.axis_index("lon")]).astype(jnp.int32)
    table = jnp.pad(rel_bias, ((0, 0), (0, 9)))
    bias1, bias2, valid = pl.pallas_call(
        functools.partial(prep_kernel, shape=shape),
        out_shape=[jax.ShapeDtypeStruct((HEADS, WIN, WIN), F32)] * 2 + [jax.ShapeDtypeStruct((21, 1, WIN), F32)],
        in_specs=[pl.BlockSpec(memory_space=pltpu.SMEM), vmem, vmem],
        out_specs=[vmem] * 3,
        scratch_shapes=[pltpu.VMEM((8 * WIN, 384), F32)],
        compiler_params=params,
        cost_estimate=pl.CostEstimate(flops=10**9, bytes_accessed=5 * 10**6, transcendentals=0),
        name="prep",
    )(place, table, key_mask)

    def column(at):
        return jnp.concatenate([north[:, at], tokens[:, at], south[:, at]], axis=0)

    west = passed_along(column(slice(cols - SLON, cols)), "lon", 1)
    east = passed_along(column(slice(0, SLON)), "lon", -1)

    g1, b1 = norm1_gain.reshape(1, C), norm1_bias.reshape(1, C)
    g2, b2 = norm2_gain.reshape(1, C), norm2_bias.reshape(1, C)
    count = 2 * WIN * ((rows - WLAT) // WLAT)
    weights = [pltpu.VMEM((C, C), BF), pltpu.VMEM((C, FF), BF), pltpu.VMEM((FF, C), BF)]
    table_shape = pltpu.VMEM((HEADS, WIN, WIN), F32)
    inner_shape = pltpu.VMEM((rows - 2 * SLAT, WLON, LEV, C), BF)
    part = pl.pallas_call(
        inner_kernel,
        out_shape=jax.ShapeDtypeStruct(tokens.shape, BF),
        in_specs=[any_space] * 6 + [vmem] * 5,
        out_specs=any_space,
        scratch_shapes=[inner_shape, pltpu.VMEM((C, 3 * C), BF), table_shape, *weights, inner_shape,
                        pltpu.VMEM((count, C), F32), pltpu.VMEM((count, C), BF), pltpu.VMEM((count, C), F32),
                        pltpu.VMEM((count, 2 * C), BF), pltpu.VMEM((count, C), BF),
                        pltpu.SemaphoreType.DMA((6,)), pltpu.SemaphoreType.DMA],
        compiler_params=params,
        cost_estimate=pl.CostEstimate(flops=12 * 10**9, bytes_accessed=12 * 10**6, transcendentals=0),
        name="inner",
    )(tokens, qkv_weight, bias1, proj_weight, fc1_weight, fc2_weight, g1, b1, valid, g2, b2)

    own = count + 4 * WIN
    strip = (SLAT, cols, LEV, C)
    halo = (rows + 2 * SLAT, SLON, LEV, C)
    return pl.pallas_call(
        edge_kernel,
        out_shape=jax.ShapeDtypeStruct(tokens.shape, BF),
        in_specs=[any_space] * 12 + [vmem] * 5,
        out_specs=any_space,
        scratch_shapes=[pltpu.VMEM((2, rows - 2 * SLAT, SLON, LEV, C), BF), pltpu.VMEM((2, *strip), BF),
                        pltpu.VMEM(halo, BF), pltpu.VMEM(halo, BF), pltpu.VMEM(strip, BF), pltpu.VMEM(strip, BF),
                        pltpu.VMEM((C, 3 * C), BF), table_shape, table_shape, *weights,
                        pltpu.VMEM((6 * WIN, C), F32), pltpu.VMEM((2 * WIN, C), F32), pltpu.VMEM((6 * WIN, 2 * C), BF),
                        pltpu.VMEM((own, C), BF), pltpu.VMEM((own, C), F32),
                        pltpu.SemaphoreType.DMA((14,)), pltpu.SemaphoreType.DMA((4,))],
        input_output_aliases={0: 0},
        compiler_params=params,
        cost_estimate=pl.CostEstimate(flops=16 * 10**9, bytes_accessed=16 * 10**6, transcendentals=0),
        name="edge",
    )(part, tokens, west, east, north, south, qkv_weight, bias1, bias2, proj_weight, fc1_weight, fc2_weight,
      g1, b1, valid, g2, b2)


def solution(mesh):
    return jax.shard_map(
        per_device,
        mesh=mesh,
        in_specs=(P("lat", "lon", None, None),) + (P(),) * 10,
        out_specs=P("lat", "lon", None, None),
        check_vma=False,
    )
```

time: 106 us -> 84 us (0.79)
  the two profiles are of different devices: /device:TPU:0 before, /device:TPU:6 now
where the time goes in v1:
time: 84 us; the launch traced here: 83.7 us
  Pallas kernels  63.6 us (76%)
  starting transfers between devices  8.02 us (10%)
  local copies, waits for them, and re-layouts  5.3 us (6%)
  waiting for transfers between devices  4.43 us (5%)
  other arithmetic  2.04 us (2%)
    pallas_call x1, Pallas kernels, per_device(): pl.pallas_call(edge_kernel, out_shape=jax.ShapeDtypeStruct(tokens.shape,...  36 us
    pallas_call x1, Pallas kernels, per_device(): pl.pallas_call(inner_kernel, out_shape=jax.ShapeDtypeStruct(tokens.shape,...  23.2 us
    ppermute x4, starting transfers between devices, passed_along(): lax.ppermute(block, axis, [((i - distance) % size, i) for i in range(size)])  8.02 us
    ppermute x4, waiting for transfers between devices, passed_along(): lax.ppermute(block, axis, [((i - distance) % size, i) for i in range(size)])  4.43 us
    pallas_call x1, Pallas kernels, per_device(): pl.pallas_call(functools.partial(prep_kernel, shape=shape), out_shape=[ja...  4.33 us
    slice x3, local copies, waits for them, and re-layouts, column(): return jnp.concatenate([north[:, at], tokens[:, at], south[:, at]], axis=0)  2.16 us
  transfers between devices with their start and end apart: 4, of which 1 were waited for; matrix products, arithmetic and copies ran while one was open for 5% of the time, Pallas kernels for 33%

profile of v1, /device:TPU:6, one launch (start us, length us, event | category | flops | bytes accessed | tf_op | source)
XLA Modules:
  0.0 83.7 jit_solution(988310541095941261)
XLA Ops:
  0.0 0.0 copy-start.2
  0.0 1.3 %fusion.1 = (bf16[3,24,4,512]{3,2,1,0:T(4,128)(2,1)S(1)}, bf16[3,24,4,512]{3,2,1,0:T(4,128)(2,1)S(1)}) fusion(bf16[36,24,4,512]{3,2,1,0:T(4,128)(2,1)} %tok_hbm.3), kind=kLoop, calls=%fused_computation.4 | loop fusion | bytes 1179648 | tf_op jit(solution)/shard_map/slice | solution.py:371
  1.3 3.9 %collective-permute-start = (bf16[3,24,4,512]{3,2,1,0:T(4,128)(2,1)S(1)}, bf16[3,24,4,512]{3,2,1,0:T(4,128)(2,1)S(1)}, u32[]{:S(2)}, u32[]{:S(2)}) collective-permute-start(bf16[3,24,4,512]{3,2,1,0:T(4,128)(2,1)S(1)} %get-tuple-element.13), channel_id=1, source_target_pairs={{7,0},{0,1},{1,2},{2,3},{3,4},{4,5},{5,6},{6,7},{15,8},{8,9},{9,10... | collective-permute-start | bytes 884744 | tf_op jit(solution)/shard_map/ppermute | solution.py:365
  5.1 0.0 collective-permute-start.1
  5.1 2.0 %fusion = (bf16[36,6,4,512]{3,2,1,0:T(4,128)(2,1)S(1)}, bf16[36,6,4,512]{3,2,1,0:T(4,128)(2,1)S(1)}) fusion(bf16[36,24,4,512]{3,2,1,0:T(4,128)(2,1)} %tok_hbm.3), kind=kLoop, calls=%fused_computation.3 | loop fusion | bytes 3538944 | tf_op jit(solution)/shard_map/slice | solution.py:392
  7.2 0.0 copy-done.2
  7.2 0.6 pad.4.table_ref
  7.8 0.6 pad_add_fusion.place_ref
  8.4 4.3 %prep.1 = (f32[8,144,144]{2,1,0:T(8,128)}, f32[8,144,144]{2,1,0:T(8,128)}, f32[21,1,144]{2,1,0:T(1,128)}) custom-call(s32[2]{0:T(128)} %pad_add_fusion.place_ref, f32[8,768]{1,0:T(8,128)} %pad.4.table_ref, s32[288,384]{1,0:T(8,128)} %mask_ref.1), custom_call_target="tpu_custom_call" | custom-call | flops 1000000000 | bytes 5000000 | tf_op jit(solution)/shard_map/prep/pallas_call | solution.py:380
  12.7 0.0 collective-permute-done.north_hbm
  12.7 0.0 copy-start
  12.7 0.1 fusion.2
  12.8 4.4 %collective-permute-done.1.south_hbm = bf16[3,24,4,512]{3,2,1,0:T(4,128)(2,1)S(1)} collective-permute-done((bf16[3,24,4,512]{3,2,1,0:T(4,128)(2,1)S(1)}, bf16[3,24,4,512]{3,2,1,0:T(4,128)(2,1)S(1)}, u32[]{:S(2)}, u32[]{:S(2)}) %collective-permute-start.1) | collective-permute-done | bytes 294944 | tf_op jit(solution)/shard_map/ppermute | solution.py:365
  17.2 0.0 copy-start.1
  17.2 0.1 fusion.3
  17.3 0.7 pad_maximum_fusion
  18.0 0.1 collective-permute-start.2
  18.1 0.7 pad_maximum_fusion.1
  18.8 4.1 %collective-permute-start.3 = (bf16[42,6,4,512]{3,2,1,0:T(4,128)(2,1)S(1)}, bf16[42,6,4,512]{3,2,1,0:T(4,128)(2,1)S(1)}, u32[]{:S(2)}, u32[]{:S(2)}) collective-permute-start(bf16[42,6,4,512]{3,2,1,0:T(4,128)(2,1)S(1)} %pad_maximum_fusion.1), channel_id=1, source_target_pairs={{8,0},{16,8},{24,16},{32,24},{40,32},{48,40},{56,48},{64,56},{72,6... | collective-permute-start | bytes 3096584 | tf_op jit(solution)/shard_map/ppermute | solution.py:365
  22.9 23.2 %inner.1.part_hbm = bf16[36,24,4,512]{3,2,1,0:T(4,128)(2,1)} custom-call(bf16[36,24,4,512]{3,2,1,0:T(4,128)(2,1)} %tok_hbm.3, bf16[512,1536]{1,0:T(8,128)(2,1)} %qkv_hbm.3, f32[8,144,144]{2,1,0:T(8,128)} %get-tuple-element.8.bias_hbm.bias1_hbm, bf16[512,512]{1,0:T(8,128)(2,1)} %proj_hbm.3, bf16[512,2048]{1,0:T(8,128)(2,1)} %fc1_hbm.3, ...), custom_call_target="tpu_custom_call" | custom-call | flops 12000000000 | bytes 12000000 | tf_op jit(solution)/shard_map/inner/pallas_call | solution.py:403
  46.1 0.0 copy-done
  46.1 0.0 copy-done.1
  46.1 0.0 collective-permute-done.2.west_hbm
  46.2 0.0 copy-start.3
  46.2 0.0 collective-permute-done.3.east_hbm
  46.2 0.0 copy-start.4
  46.2 1.0 %copy-done.3 = bf16[42,6,4,512]{3,2,1,0:T(4,128)(2,1)} copy-done((bf16[42,6,4,512]{3,2,1,0:T(4,128)(2,1)}, bf16[42,6,4,512]{3,2,1,0:T(4,128)(2,1)S(1)}, u32[]{:S(2)}) %copy-start.3) | copy-done | bytes 1032216
  47.1 0.3 copy-done.4
  47.4 36.0 %edge.1 = bf16[36,24,4,512]{3,2,1,0:T(4,128)(2,1)} custom-call(bf16[36,24,4,512]{3,2,1,0:T(4,128)(2,1)} %inner.1.part_hbm, bf16[36,24,4,512]{3,2,1,0:T(4,128)(2,1)} %tok_hbm.3, bf16[42,6,4,512]{3,2,1,0:T(4,128)(2,1)} %copy-done.3, bf16[42,6,4,512]{3,2,1,0:T(4,128)(2,1)} %copy-done.4, ...), custom_call_target="tpu_custom_call", output_to_operand_aliasing={{}: (0, {})} | custom-call | flops 16000000000 | bytes 16000000 | tf_op jit(solution)/shard_map/edge/pallas_call | solution.py:420
Async XLA Ops:
  0.0 7.2 %copy-start.2 = (f32[8,759]{1,0:T(8,128)S(1)}, f32[8,759]{1,0:T(8,128)}, u32[]{:S(2)}) copy-start(f32[8,759]{1,0:T(8,128)} %param.15) | copy-start | bytes 72868
  1.3 11.5 %collective-permute-start = (bf16[3,24,4,512]{3,2,1,0:T(4,128)(2,1)S(1)}, bf16[3,24,4,512]{3,2,1,0:T(4,128)(2,1)S(1)}, u32[]{:S(2)}, u32[]{:S(2)}) collective-permute-start(bf16[3,24,4,512]{3,2,1,0:T(4,128)(2,1)S(1)} %get-tuple-element.13), channel_id=1, source_target_pairs={{7,0},{0,1},{1,2},{2,3},{3,4},{4,5},{5,6},{6,7},{15,8},{8,9},{9,10... | collective-permute-start | bytes 884744 | tf_op jit(solution)/shard_map/ppermute | solution.py:365
  5.1 12.1 %collective-permute-start.1 = (bf16[3,24,4,512]{3,2,1,0:T(4,128)(2,1)S(1)}, bf16[3,24,4,512]{3,2,1,0:T(4,128)(2,1)S(1)}, u32[]{:S(2)}, u32[]{:S(2)}) collective-permute-start(bf16[3,24,4,512]{3,2,1,0:T(4,128)(2,1)S(1)} %get-tuple-element.14), channel_id=1, source_target_pairs={{1,0},{2,1},{3,2},{4,3},{5,4},{6,5},{7,6},{0,7},{9,8},{10,9},{11,1... | collective-permute-start | bytes 884744 | tf_op jit(solution)/shard_map/ppermute | solution.py:365
  12.7 33.4 %copy-start = (bf16[3,24,4,512]{3,2,1,0:T(4,128)(2,1)}, bf16[3,24,4,512]{3,2,1,0:T(4,128)(2,1)S(1)}, u32[]{:S(2)}) copy-start(bf16[3,24,4,512]{3,2,1,0:T(4,128)(2,1)S(1)} %collective-permute-done.north_hbm) | copy-start | bytes 884740
  17.2 28.9 %copy-start.1 = (bf16[3,24,4,512]{3,2,1,0:T(4,128)(2,1)}, bf16[3,24,4,512]{3,2,1,0:T(4,128)(2,1)S(1)}, u32[]{:S(2)}) copy-start(bf16[3,24,4,512]{3,2,1,0:T(4,128)(2,1)S(1)} %collective-permute-done.1.south_hbm) | copy-start | bytes 884740
  18.0 28.1 %collective-permute-start.2 = (bf16[42,6,4,512]{3,2,1,0:T(4,128)(2,1)S(1)}, bf16[42,6,4,512]{3,2,1,0:T(4,128)(2,1)S(1)}, u32[]{:S(2)}, u32[]{:S(2)}) collective-permute-start(bf16[42,6,4,512]{3,2,1,0:T(4,128)(2,1)S(1)} %pad_maximum_fusion), channel_id=1, source_target_pairs={{120,0},{0,8},{8,16},{16,24},{24,32},{32,40},{40,48},{48,56},{56,6... | collective-permute-start | bytes 3096584 | tf_op jit(solution)/shard_map/ppermute | solution.py:365
  18.8 27.3 %collective-permute-start.3 = (bf16[42,6,4,512]{3,2,1,0:T(4,128)(2,1)S(1)}, bf16[42,6,4,512]{3,2,1,0:T(4,128)(2,1)S(1)}, u32[]{:S(2)}, u32[]{:S(2)}) collective-permute-start(bf16[42,6,4,512]{3,2,1,0:T(4,128)(2,1)S(1)} %pad_maximum_fusion.1), channel_id=1, source_target_pairs={{8,0},{16,8},{24,16},{32,24},{40,32},{48,40},{56,48},{64,56},{72,6... | collective-permute-start | bytes 3096584 | tf_op jit(solution)/shard_map/ppermute | solution.py:365
  46.2 1.0 %copy-start.3 = (bf16[42,6,4,512]{3,2,1,0:T(4,128)(2,1)}, bf16[42,6,4,512]{3,2,1,0:T(4,128)(2,1)S(1)}, u32[]{:S(2)}) copy-start(bf16[42,6,4,512]{3,2,1,0:T(4,128)(2,1)S(1)} %collective-permute-done.2.west_hbm) | copy-start | bytes 3096580
  46.2 1.3 %copy-start.4 = (bf16[42,6,4,512]{3,2,1,0:T(4,128)(2,1)}, bf16[42,6,4,512]{3,2,1,0:T(4,128)(2,1)S(1)}, u32[]{:S(2)}) copy-start(bf16[42,6,4,512]{3,2,1,0:T(4,128)(2,1)S(1)} %collective-permute-done.3.east_hbm) | copy-start | bytes 3096580

commit v2 on v1

--- a/solution.py
+++ b/solution.py
@@ -28,7 +28,7 @@
 BF = jnp.bfloat16
 F32 = jnp.float32
 PAIRS = ((1, 2), (3, 0))
-VMEM_LIMIT = 56 * 1024 * 1024
+VMEM_LIMIT = 44 * 1024 * 1024
 
 
 def order_columns():
@@ -44,51 +44,56 @@
     return 3 * half + cell // 12, cell % 12, r
 
 
-def prep_kernel(place_ref, table_ref, mask_ref, bias1_ref, bias2_ref, valid_ref, rows_ref, *, shape):
-    lat, lon, lats = place_ref[0], place_ref[1], shape[0] // shape[2]
-    table = table_ref[...] * LOG2E
-    out_refs = (bias1_ref, bias2_ref)
-    for which, order in enumerate(order_columns()):
-        for t, (p, q, r) in enumerate(order):
-            start = p * 69 + q * 3 + r
-            rows_ref[8 * t : 8 * t + 8, :] = table[:, start : start + 384]
-        rows = rows_ref[...]
-        high = rows.astype(BF)
-        low = (rows - high.astype(F32)).astype(BF)
-        k = lax.broadcasted_iota(jnp.int32, (384, WIN), 0)
-        p, q, r = lane_pqr(lax.broadcasted_iota(jnp.int32, (384, WIN), 1), which)
-        pick = (k == 379 - (p * 69 + q * 3 + r)).astype(F32).astype(BF)
+def prep_kernel(table_ref, mask_ref, tok_hbm, bias1_ref, bias2_ref, valid_ref, low_hbm, high_hbm,
+                wide_ref, rows_ref, sem, *, shape):
+    nlat, nlon, tile_rows, tile_cols = shape
+    copies = start_copies([(tok_hbm.at[:, pl.ds(0, SLON)], low_hbm),
+                           (tok_hbm.at[:, pl.ds(tile_cols - SLON, SLON)], high_hbm)], sem)
+    lat, lon, lats = lax.axis_index("lat"), lax.axis_index("lon"), nlat // tile_rows
+    first, second = order_columns()
+    wide_ref[...] = jnp.zeros_like(wide_ref)
+    wide_ref[:, : table_ref.shape[1]] = table_ref[...] * LOG2E
+    for t, (p, q, r) in enumerate(first):
+        start = p * 69 + q * 3 + r
+        rows_ref[8 * t : 8 * t + 8, :] = wide_ref[:, start : start + 384]
+    rows = rows_ref[...]
+    high = rows.astype(BF)
+    low = (rows - high.astype(F32)).astype(BF)
+    k = lax.broadcasted_iota(jnp.int32, (384, WIN), 0)
+    for which, out_ref in enumerate((bias1_ref, bias2_ref)):
+        p, q, r = lane_pqr(lax.broadcasted_iota(jnp.int32, (1, WIN), 1), which)
+        pick = jnp.where(k == 379 - (p * 69 + q * 3 + r), 1.0, 0.0).astype(BF)
         full = jnp.dot(high, pick, preferred_element_type=F32) + jnp.dot(low, pick, preferred_element_type=F32)
-        full = jnp.transpose(full.reshape(WIN, HEADS, WIN), (1, 0, 2))
-        out_refs[which][...] = full
-    nlat, nlon, tile_rows, tile_cols = shape
-    row = lax.broadcasted_iota(jnp.int32, (48, nlat), 0)
+        full = full.reshape(WIN, HEADS, WIN)
+        if which == 1:
+            full = jnp.stack([full[first.index(pqr)] for pqr in second])
+        out_ref[...] = jnp.transpose(full, (1, 0, 2))
+    row = lax.broadcasted_iota(jnp.int32, (48, 1), 0)
     col = lax.broadcasted_iota(jnp.int32, (48, nlat), 1)
     want = lax.rem(lat * tile_rows - SLAT + row + nlat, nlat)
-    pick_rows = (want == col).astype(F32).astype(BF)
+    pick_rows = jnp.where(want == col, 1.0, 0.0).astype(BF)
     mask = (mask_ref[...] > 0).astype(F32).astype(BF)
     picked = jnp.dot(pick_rows, mask, preferred_element_type=F32).astype(BF)
+    row = lax.broadcasted_iota(jnp.int32, (nlon, 3 * WIN), 0)
+    row48 = lax.broadcasted_iota(jnp.int32, (48, 3 * WIN), 0)
+    lane = lax.broadcasted_iota(jnp.int32, (1, 3 * WIN), 1)
     for which in range(2):
-        row = lax.broadcasted_iota(jnp.int32, (nlon, 3 * WIN), 0)
-        lane = lax.broadcasted_iota(jnp.int32, (nlon, 3 * WIN), 1)
-        _, q, _ = lane_pqr(lane % WIN, which)
+        p, q, _ = lane_pqr(lane % WIN, which)
         want = lax.rem(lon * tile_cols - SLON + 12 * (lane // WIN) + q + nlon, nlon)
-        pick_cols = (want == row).astype(F32).astype(BF)
+        pick_cols = jnp.where(want == row, 1.0, 0.0).astype(BF)
         spread = jnp.dot(picked, pick_cols, preferred_element_type=F32)
-        row = lax.broadcasted_iota(jnp.int32, (48, 3 * WIN), 0)
-        lane = lax.broadcasted_iota(jnp.int32, (48, 3 * WIN), 1)
-        p, _, _ = lane_pqr(lane % WIN, which)
-        lane1 = lax.broadcasted_iota(jnp.int32, (1, 3 * WIN), 1)
         for window in (range(1, 6) if which == 0 else (0, 6)):
-            value = jnp.sum(jnp.where(row == 6 * window + p, spread, 0.0), axis=0, keepdims=True)
+            value = jnp.sum(jnp.where(row48 == 6 * window + p, spread, 0.0), axis=0, keepdims=True)
             ok = value > 0.5
             if window == 0:
-                ok = ok & ((lat > 0) | (lane1 % WIN >= HALF))
+                ok = ok & ((lat > 0) | (lane % WIN >= HALF))
             if window == 6:
-                ok = ok & ((lat < lats - 1) | (lane1 % WIN < HALF))
+                ok = ok & ((lat < lats - 1) | (lane % WIN < HALF))
             value = jnp.where(ok, 0.0, NEG)
-            for k in range(3):
-                valid_ref[3 * window + k] = value[:, k * WIN : (k + 1) * WIN]
+            for n in range(3):
+                valid_ref[3 * window + n] = value[:, n * WIN : (n + 1) * WIN]
+    for copy in copies:
+        copy.wait()
 
 
 def layer_norm(values, gain, offset):
@@ -109,25 +114,22 @@
 
 def attend(q, k, v, bias_of, block_mask):
     n = q.shape[0]
-    head_of = lax.broadcasted_iota(jnp.int32, (1, 256), 1) // HEAD_DIM
+    head_of = lax.broadcasted_iota(jnp.int32, (1, 2 * HEAD_DIM), 1) // HEAD_DIM
+    ones = jnp.ones((WIN, 2 * HEAD_DIM), BF)
     parts = []
-    for g in range(2):
-        lanes = slice(256 * g, 256 * g + 256)
+    for g in range(HEADS // 2):
+        lanes = slice(2 * HEAD_DIM * g, 2 * HEAD_DIM * (g + 1))
         qg = q[:, lanes]
-        stacked = jnp.concatenate([jnp.where(head_of == j, qg, 0.0) for j in range(4)], axis=0).astype(BF)
+        stacked = jnp.concatenate([jnp.where(head_of == j, qg, 0.0) for j in range(2)], axis=0).astype(BF)
         scores = lax.dot_general(stacked, k[:, lanes], (((1,), (1,)), ((), ())), preferred_element_type=F32)
-        probs, scale = [], []
-        for j in range(4):
-            s = scores[j * n : (j + 1) * n] + (bias_of(4 * g + j) + block_mask)
-            powered = jnp.exp2(s - jnp.max(s, axis=-1, keepdims=True))
-            scale.append(1.0 / jnp.sum(powered, axis=-1, keepdims=True))
-            probs.append(powered)
+        probs = []
+        for j in range(2):
+            s = scores[j * n : (j + 1) * n] + (bias_of(2 * g + j) + block_mask)
+            probs.append(jnp.exp2(s - jnp.max(s, axis=-1, keepdims=True)))
         probs = jnp.concatenate(probs, axis=0).astype(BF)
-        out = jnp.dot(probs, v[:, lanes], preferred_element_type=F32)
-        context = out[:n] * scale[0]
-        for j in range(1, 4):
-            context = jnp.where(head_of == j, out[j * n : (j + 1) * n] * scale[j], context)
-        parts.append(context)
+        out = jnp.dot(probs, jnp.concatenate([v[:, lanes], ones], axis=1), preferred_element_type=F32)
+        out = jnp.where(jnp.concatenate([head_of, head_of], axis=1) == 0, out[:n], out[n:])
+        parts.append(out[:, : 2 * HEAD_DIM] / out[:, 2 * HEAD_DIM :])
     return jnp.concatenate(parts, axis=1)
 
 
@@ -143,8 +145,8 @@
 
 
 def block_masks(valid, first, n):
-    t = lax.broadcasted_iota(jnp.int32, (n, WIN), 0) + first
-    u = lax.broadcasted_iota(jnp.int32, (n, WIN), 1)
+    t = lax.broadcasted_iota(jnp.int32, (n, 1), 0) + first
+    u = lax.broadcasted_iota(jnp.int32, (1, WIN), 1)
     joint = jnp.where(t == u, 0.0, jnp.broadcast_to(valid, (n, WIN)))
     same = (t // QUART) % 2 == (u // QUART) % 2
     return joint, jnp.where(same, joint, NEG)
@@ -375,24 +377,24 @@
     any_space = pl.BlockSpec(memory_space=pl.ANY)
     params = pltpu.CompilerParams(vmem_limit_bytes=VMEM_LIMIT)
     shape = (*key_mask.shape, rows, cols)
-    place = jnp.stack([lax.axis_index("lat"), lax.axis_index("lon")]).astype(jnp.int32)
-    table = jnp.pad(rel_bias, ((0, 0), (0, 9)))
-    bias1, bias2, valid = pl.pallas_call(
+    edge = jax.ShapeDtypeStruct((rows, SLON, LEV, C), BF)
+    bias1, bias2, valid, low, high = pl.pallas_call(
         functools.partial(prep_kernel, shape=shape),
-        out_shape=[jax.ShapeDtypeStruct((HEADS, WIN, WIN), F32)] * 2 + [jax.ShapeDtypeStruct((21, 1, WIN), F32)],
-        in_specs=[pl.BlockSpec(memory_space=pltpu.SMEM), vmem, vmem],
-        out_specs=[vmem] * 3,
-        scratch_shapes=[pltpu.VMEM((8 * WIN, 384), F32)],
-        compiler_params=params,
+        out_shape=[jax.ShapeDtypeStruct((HEADS, WIN, WIN), F32)] * 2 + [jax.ShapeDtypeStruct((21, 1, WIN), F32)]
+        + [edge] * 2,
+        in_specs=[vmem, vmem, any_space],
+        out_specs=[vmem] * 3 + [any_space] * 2,
+        scratch_shapes=[pltpu.VMEM((HEADS, 768), F32), pltpu.VMEM((8 * WIN, 384), F32), pltpu.SemaphoreType.DMA((2,))],
+        compiler_params=pltpu.CompilerParams(vmem_limit_bytes=60 * 1024 * 1024),
         cost_estimate=pl.CostEstimate(flops=10**9, bytes_accessed=5 * 10**6, transcendentals=0),
         name="prep",
-    )(place, table, key_mask)
-
-    def column(at):
-        return jnp.concatenate([north[:, at], tokens[:, at], south[:, at]], axis=0)
-
-    west = passed_along(column(slice(cols - SLON, cols)), "lon", 1)
-    east = passed_along(column(slice(0, SLON)), "lon", -1)
+    )(rel_bias, key_mask, tokens)
+
+    def column(mid, at):
+        return jnp.concatenate([north[:, at], mid, south[:, at]], axis=0)
+
+    west = passed_along(column(high, slice(cols - SLON, cols)), "lon", 1)
+    east = passed_along(column(low, slice(0, SLON)), "lon", -1)
 
     g1, b1 = norm1_gain.reshape(1, C), norm1_bias.reshape(1, C)
     g2, b2 = norm2_gain.reshape(1, C), norm2_bias.reshape(1, C)

time: 84 us -> 129 us (1.54)
  the two profiles are of different devices: /device:TPU:6 before, /device:TPU:0 now
where the time goes in v2:
time: 129 us
  Pallas kernels  112 us (87%)
  starting transfers between devices  9.36 us (7%)
  other arithmetic  3.95 us (3%)
  local copies, waits for them, and re-layouts  2.68 us (2%)
    pallas_call x1, Pallas kernels, per_device(): pl.pallas_call(functools.partial(prep_kernel, shape=shape), out_shape=[ja...  57.3 us
    pallas_call x1, Pallas kernels, per_device(): pl.pallas_call(edge_kernel, out_shape=jax.ShapeDtypeStruct(tokens.shape,...  33 us
    pallas_call x1, Pallas kernels, per_device(): pl.pallas_call(inner_kernel, out_shape=jax.ShapeDtypeStruct(tokens.shape,...  22.1 us
    ppermute x4, starting transfers between devices, passed_along(): lax.ppermute(block, axis, [((i - distance) % size, i) for i in range(size)])  9.36 us
    concatenate x2, other arithmetic, column(): return jnp.concatenate([north[:, at], mid, south[:, at]], axis=0)  3.95 us
  transfers between devices with their start and end apart: 4, of which 0 were waited for; matrix products, arithmetic and copies ran while one was open for 2% of the time, Pallas kernels for 62%

profile of v2, /device:TPU:0, one launch (start us, length us, event | category | flops | bytes accessed | tf_op | source)
XLA Modules:
  0.0 128.8 jit_solution(3862578163535042247)
XLA Ops:
  0.0 1.3 fusion
  1.3 1.6 %collective-permute-start = (bf16[3,24,4,512]{3,2,1,0:T(4,128)(2,1)S(1)}, bf16[3,24,4,512]{3,2,1,0:T(4,128)(2,1)S(1)}, u32[]{:S(2)}, u32[]{:S(2)}) collective-permute-start(bf16[3,24,4,512]{3,2,1,0:T(4,128)(2,1)S(1)} %get-tuple-element.15), channel_id=1, source_target_pairs={{7,0},{0,1},{1,2},{2,3},{3,4},{4,5},{5,6},{6,7},{15,8},{8,9},{9,10... | collective-permute-start | bytes 884744 | tf_op jit(solution)/shard_map/ppermute | solution.py:367
  2.9 4.7 %collective-permute-start.1 = (bf16[3,24,4,512]{3,2,1,0:T(4,128)(2,1)S(1)}, bf16[3,24,4,512]{3,2,1,0:T(4,128)(2,1)S(1)}, u32[]{:S(2)}, u32[]{:S(2)}) collective-permute-start(bf16[3,24,4,512]{3,2,1,0:T(4,128)(2,1)S(1)} %get-tuple-element.16), channel_id=1, source_target_pairs={{1,0},{2,1},{3,2},{4,3},{5,4},{6,5},{7,6},{0,7},{9,8},{10,9},{11,1... | collective-permute-start | bytes 884744 | tf_op jit(solution)/shard_map/ppermute | solution.py:367
  7.6 0.0 copy-start.2
  7.6 0.0 copy-start.7
  7.6 0.0 copy-start.8
  7.6 0.0 copy-start.9
  7.6 0.0 copy-start.10
  7.6 57.3 %prep.1 = (f32[8,144,144]{2,1,0:T(8,128)}, f32[8,144,144]{2,1,0:T(8,128)}, f32[21,1,144]{2,1,0:T(1,128)}, bf16[36,6,4,512]{3,2,1,0:T(4,128)(2,1)}, bf16[36,6,4,512]{3,2,1,0:T(4,128)(2,1)}) custom-call(f32[8,759]{1,0:T(8,128)} %table_ref.1, s32[288,384]{1,0:T(8,128)} %mask_ref.1, bf16[36,24,4,512]{3,2,1,0:T(4,128)(2,1)} %tok_hbm.5), custom_call_target="tpu_custom_call" | custom-call | flops 1000000000 | bytes 5000000 | tf_op jit(solution)/shard_map/prep/pallas_call | solution.py:381
  64.9 0.0 collective-permute-done.north_hbm
  64.9 0.0 copy-start.5
  64.9 0.1 fusion.1
  65.0 0.0 collective-permute-done.1.south_hbm
  65.0 0.0 copy-start.1
  65.0 0.1 fusion.2
  65.0 0.0 copy-start
  65.0 0.0 copy-start.6
  65.1 2.0 %pad_maximum_fusion.1 = bf16[42,6,4,512]{3,2,1,0:T(4,128)(2,1)S(1)} fusion(bf16[3,6,4,512]{3,2,1,0:T(4,128)(2,1)S(1)} %get-tuple-element.19, bf16[36,6,4,512]{3,2,1,0:T(4,128)(2,1)} %get-tuple-element.13, bf16[3,6,4,512]{3,2,1,0:T(4,128)(2,1)S(1)} %get-tuple-element.17), kind=kLoop, calls=%fused_computation.1 | loop fusion | flops 1032192 | bytes 2064384 | tf_op jit(solution)/shard_map/concatenate | solution.py:394
  67.1 2.8 %collective-permute-start.3 = (bf16[42,6,4,512]{3,2,1,0:T(4,128)(2,1)S(1)}, bf16[42,6,4,512]{3,2,1,0:T(4,128)(2,1)S(1)}, u32[]{:S(2)}, u32[]{:S(2)}) collective-permute-start(bf16[42,6,4,512]{3,2,1,0:T(4,128)(2,1)S(1)} %pad_maximum_fusion.1), channel_id=1, source_target_pairs={{8,0},{16,8},{24,16},{32,24},{40,32},{48,40},{56,48},{64,56},{72,6... | collective-permute-start | bytes 3096584 | tf_op jit(solution)/shard_map/ppermute | solution.py:367
  69.9 1.9 %pad_maximum_fusion = bf16[42,6,4,512]{3,2,1,0:T(4,128)(2,1)S(1)} fusion(bf16[3,6,4,512]{3,2,1,0:T(4,128)(2,1)S(1)} %get-tuple-element.20, bf16[36,6,4,512]{3,2,1,0:T(4,128)(2,1)} %get-tuple-element.12, bf16[3,6,4,512]{3,2,1,0:T(4,128)(2,1)S(1)} %get-tuple-element.18), kind=kLoop, calls=%fused_computation | loop fusion | flops 1032192 | bytes 2064384 | tf_op jit(solution)/shard_map/concatenate | solution.py:394
  71.8 0.3 collective-permute-start.2
  72.1 0.0 copy-done.2
  72.1 0.0 copy-done.7
  72.1 0.0 copy-done.8
  72.1 0.0 copy-done.9
  72.1 0.0 copy-done.10
  72.1 0.0 copy-done.5
  72.1 0.0 copy-done.1
  72.1 0.0 copy-done
  72.2 0.0 copy-done.6
  72.2 0.0 copy-start.3
  72.2 1.3 copy-done.3
  73.4 0.0 copy-start.4
  73.4 22.1 %inner.1.part_hbm = bf16[36,24,4,512]{3,2,1,0:T(4,128)(2,1)} custom-call(bf16[36,24,4,512]{3,2,1,0:T(4,128)(2,1)} %tok_hbm.5, bf16[512,1536]{1,0:T(8,128)(2,1)S(1)} %copy-done.2, f32[8,144,144]{2,1,0:T(8,128)S(1)} %copy-done.3, bf16[512,512]{1,0:T(8,128)(2,1)S(1)} %copy-done.5, bf16[512,2048]{1,0:T(8,128)(2,1)S(1)} %copy-done, ...), custom_call_target="tpu_custom_call" | custom-call | flops 12000000000 | bytes 12000000 | tf_op jit(solution)/shard_map/inner/pallas_call | solution.py:405
  95.6 0.0 collective-permute-done.3.east_hbm
  95.6 0.0 collective-permute-done.2.west_hbm
  95.6 0.0 copy-done.4
  95.6 33.0 %edge.1 = bf16[36,24,4,512]{3,2,1,0:T(4,128)(2,1)} custom-call(bf16[36,24,4,512]{3,2,1,0:T(4,128)(2,1)} %inner.1.part_hbm, bf16[36,24,4,512]{3,2,1,0:T(4,128)(2,1)} %tok_hbm.5, bf16[42,6,4,512]{3,2,1,0:T(4,128)(2,1)S(1)} %collective-permute-done.2.west_hbm, ...), custom_call_target="tpu_custom_call", output_to_operand_aliasing={{}: (0, {})} | custom-call | flops 16000000000 | bytes 16000000 | tf_op jit(solution)/shard_map/edge/pallas_call | solution.py:422
Async XLA Ops:
  1.3 63.6 %collective-permute-start = (bf16[3,24,4,512]{3,2,1,0:T(4,128)(2,1)S(1)}, bf16[3,24,4,512]{3,2,1,0:T(4,128)(2,1)S(1)}, u32[]{:S(2)}, u32[]{:S(2)}) collective-permute-start(bf16[3,24,4,512]{3,2,1,0:T(4,128)(2,1)S(1)} %get-tuple-element.15), channel_id=1, source_target_pairs={{7,0},{0,1},{1,2},{2,3},{3,4},{4,5},{5,6},{6,7},{15,8},{8,9},{9,10... | collective-permute-start | bytes 884744 | tf_op jit(solution)/shard_map/ppermute | solution.py:367
  2.9 62.1 %collective-permute-start.1 = (bf16[3,24,4,512]{3,2,1,0:T(4,128)(2,1)S(1)}, bf16[3,24,4,512]{3,2,1,0:T(4,128)(2,1)S(1)}, u32[]{:S(2)}, u32[]{:S(2)}) collective-permute-start(bf16[3,24,4,512]{3,2,1,0:T(4,128)(2,1)S(1)} %get-tuple-element.16), channel_id=1, source_target_pairs={{1,0},{2,1},{3,2},{4,3},{5,4},{6,5},{7,6},{0,7},{9,8},{10,9},{11,1... | collective-permute-start | bytes 884744 | tf_op jit(solution)/shard_map/ppermute | solution.py:367
  7.6 64.5 %copy-start.2 = (bf16[512,1536]{1,0:T(8,128)(2,1)S(1)}, bf16[512,1536]{1,0:T(8,128)(2,1)}, u32[]{:S(2)}) copy-start(bf16[512,1536]{1,0:T(8,128)(2,1)} %qkv_hbm.3) | copy-start | bytes 4718596
  7.6 64.5 %copy-start.7 = (f32[512]{0:T(512)S(1)}, f32[512]{0:T(512)}, u32[]{:S(2)}) copy-start(f32[512]{0:T(512)} %param.12) | copy-start | bytes 6148
  7.6 64.5 %copy-start.8 = (f32[512]{0:T(512)S(1)}, f32[512]{0:T(512)}, u32[]{:S(2)}) copy-start(f32[512]{0:T(512)} %param.13) | copy-start | bytes 6148
  7.6 64.5 %copy-start.9 = (f32[512]{0:T(512)S(1)}, f32[512]{0:T(512)}, u32[]{:S(2)}) copy-start(f32[512]{0:T(512)} %param.18) | copy-start | bytes 6148
  7.6 64.5 %copy-start.10 = (f32[512]{0:T(512)S(1)}, f32[512]{0:T(512)}, u32[]{:S(2)}) copy-start(f32[512]{0:T(512)} %param.19) | copy-start | bytes 6148
  64.9 7.2 %copy-start.5 = (bf16[512,512]{1,0:T(8,128)(2,1)S(1)}, bf16[512,512]{1,0:T(8,128)(2,1)}, u32[]{:S(2)}) copy-start(bf16[512,512]{1,0:T(8,128)(2,1)} %proj_hbm.3) | copy-start | bytes 1572868
  65.0 7.2 %copy-start.1 = (bf16[2048,512]{1,0:T(8,128)(2,1)S(1)}, bf16[2048,512]{1,0:T(8,128)(2,1)}, u32[]{:S(2)}) copy-start(bf16[2048,512]{1,0:T(8,128)(2,1)} %fc2_hbm.3) | copy-start | bytes 6291460
  65.0 7.1 %copy-start = (bf16[512,2048]{1,0:T(8,128)(2,1)S(1)}, bf16[512,2048]{1,0:T(8,128)(2,1)}, u32[]{:S(2)}) copy-start(bf16[512,2048]{1,0:T(8,128)(2,1)} %fc1_hbm.3) | copy-start | bytes 6291460
  65.0 7.1 %copy-start.6 = (f32[21,1,144]{2,1,0:T(1,128)S(1)}, f32[21,1,144]{2,1,0:T(1,128)}, u32[]{:S(2)}) copy-start(f32[21,1,144]{2,1,0:T(1,128)} %get-tuple-element.11.valid_ref) | copy-start | bytes 36292
  67.1 28.5 %collective-permute-start.3 = (bf16[42,6,4,512]{3,2,1,0:T(4,128)(2,1)S(1)}, bf16[42,6,4,512]{3,2,1,0:T(4,128)(2,1)S(1)}, u32[]{:S(2)}, u32[]{:S(2)}) collective-permute-start(bf16[42,6,4,512]{3,2,1,0:T(4,128)(2,1)S(1)} %pad_maximum_fusion.1), channel_id=1, source_target_pairs={{8,0},{16,8},{24,16},{32,24},{40,32},{48,40},{56,48},{64,56},{72,6... | collective-permute-start | bytes 3096584 | tf_op jit(solution)/shard_map/ppermute | solution.py:367
  71.8 23.8 %collective-permute-start.2 = (bf16[42,6,4,512]{3,2,1,0:T(4,128)(2,1)S(1)}, bf16[42,6,4,512]{3,2,1,0:T(4,128)(2,1)S(1)}, u32[]{:S(2)}, u32[]{:S(2)}) collective-permute-start(bf16[42,6,4,512]{3,2,1,0:T(4,128)(2,1)S(1)} %pad_maximum_fusion), channel_id=1, source_target_pairs={{120,0},{0,8},{8,16},{16,24},{24,32},{32,40},{40,48},{48,56},{56,6... | collective-permute-start | bytes 3096584 | tf_op jit(solution)/shard_map/ppermute | solution.py:367
  72.2 1.3 copy-start.3
  73.4 22.2 %copy-start.4 = (f32[8,144,144]{2,1,0:T(8,128)S(1)}, f32[8,144,144]{2,1,0:T(8,128)}, u32[]{:S(2)}) copy-start(f32[8,144,144]{2,1,0:T(8,128)} %get-tuple-element.14.bias2_hbm) | copy-start | bytes 1990660

commit v3 on v2

--- a/solution.py
+++ b/solution.py
@@ -44,11 +44,8 @@
     return 3 * half + cell // 12, cell % 12, r
 
 
-def prep_kernel(table_ref, mask_ref, tok_hbm, bias1_ref, bias2_ref, valid_ref, low_hbm, high_hbm,
-                wide_ref, rows_ref, sem, *, shape):
+def prep_kernel(table_ref, mask_ref, bias1_ref, bias2_ref, valid_ref, wide_ref, rows_ref, *, shape):
     nlat, nlon, tile_rows, tile_cols = shape
-    copies = start_copies([(tok_hbm.at[:, pl.ds(0, SLON)], low_hbm),
-                           (tok_hbm.at[:, pl.ds(tile_cols - SLON, SLON)], high_hbm)], sem)
     lat, lon, lats = lax.axis_index("lat"), lax.axis_index("lon"), nlat // tile_rows
     first, second = order_columns()
     wide_ref[...] = jnp.zeros_like(wide_ref)
@@ -92,8 +89,6 @@
             value = jnp.where(ok, 0.0, NEG)
             for n in range(3):
                 valid_ref[3 * window + n] = value[:, n * WIN : (n + 1) * WIN]
-    for copy in copies:
-        copy.wait()
 
 
 def layer_norm(values, gain, offset):
@@ -134,7 +129,8 @@
 
 
 def feed(middle, gain, offset, fc1_ref, fc2_ref):
-    normed = layer_norm(middle, gain, offset).astype(BF)
+    normed = jnp.concatenate([layer_norm(middle[at : at + 48], gain, offset).astype(BF)
+                              for at in range(0, middle.shape[0], 48)], axis=0)
     total = None
     for j in range(4):
         v = jnp.dot(normed, fc1_ref[:, 512 * j : 512 * j + 512], preferred_element_type=F32)
@@ -152,10 +148,14 @@
     return joint, jnp.where(same, joint, NEG)
 
 
-def put_levels(levels, into_ref, at, step):
+def put_block(block, gain, offset, normed_to=(), raw_to=()):
+    levels = by_level(block)
     for pair in range(2):
         rows = jnp.concatenate([levels[level] for level in PAIRS[pair]], axis=0)
-        into_ref[pl.ds(pl.multiple_of(at + step * pair, 8), HALF), :] = rows
+        normed = layer_norm(rows, gain, offset)
+        for places, value in ((raw_to, rows), (normed_to, normed)):
+            for ref, at, step in places:
+                ref[pl.ds(pl.multiple_of(at + step * pair, 8), HALF), :] = value
 
 
 def take_levels(from_ref, at, step):
@@ -184,7 +184,7 @@
 
 
 def inner_kernel(tok_hbm, qkv_hbm, bias_hbm, proj_hbm, fc1_hbm, fc2_hbm, g1_ref, b1_ref, valid_ref, g2_ref, b2_ref,
-                 out_hbm, tok_ref, qkv_ref, bias_ref, proj_ref, fc1_ref, fc2_ref, out_ref, xs_ref, norm_ref, q_ref,
+                 out_hbm, tok_ref, qkv_ref, bias_ref, proj_ref, fc1_ref, fc2_ref, out_ref, xs_ref, q_ref,
                  kv_ref, ctx_ref, sem, out_sem):
     steps = tok_ref.shape[0] // WLAT
     inner = (pl.ds(SLAT, WLAT * steps), pl.ds(SLON, WLON))
@@ -199,8 +199,8 @@
         at = pl.multiple_of(big * i, big)
         x = tok_ref[pl.ds(WLAT * i, WLAT)]
         for h in range(2):
-            put_levels(by_level(x[:, 6 * h : 6 * h + 6]), xs_ref, at + HALF * h, WIN)
-        norm_ref[pl.ds(at, big), :] = layer_norm(xs_ref[pl.ds(at, big), :], g1_ref[...], b1_ref[...]).astype(BF)
+            put_block(x[:, 6 * h : 6 * h + 6], g1_ref[...], b1_ref[...], [(q_ref, at + HALF * h, WIN)],
+                      [(xs_ref, at + HALF * h, WIN)])
         return carry
 
     lax.fori_loop(0, steps, load, 0)
@@ -208,7 +208,7 @@
 
     def project(i, carry):
         rows = pl.ds(pl.multiple_of(part * i, 16), part)
-        normed = norm_ref[rows, :]
+        normed = q_ref[rows, :].astype(BF)
         q_ref[rows, :] = jnp.dot(normed, qkv_ref[:, :C], preferred_element_type=F32) * Q_SCALE
         kv_ref[rows, :] = jnp.dot(normed, qkv_ref[:, C:], preferred_element_type=F32).astype(BF)
         return carry
@@ -235,16 +235,20 @@
 
     lax.fori_loop(0, 2, rest, 0)
 
+    def out_copy(i):
+        return pltpu.make_async_copy(out_ref.at[pl.ds(WLAT * i, WLAT)],
+                                     out_hbm.at[pl.ds(SLAT + WLAT * i, WLAT), pl.ds(SLON, WLON)], out_sem.at[i])
+
     def store(i, carry):
         for h in range(2):
             levels = take_levels(xs_ref, pl.multiple_of(big * i, big) + HALF * h, WIN)
             out_ref[pl.ds(WLAT * i, WLAT), 6 * h : 6 * h + 6] = from_level(levels, (WLAT, 6, LEV, C))
+        out_copy(i).start()
         return carry
 
     lax.fori_loop(0, steps, store, 0)
-    out = pltpu.make_async_copy(out_ref, out_hbm.at[inner], out_sem)
-    out.start()
-    out.wait()
+    for i in range(steps):
+        out_copy(i).wait()
 
 
 def edge_kernel(part_hbm, tok_hbm, west_hbm, east_hbm, north_hbm, south_hbm, qkv_hbm, bias1_hbm, bias2_hbm, proj_hbm,
@@ -265,9 +269,6 @@
         (fc1_hbm, fc1_ref), (fc2_hbm, fc2_ref)], sem)
     big = 2 * WIN
 
-    def normed_rows(ref, first, count):
-        return layer_norm(ref[first : first + count, :], g1_ref[...], b1_ref[...])
-
     for copy in copies[:6]:
         copy.wait()
 
@@ -275,14 +276,13 @@
         at = pl.multiple_of(big * i, big)
         own_rows, halo_rows = pl.ds(WLAT * i, WLAT), pl.ds(2 * SLAT + WLAT * i, WLAT)
         for side, halo_ref in ((0, west_ref), (1, east_ref)):
-            own = by_level(own_ref[side, own_rows])
-            put_levels(own, xs_ref, big * side + (HALF if side == 0 else 0), WIN)
-            put_levels(by_level(halo_ref[halo_rows]), xs_ref, big * side + (0 if side == 0 else HALF), WIN)
-            put_levels(own, mid_ref, at + WIN * side, HALF)
-        normed = normed_rows(xs_ref, 0, 2 * big)
-        kv_ref[: 2 * big, :] = jnp.dot(normed.astype(BF), qkv_ref[:, C:], preferred_element_type=F32).astype(BF)
-        own = jnp.concatenate([normed[HALF:WIN], normed[WIN + HALF : big], normed[big : big + HALF],
-                               normed[big + WIN : big + WIN + HALF]], axis=0)
+            put_block(own_ref[side, own_rows], g1_ref[...], b1_ref[...],
+                      [(xs_ref, big * side + (HALF if side == 0 else 0), WIN)], [(mid_ref, at + WIN * side, HALF)])
+            put_block(halo_ref[halo_rows], g1_ref[...], b1_ref[...],
+                      [(xs_ref, big * side + (0 if side == 0 else HALF), WIN)])
+        kv_ref[: 2 * big, :] = jnp.dot(xs_ref[: 2 * big, :].astype(BF), qkv_ref[:, C:],
+                                       preferred_element_type=F32).astype(BF)
+        own = jnp.concatenate([xs_ref[at : at + HALF, :] for at in (HALF, WIN + HALF, big, big + WIN)], axis=0)
         q_ref[...] = jnp.dot(own.astype(BF), qkv_ref[:, :C], preferred_element_type=F32) * Q_SCALE
         contexts = []
         for side in range(2):
@@ -310,16 +310,15 @@
         halo = jnp.concatenate([west_ref[outside], near_ref[...], east_ref[outside]], axis=1)
         for k in range(3):
             window = slice(WLON * k, WLON * k + WLON)
-            put_levels(by_level(own[:, window]), xs_ref, big * k + first, WIN)
-            put_levels(by_level(halo[:, window]), xs_ref, big * k + HALF - first, WIN)
-            if k == 1:
-                put_levels(by_level(own[:, window]), mid_ref, at, HALF)
+            mid = k == 1
+            put_block(own[:, window], g1_ref[...], b1_ref[...],
+                      [(xs_ref, big * k + first, WIN)] + ([(q_ref, 0, HALF)] if mid else []),
+                      [(mid_ref, at, HALF)] if mid else [])
+            put_block(halo[:, window], g1_ref[...], b1_ref[...], [(xs_ref, big * k + HALF - first, WIN)])
         corner = jnp.concatenate([strip_ref[which, :, cols - SLON :], strip_ref[which, :, :SLON]], axis=1)
-        put_levels(by_level(corner), mid_ref, at + WIN, HALF)
-        kv_ref[...] = jnp.dot(normed_rows(xs_ref, 0, 3 * big).astype(BF), qkv_ref[:, C:],
-                              preferred_element_type=F32).astype(BF)
-        q_ref[...] = jnp.dot(normed_rows(mid_ref, at, big).astype(BF), qkv_ref[:, :C],
-                             preferred_element_type=F32) * Q_SCALE
+        put_block(corner, g1_ref[...], b1_ref[...], [(q_ref, WIN, HALF)], [(mid_ref, at + WIN, HALF)])
+        kv_ref[...] = jnp.dot(xs_ref[...].astype(BF), qkv_ref[:, C:], preferred_element_type=F32).astype(BF)
+        q_ref[...] = jnp.dot(q_ref[...].astype(BF), qkv_ref[:, :C], preferred_element_type=F32) * Q_SCALE
         contexts = {}
         for k in range(3):
             masks = block_masks(valid_ref[18 * which + k], first, HALF)
@@ -343,21 +342,33 @@
 
     lax.fori_loop(0, 3, rest, 0)
 
+    def side_copy(i, side):
+        return pltpu.make_async_copy(
+            own_ref.at[side, pl.ds(WLAT * i, WLAT)],
+            out_hbm.at[pl.ds(SLAT + WLAT * i, WLAT), pl.ds(side * (cols - SLON), SLON)], out_sem.at[2 * i + side])
+
     def store(i, carry):
         at = pl.multiple_of(big * i, big)
         for side in range(2):
             block = from_level(take_levels(mid_ref, at + WIN * side, HALF), (WLAT, SLON, LEV, C))
             own_ref[side, pl.ds(WLAT * i, WLAT)] = block
+            side_copy(i, side).start()
         return carry
 
     lax.fori_loop(0, steps, store, 0)
+    outs = []
     for which in range(2):
         at = big * (steps + which)
         strip_ref[which, :, SLON : SLON + WLON] = from_level(take_levels(mid_ref, at, HALF), (SLAT, WLON, LEV, C))
         block = from_level(take_levels(mid_ref, at + WIN, HALF), (SLAT, WLON, LEV, C))
         strip_ref[which, :, cols - SLON :] = block[:, :SLON]
         strip_ref[which, :, :SLON] = block[:, SLON:]
-    outs = start_copies([(here, out_hbm.at[at]) for here, at in places], out_sem)
+        outs.append(pltpu.make_async_copy(strip_ref.at[which], out_hbm.at[strip_at[which]],
+                                          out_sem.at[2 * steps + which]))
+        outs[-1].start()
+    for i in range(steps):
+        for side in range(2):
+            side_copy(i, side).wait()
     for copy in outs:
         copy.wait()
 
@@ -377,24 +388,22 @@
     any_space = pl.BlockSpec(memory_space=pl.ANY)
     params = pltpu.CompilerParams(vmem_limit_bytes=VMEM_LIMIT)
     shape = (*key_mask.shape, rows, cols)
-    edge = jax.ShapeDtypeStruct((rows, SLON, LEV, C), BF)
-    bias1, bias2, valid, low, high = pl.pallas_call(
+    bias1, bias2, valid = pl.pallas_call(
         functools.partial(prep_kernel, shape=shape),
-        out_shape=[jax.ShapeDtypeStruct((HEADS, WIN, WIN), F32)] * 2 + [jax.ShapeDtypeStruct((21, 1, WIN), F32)]
-        + [edge] * 2,
-        in_specs=[vmem, vmem, any_space],
-        out_specs=[vmem] * 3 + [any_space] * 2,
-        scratch_shapes=[pltpu.VMEM((HEADS, 768), F32), pltpu.VMEM((8 * WIN, 384), F32), pltpu.SemaphoreType.DMA((2,))],
-        compiler_params=pltpu.CompilerParams(vmem_limit_bytes=60 * 1024 * 1024),
+        out_shape=[jax.ShapeDtypeStruct((HEADS, WIN, WIN), F32)] * 2 + [jax.ShapeDtypeStruct((21, 1, WIN), F32)],
+        in_specs=[vmem, vmem],
+        out_specs=[vmem] * 3,
+        scratch_shapes=[pltpu.VMEM((HEADS, 768), F32), pltpu.VMEM((8 * WIN, 384), F32)],
+        compiler_params=pltpu.CompilerParams(vmem_limit_bytes=56 * 1024 * 1024),
         cost_estimate=pl.CostEstimate(flops=10**9, bytes_accessed=5 * 10**6, transcendentals=0),
         name="prep",
-    )(rel_bias, key_mask, tokens)
-
-    def column(mid, at):
-        return jnp.concatenate([north[:, at], mid, south[:, at]], axis=0)
-
-    west = passed_along(column(high, slice(cols - SLON, cols)), "lon", 1)
-    east = passed_along(column(low, slice(0, SLON)), "lon", -1)
+    )(rel_bias, key_mask)
+
+    def column(at):
+        return jnp.concatenate([north[:, at], tokens[:, at], south[:, at]], axis=0)
+
+    west = passed_along(column(slice(cols - SLON, cols)), "lon", 1)
+    east = passed_along(column(slice(0, SLON)), "lon", -1)
 
     g1, b1 = norm1_gain.reshape(1, C), norm1_bias.reshape(1, C)
     g2, b2 = norm2_gain.reshape(1, C), norm2_bias.reshape(1, C)
@@ -408,9 +417,9 @@
         in_specs=[any_space] * 6 + [vmem] * 5,
         out_specs=any_space,
         scratch_shapes=[inner_shape, pltpu.VMEM((C, 3 * C), BF), table_shape, *weights, inner_shape,
-                        pltpu.VMEM((count, C), F32), pltpu.VMEM((count, C), BF), pltpu.VMEM((count, C), F32),
+                        pltpu.VMEM((count, C), F32), pltpu.VMEM((count, C), F32),
                         pltpu.VMEM((count, 2 * C), BF), pltpu.VMEM((count, C), BF),
-                        pltpu.SemaphoreType.DMA((6,)), pltpu.SemaphoreType.DMA],
+                        pltpu.SemaphoreType.DMA((6,)), pltpu.SemaphoreType.DMA((count // (2 * WIN),))],
         compiler_params=params,
         cost_estimate=pl.CostEstimate(flops=12 * 10**9, bytes_accessed=12 * 10**6, transcendentals=0),
         name="inner",
@@ -429,7 +438,7 @@
                         pltpu.VMEM((C, 3 * C), BF), table_shape, table_shape, *weights,
                         pltpu.VMEM((6 * WIN, C), F32), pltpu.VMEM((2 * WIN, C), F32), pltpu.VMEM((6 * WIN, 2 * C), BF),
                         pltpu.VMEM((own, C), BF), pltpu.VMEM((own, C), F32),
-                        pltpu.SemaphoreType.DMA((14,)), pltpu.SemaphoreType.DMA((4,))],
+                        pltpu.SemaphoreType.DMA((14,)), pltpu.SemaphoreType.DMA((own // WIN,))],
         input_output_aliases={0: 0},
         compiler_params=params,
         cost_estimate=pl.CostEstimate(flops=16 * 10**9, bytes_accessed=16 * 10**6, transcendentals=0),

time: 129 us -> 80.5 us (0.62)
  the two profiles are of different devices: /device:TPU:0 before, /device:TPU:7 now
where the time goes in v3:
time: 80.5 us; the launch traced here: 80.3 us
  Pallas kernels  59.1 us (73%)
  waiting for transfers between devices  6.73 us (8%)
  starting transfers between devices  6.33 us (8%)
  local copies, waits for them, and re-layouts  5.1 us (6%)
  other arithmetic  2.63 us (3%)
    pallas_call x1, Pallas kernels, per_device(): pl.pallas_call(edge_kernel, out_shape=jax.ShapeDtypeStruct(tokens.shape,...  33 us
    pallas_call x1, Pallas kernels, per_device(): pl.pallas_call(inner_kernel, out_shape=jax.ShapeDtypeStruct(tokens.shape,...  21.6 us
    ppermute x4, waiting for transfers between devices, passed_along(): lax.ppermute(block, axis, [((i - distance) % size, i) for i in range(size)])  6.73 us
    ppermute x4, starting transfers between devices, passed_along(): lax.ppermute(block, axis, [((i - distance) % size, i) for i in range(size)])  6.33 us
    pallas_call x1, Pallas kernels, per_device(): pl.pallas_call(functools.partial(prep_kernel, shape=shape), out_shape=[ja...  4.54 us
    slice x3, local copies, waits for them, and re-layouts, column(): return jnp.concatenate([north[:, at], tokens[:, at], south[:, at]], axis=0)  3.08 us
    concatenate x2, other arithmetic, column(): return jnp.concatenate([north[:, at], tokens[:, at], south[:, at]], axis=0)  2.63 us
    slice x1, local copies, waits for them, and re-layouts, per_device(): north = passed_along(tokens[rows - SLAT:], 'lat', 1)  1.96 us
  transfers between devices with their start and end apart: 4, of which 2 were waited for; matrix products, arithmetic and copies ran while one was open for 5% of the time, Pallas kernels for 33%

profile of v3, /device:TPU:7, one launch (start us, length us, event | category | flops | bytes accessed | tf_op | source)
XLA Modules:
  0.0 80.3 jit_solution(4955558150270585053)
XLA Ops:
  0.0 2.0 %fusion.1 = (bf16[3,24,4,512]{3,2,1,0:T(4,128)(2,1)}, bf16[3,24,4,512]{3,2,1,0:T(4,128)(2,1)S(1)}) fusion(bf16[36,24,4,512]{3,2,1,0:T(4,128)(2,1)} %tok_hbm.3), kind=kLoop, calls=%fused_computation.3 | loop fusion | bytes 1179648 | tf_op jit(solution)/shard_map/slice | solution.py:384
  2.0 3.5 %collective-permute-start = (bf16[3,24,4,512]{3,2,1,0:T(4,128)(2,1)}, bf16[3,24,4,512]{3,2,1,0:T(4,128)(2,1)S(1)}, u32[]{:S(2)}, u32[]{:S(2)}) collective-permute-start(bf16[3,24,4,512]{3,2,1,0:T(4,128)(2,1)} %get-tuple-element.13), channel_id=1, source_target_pairs={{7,0},{0,1},{1,2},{2,3},{3,4},{4,5},{5,6},{6,7},{15,8},{8,9},{9,10... | collective-permute-start | bytes 884744 | tf_op jit(solution)/shard_map/ppermute | solution.py:378
  5.5 0.0 collective-permute-start.1
  5.5 3.0 %fusion = (bf16[36,6,4,512]{3,2,1,0:T(4,128)(2,1)S(1)}, bf16[36,6,4,512]{3,2,1,0:T(4,128)(2,1)}) fusion(bf16[36,24,4,512]{3,2,1,0:T(4,128)(2,1)} %tok_hbm.3), kind=kLoop, calls=%fused_computation.2 | loop fusion | bytes 3538944 | tf_op jit(solution)/shard_map/slice | solution.py:403
  8.5 0.0 copy-start
  8.5 0.0 copy-start.1
  8.5 0.0 copy-start.2
  8.5 0.0 copy-start.3
  8.5 0.0 copy-start.4
  8.5 0.0 copy-start.5
  8.5 0.0 copy-start.6
  8.5 0.0 copy-start.7
  8.5 4.5 %prep.1 = (f32[8,144,144]{2,1,0:T(8,128)}, f32[8,144,144]{2,1,0:T(8,128)}, f32[21,1,144]{2,1,0:T(1,128)}) custom-call(f32[8,759]{1,0:T(8,128)} %table_ref.1, s32[288,384]{1,0:T(8,128)} %mask_ref.1), custom_call_target="tpu_custom_call" | custom-call | flops 1000000000 | bytes 5000000 | tf_op jit(solution)/shard_map/prep/pallas_call | solution.py:391
  13.1 0.0 copy-start.8
  13.1 0.0 copy-start.10
  13.1 0.0 collective-permute-done.north_hbm
  13.1 0.1 fusion.2
  13.1 3.5 %collective-permute-done.1.south_hbm = bf16[3,24,4,512]{3,2,1,0:T(4,128)(2,1)S(1)} collective-permute-done((bf16[3,24,4,512]{3,2,1,0:T(4,128)(2,1)S(1)}, bf16[3,24,4,512]{3,2,1,0:T(4,128)(2,1)S(1)}, u32[]{:S(2)}, u32[]{:S(2)}) %collective-permute-start.1) | collective-permute-done | bytes 294944 | tf_op jit(solution)/shard_map/ppermute | solution.py:378
  16.6 0.1 fusion.3
  16.7 1.9 %pad_maximum_fusion = bf16[42,6,4,512]{3,2,1,0:T(4,128)(2,1)S(1)} fusion(bf16[3,6,4,512]{3,2,1,0:T(4,128)(2,1)S(1)} %get-tuple-element.18, bf16[36,6,4,512]{3,2,1,0:T(4,128)(2,1)} %get-tuple-element.12, bf16[3,6,4,512]{3,2,1,0:T(4,128)(2,1)S(1)} %get-tuple-element.16), kind=kLoop, calls=%fused_computation | loop fusion | flops 1032192 | bytes 2064384 | tf_op jit(solution)/shard_map/concatenate | solution.py:403
  18.6 2.6 %collective-permute-start.2 = (bf16[42,6,4,512]{3,2,1,0:T(4,128)(2,1)S(1)}, bf16[42,6,4,512]{3,2,1,0:T(4,128)(2,1)S(1)}, u32[]{:S(2)}, u32[]{:S(2)}) collective-permute-start(bf16[42,6,4,512]{3,2,1,0:T(4,128)(2,1)S(1)} %pad_maximum_fusion), channel_id=1, source_target_pairs={{120,0},{0,8},{8,16},{16,24},{24,32},{32,40},{40,48},{48,56},{56,6... | collective-permute-start | bytes 3096584 | tf_op jit(solution)/shard_map/ppermute | solution.py:378
  21.2 0.7 pad_maximum_fusion.1
  21.9 0.3 collective-permute-start.3
  22.2 0.0 copy-done
  22.2 0.0 copy-done.1
  22.2 0.0 copy-done.2
  22.2 0.0 copy-done.3
  22.2 0.0 copy-done.4
  22.2 0.0 copy-done.5
  22.2 0.0 copy-done.6
  22.2 0.0 copy-done.7
  22.2 0.0 copy-done.8
  22.3 0.0 copy-done.10
  22.3 0.0 copy-start.9
  22.3 21.6 %inner.1.part_hbm = bf16[36,24,4,512]{3,2,1,0:T(4,128)(2,1)} custom-call(bf16[36,24,4,512]{3,2,1,0:T(4,128)(2,1)} %tok_hbm.3, bf16[512,1536]{1,0:T(8,128)(2,1)S(1)} %copy-done.2, f32[8,144,144]{2,1,0:T(8,128)S(1)} %copy-done.8, bf16[512,512]{1,0:T(8,128)(2,1)S(1)} %copy-done.3, bf16[512,2048]{1,0:T(8,128)(2,1)S(1)} %copy-done, ...), custom_call_target="tpu_custom_call" | custom-call | flops 12000000000 | bytes 12000000 | tf_op jit(solution)/shard_map/inner/pallas_call | solution.py:414
  43.8 0.0 collective-permute-done.2.west_hbm
  43.9 3.2 %collective-permute-done.3.east_hbm = bf16[42,6,4,512]{3,2,1,0:T(4,128)(2,1)S(1)} collective-permute-done((bf16[42,6,4,512]{3,2,1,0:T(4,128)(2,1)S(1)}, bf16[42,6,4,512]{3,2,1,0:T(4,128)(2,1)S(1)}, u32[]{:S(2)}, u32[]{:S(2)}) %collective-permute-start.3) | collective-permute-done | bytes 1032224 | tf_op jit(solution)/shard_map/ppermute | solution.py:378
  47.1 0.0 copy-done.9
  47.1 33.0 %edge.1 = bf16[36,24,4,512]{3,2,1,0:T(4,128)(2,1)} custom-call(bf16[36,24,4,512]{3,2,1,0:T(4,128)(2,1)} %inner.1.part_hbm, bf16[36,24,4,512]{3,2,1,0:T(4,128)(2,1)} %tok_hbm.3, bf16[42,6,4,512]{3,2,1,0:T(4,128)(2,1)S(1)} %collective-permute-done.2.west_hbm, ...), custom_call_target="tpu_custom_call", output_to_operand_aliasing={{}: (0, {})} | custom-call | flops 16000000000 | bytes 16000000 | tf_op jit(solution)/shard_map/edge/pallas_call | solution.py:431
Async XLA Ops:
  2.0 11.1 %collective-permute-start = (bf16[3,24,4,512]{3,2,1,0:T(4,128)(2,1)}, bf16[3,24,4,512]{3,2,1,0:T(4,128)(2,1)S(1)}, u32[]{:S(2)}, u32[]{:S(2)}) collective-permute-start(bf16[3,24,4,512]{3,2,1,0:T(4,128)(2,1)} %get-tuple-element.13), channel_id=1, source_target_pairs={{7,0},{0,1},{1,2},{2,3},{3,4},{4,5},{5,6},{6,7},{15,8},{8,9},{9,10... | collective-permute-start | bytes 884744 | tf_op jit(solution)/shard_map/ppermute | solution.py:378
  5.5 11.2 %collective-permute-start.1 = (bf16[3,24,4,512]{3,2,1,0:T(4,128)(2,1)S(1)}, bf16[3,24,4,512]{3,2,1,0:T(4,128)(2,1)S(1)}, u32[]{:S(2)}, u32[]{:S(2)}) collective-permute-start(bf16[3,24,4,512]{3,2,1,0:T(4,128)(2,1)S(1)} %get-tuple-element.14), channel_id=1, source_target_pairs={{1,0},{2,1},{3,2},{4,3},{5,4},{6,5},{7,6},{0,7},{9,8},{10,9},{11,1... | collective-permute-start | bytes 884744 | tf_op jit(solution)/shard_map/ppermute | solution.py:378
  8.5 13.7 %copy-start = (bf16[512,2048]{1,0:T(8,128)(2,1)S(1)}, bf16[512,2048]{1,0:T(8,128)(2,1)}, u32[]{:S(2)}) copy-start(bf16[512,2048]{1,0:T(8,128)(2,1)} %fc1_hbm.3) | copy-start | bytes 6291460
  8.5 13.7 %copy-start.1 = (bf16[2048,512]{1,0:T(8,128)(2,1)S(1)}, bf16[2048,512]{1,0:T(8,128)(2,1)}, u32[]{:S(2)}) copy-start(bf16[2048,512]{1,0:T(8,128)(2,1)} %fc2_hbm.3) | copy-start | bytes 6291460
  8.5 13.7 %copy-start.2 = (bf16[512,1536]{1,0:T(8,128)(2,1)S(1)}, bf16[512,1536]{1,0:T(8,128)(2,1)}, u32[]{:S(2)}) copy-start(bf16[512,1536]{1,0:T(8,128)(2,1)} %qkv_hbm.3) | copy-start | bytes 4718596
  8.5 13.7 %copy-start.3 = (bf16[512,512]{1,0:T(8,128)(2,1)S(1)}, bf16[512,512]{1,0:T(8,128)(2,1)}, u32[]{:S(2)}) copy-start(bf16[512,512]{1,0:T(8,128)(2,1)} %proj_hbm.3) | copy-start | bytes 1572868
  8.5 13.7 %copy-start.4 = (f32[512]{0:T(512)S(1)}, f32[512]{0:T(512)}, u32[]{:S(2)}) copy-start(f32[512]{0:T(512)} %param.12) | copy-start | bytes 6148
  8.5 13.7 %copy-start.5 = (f32[512]{0:T(512)S(1)}, f32[512]{0:T(512)}, u32[]{:S(2)}) copy-start(f32[512]{0:T(512)} %param.13) | copy-start | bytes 6148
  8.5 13.7 %copy-start.6 = (f32[512]{0:T(512)S(1)}, f32[512]{0:T(512)}, u32[]{:S(2)}) copy-start(f32[512]{0:T(512)} %param.18) | copy-start | bytes 6148
  8.5 13.7 %copy-start.7 = (f32[512]{0:T(512)S(1)}, f32[512]{0:T(512)}, u32[]{:S(2)}) copy-start(f32[512]{0:T(512)} %param.19) | copy-start | bytes 6148
  13.1 9.2 %copy-start.8 = (f32[8,144,144]{2,1,0:T(8,128)S(1)}, f32[8,144,144]{2,1,0:T(8,128)}, u32[]{:S(2)}) copy-start(f32[8,144,144]{2,1,0:T(8,128)} %get-tuple-element.8.bias_hbm.bias1_hbm) | copy-start | bytes 1990660
  13.1 9.2 %copy-start.10 = (f32[21,1,144]{2,1,0:T(1,128)S(1)}, f32[21,1,144]{2,1,0:T(1,128)}, u32[]{:S(2)}) copy-start(f32[21,1,144]{2,1,0:T(1,128)} %get-tuple-element.9.valid_ref) | copy-start | bytes 36292
  18.6 25.2 %collective-permute-start.2 = (bf16[42,6,4,512]{3,2,1,0:T(4,128)(2,1)S(1)}, bf16[42,6,4,512]{3,2,1,0:T(4,128)(2,1)S(1)}, u32[]{:S(2)}, u32[]{:S(2)}) collective-permute-start(bf16[42,6,4,512]{3,2,1,0:T(4,128)(2,1)S(1)} %pad_maximum_fusion), channel_id=1, source_target_pairs={{120,0},{0,8},{8,16},{16,24},{24,32},{32,40},{40,48},{48,56},{56,6... | collective-permute-start | bytes 3096584 | tf_op jit(solution)/shard_map/ppermute | solution.py:378
  21.9 25.2 %collective-permute-start.3 = (bf16[42,6,4,512]{3,2,1,0:T(4,128)(2,1)S(1)}, bf16[42,6,4,512]{3,2,1,0:T(4,128)(2,1)S(1)}, u32[]{:S(2)}, u32[]{:S(2)}) collective-permute-start(bf16[42,6,4,512]{3,2,1,0:T(4,128)(2,1)S(1)} %pad_maximum_fusion.1), channel_id=1, source_target_pairs={{8,0},{16,8},{24,16},{32,24},{40,32},{48,40},{56,48},{64,56},{72,6... | collective-permute-start | bytes 3096584 | tf_op jit(solution)/shard_map/ppermute | solution.py:378
  22.3 24.8 %copy-start.9 = (f32[8,144,144]{2,1,0:T(8,128)S(1)}, f32[8,144,144]{2,1,0:T(8,128)}, u32[]{:S(2)}) copy-start(f32[8,144,144]{2,1,0:T(8,128)} %get-tuple-element.10.bias2_hbm) | copy-start | bytes 1990660

commit v4 on v3

--- a/solution.py
+++ b/solution.py
@@ -195,15 +195,15 @@
 
     copies[0].wait()
 
-    def load(i, carry):
+    def load(i):
         at = pl.multiple_of(big * i, big)
         x = tok_ref[pl.ds(WLAT * i, WLAT)]
         for h in range(2):
             put_block(x[:, 6 * h : 6 * h + 6], g1_ref[...], b1_ref[...], [(q_ref, at + HALF * h, WIN)],
                       [(xs_ref, at + HALF * h, WIN)])
-        return carry
-
-    lax.fori_loop(0, steps, load, 0)
+
+    for i in range(steps):
+        load(i)
     copies[1].wait()
 
     def project(i, carry):
@@ -216,15 +216,15 @@
     lax.fori_loop(0, 2, project, 0)
     copies[2].wait()
 
-    def attention(i, carry):
+    def attention(i):
         masks = block_masks(valid_ref[3 * (i + 1) + 1], 0, WIN)
         for pair in range(2):
             rows = pl.ds(pl.multiple_of(big * i + WIN * pair, WIN), WIN)
             ctx_ref[rows, :] = attend(q_ref[rows, :], kv_ref[rows, :C], kv_ref[rows, C:],
                                       lambda h: bias_ref[h], masks[pair]).astype(BF)
-        return carry
-
-    lax.fori_loop(0, steps, attention, 0)
+
+    for i in range(steps):
+        attention(i)
     for copy in copies[3:]:
         copy.wait()
 
@@ -272,31 +272,35 @@
     for copy in copies[:6]:
         copy.wait()
 
-    def sides(i, carry):
-        at = pl.multiple_of(big * i, big)
+    def sides(i):
+        at = big * i
+        base, mine_base = 2 * big * (i % 2), big * (i % 2)
         own_rows, halo_rows = pl.ds(WLAT * i, WLAT), pl.ds(2 * SLAT + WLAT * i, WLAT)
         for side, halo_ref in ((0, west_ref), (1, east_ref)):
+            here, there = (HALF, 0) if side == 0 else (0, HALF)
             put_block(own_ref[side, own_rows], g1_ref[...], b1_ref[...],
-                      [(xs_ref, big * side + (HALF if side == 0 else 0), WIN)], [(mid_ref, at + WIN * side, HALF)])
-            put_block(halo_ref[halo_rows], g1_ref[...], b1_ref[...],
-                      [(xs_ref, big * side + (0 if side == 0 else HALF), WIN)])
-        kv_ref[: 2 * big, :] = jnp.dot(xs_ref[: 2 * big, :].astype(BF), qkv_ref[:, C:],
-                                       preferred_element_type=F32).astype(BF)
-        own = jnp.concatenate([xs_ref[at : at + HALF, :] for at in (HALF, WIN + HALF, big, big + WIN)], axis=0)
-        q_ref[...] = jnp.dot(own.astype(BF), qkv_ref[:, :C], preferred_element_type=F32) * Q_SCALE
+                      [(xs_ref, base + big * side + here, WIN)], [(mid_ref, at + WIN * side, HALF)])
+            put_block(halo_ref[halo_rows], g1_ref[...], b1_ref[...], [(xs_ref, base + big * side + there, WIN)])
+        keys_all = slice(base, base + 2 * big)
+        kv_ref[keys_all, :] = jnp.dot(xs_ref[keys_all, :].astype(BF), qkv_ref[:, C:],
+                                      preferred_element_type=F32).astype(BF)
+        own = jnp.concatenate([xs_ref[base + row : base + row + HALF, :]
+                               for row in (HALF, WIN + HALF, big, big + WIN)], axis=0)
+        q_ref[mine_base : mine_base + big, :] = jnp.dot(own.astype(BF), qkv_ref[:, :C],
+                                                        preferred_element_type=F32) * Q_SCALE
         contexts = []
         for side in range(2):
             first = HALF if side == 0 else 0
             masks = block_masks(valid_ref[3 * (i + 1) + 2 * side], first, HALF)
             for pair in range(2):
-                mine, keys = WIN * side + HALF * pair, big * side + WIN * pair
+                mine, keys = mine_base + WIN * side + HALF * pair, base + big * side + WIN * pair
                 contexts.append(attend(q_ref[mine : mine + HALF, :], kv_ref[keys : keys + WIN, :C],
                                        kv_ref[keys : keys + WIN, C:],
                                        lambda h: bias1_ref[h, first : first + HALF, :], masks[pair]))
-        ctx_ref[pl.ds(at, big), :] = jnp.concatenate(contexts, axis=0).astype(BF)
-        return carry
-
-    lax.fori_loop(0, steps, sides, 0)
+        ctx_ref[at : at + big, :] = jnp.concatenate(contexts, axis=0).astype(BF)
+
+    for i in range(steps):
+        sides(i)
     for copy in copies[6:11]:
         copy.wait()
 
@@ -317,8 +321,9 @@
             put_block(halo[:, window], g1_ref[...], b1_ref[...], [(xs_ref, big * k + HALF - first, WIN)])
         corner = jnp.concatenate([strip_ref[which, :, cols - SLON :], strip_ref[which, :, :SLON]], axis=1)
         put_block(corner, g1_ref[...], b1_ref[...], [(q_ref, WIN, HALF)], [(mid_ref, at + WIN, HALF)])
-        kv_ref[...] = jnp.dot(xs_ref[...].astype(BF), qkv_ref[:, C:], preferred_element_type=F32).astype(BF)
-        q_ref[...] = jnp.dot(q_ref[...].astype(BF), qkv_ref[:, :C], preferred_element_type=F32) * Q_SCALE
+        kv_ref[: 3 * big, :] = jnp.dot(xs_ref[: 3 * big, :].astype(BF), qkv_ref[:, C:],
+                                       preferred_element_type=F32).astype(BF)
+        q_ref[:big, :] = jnp.dot(q_ref[:big, :].astype(BF), qkv_ref[:, :C], preferred_element_type=F32) * Q_SCALE
         contexts = {}
         for k in range(3):
             masks = block_masks(valid_ref[18 * which + k], first, HALF)
@@ -394,7 +399,7 @@
         in_specs=[vmem, vmem],
         out_specs=[vmem] * 3,
         scratch_shapes=[pltpu.VMEM((HEADS, 768), F32), pltpu.VMEM((8 * WIN, 384), F32)],
-        compiler_params=pltpu.CompilerParams(vmem_limit_bytes=56 * 1024 * 1024),
+        compiler_params=pltpu.CompilerParams(vmem_limit_bytes=40 * 1024 * 1024),
         cost_estimate=pl.CostEstimate(flops=10**9, bytes_accessed=5 * 10**6, transcendentals=0),
         name="prep",
     )(rel_bias, key_mask)
@@ -436,7 +441,7 @@
         scratch_shapes=[pltpu.VMEM((2, rows - 2 * SLAT, SLON, LEV, C), BF), pltpu.VMEM((2, *strip), BF),
                         pltpu.VMEM(halo, BF), pltpu.VMEM(halo, BF), pltpu.VMEM(strip, BF), pltpu.VMEM(strip, BF),
                         pltpu.VMEM((C, 3 * C), BF), table_shape, table_shape, *weights,
-                        pltpu.VMEM((6 * WIN, C), F32), pltpu.VMEM((2 * WIN, C), F32), pltpu.VMEM((6 * WIN, 2 * C), BF),
+                        pltpu.VMEM((8 * WIN, C), F32), pltpu.VMEM((4 * WIN, C), F32), pltpu.VMEM((8 * WIN, 2 * C), BF),
                         pltpu.VMEM((own, C), BF), pltpu.VMEM((own, C), F32),
                         pltpu.SemaphoreType.DMA((14,)), pltpu.SemaphoreType.DMA((own // WIN,))],
         input_output_aliases={0: 0},

time: 80.5 us -> 78.1 us (0.970)
  waiting for transfers between devices: 6.73 us -> 12.4 us
  Pallas kernels: 59.1 us -> 53.7 us
  local copies, waits for them, and re-layouts: 5.1 us -> 3.52 us
  other arithmetic: 2.63 us -> 1.46 us
    ppermute x4, waiting for transfers between devices: 6.73 us -> 12.4 us  [passed_along(): lax.ppermute(block, axis, [((i - distance) % size, i) for i in range(size)])]
    pallas_call x1, Pallas kernels: 21.6 us -> 19 us  [per_device(): pl.pallas_call(inner_kernel, out_shape=jax.ShapeDtypeStruct(tokens.shape,...]
    pallas_call x1, Pallas kernels: 4.54 us -> 2.3 us  [per_device(): pl.pallas_call(functools.partial(prep_kernel, shape=shape), out_shape=[ja...]
    concatenate x2, other arithmetic: 2.63 us -> 1.46 us  [column(): return jnp.concatenate([north[:, at], tokens[:, at], south[:, at]], axis=0)]
    slice x3, local copies, waits for them, and re-layouts: 3.08 us -> 2.16 us  [column(): return jnp.concatenate([north[:, at], tokens[:, at], south[:, at]], axis=0)]
  transfers between devices with their start and end apart: 4 -> 4, of which waited for: 2 -> 4; matrix products, arithmetic and copies ran while one was open for 5% -> 4% of each run, Pallas kernels for 33% -> 27%
where the time goes in v4:
time: 78.1 us; the launch traced here: 77.9 us
  Pallas kernels  53.7 us (69%)
  waiting for transfers between devices  12.4 us (16%)
  starting transfers between devices  6.39 us (8%)
  local copies, waits for them, and re-layouts  3.52 us (5%)
  other arithmetic  1.46 us (2%)
    pallas_call x1, Pallas kernels, per_device(): pl.pallas_call(edge_kernel, out_shape=jax.ShapeDtypeStruct(tokens.shape,...  32.4 us
    pallas_call x1, Pallas kernels, per_device(): pl.pallas_call(inner_kernel, out_shape=jax.ShapeDtypeStruct(tokens.shape,...  19 us
    ppermute x4, waiting for transfers between devices, passed_along(): lax.ppermute(block, axis, [((i - distance) % size, i) for i in range(size)])  12.4 us
    ppermute x4, starting transfers between devices, passed_along(): lax.ppermute(block, axis, [((i - distance) % size, i) for i in range(size)])  6.39 us
    pallas_call x1, Pallas kernels, per_device(): pl.pallas_call(functools.partial(prep_kernel, shape=shape), out_shape=[ja...  2.3 us
    slice x3, local copies, waits for them, and re-layouts, column(): return jnp.concatenate([north[:, at], tokens[:, at], south[:, at]], axis=0)  2.16 us
  transfers between devices with their start and end apart: 4, of which 4 were waited for; matrix products, arithmetic and copies ran while one was open for 4% of the time, Pallas kernels for 27%

profile of v4, /device:TPU:7, one launch (start us, length us, event | category | flops | bytes accessed | tf_op | source)
XLA Modules:
  0.0 77.9 jit_solution(3033721436182947993)
XLA Ops:
  0.0 0.0 copy-start.4
  0.0 0.0 copy-start.5
  0.0 1.3 %fusion.1 = (bf16[3,24,4,512]{3,2,1,0:T(4,128)(2,1)S(1)}, bf16[3,24,4,512]{3,2,1,0:T(4,128)(2,1)S(1)}) fusion(bf16[36,24,4,512]{3,2,1,0:T(4,128)(2,1)} %tok_hbm.3), kind=kLoop, calls=%fused_computation.3 | loop fusion | bytes 1179648 | tf_op jit(solution)/shard_map/slice | solution.py:389
  1.3 3.6 %collective-permute-start = (bf16[3,24,4,512]{3,2,1,0:T(4,128)(2,1)S(1)}, bf16[3,24,4,512]{3,2,1,0:T(4,128)(2,1)S(1)}, u32[]{:S(2)}, u32[]{:S(2)}) collective-permute-start(bf16[3,24,4,512]{3,2,1,0:T(4,128)(2,1)S(1)} %get-tuple-element.13), channel_id=1, source_target_pairs={{7,0},{0,1},{1,2},{2,3},{3,4},{4,5},{5,6},{6,7},{15,8},{8,9},{9,10... | collective-permute-start | bytes 884744 | tf_op jit(solution)/shard_map/ppermute | solution.py:383
  4.9 0.0 collective-permute-start.1
  4.9 2.0 %fusion = (bf16[36,6,4,512]{3,2,1,0:T(4,128)(2,1)S(1)}, bf16[36,6,4,512]{3,2,1,0:T(4,128)(2,1)S(1)}) fusion(bf16[36,24,4,512]{3,2,1,0:T(4,128)(2,1)} %tok_hbm.3), kind=kLoop, calls=%fused_computation.2 | loop fusion | bytes 3538944 | tf_op jit(solution)/shard_map/slice | solution.py:408
  7.0 0.0 copy-done.4
  7.0 0.0 copy-done.5
  7.0 0.0 copy-start
  7.0 0.0 copy-start.1
  7.0 0.0 copy-start.2
  7.0 0.0 copy-start.3
  7.0 0.0 copy-start.6
  7.0 0.0 copy-start.7
  7.0 0.0 copy-start.8
  7.1 0.0 copy-start.9
  7.1 2.3 %prep.1 = (f32[8,144,144]{2,1,0:T(8,128)S(1)}, f32[8,144,144]{2,1,0:T(8,128)S(1)}, f32[21,1,144]{2,1,0:T(1,128)S(1)}) custom-call(f32[8,759]{1,0:T(8,128)S(1)} %copy-done.5, s32[288,384]{1,0:T(8,128)S(1)} %copy-done.4), custom_call_target="tpu_custom_call" | custom-call | flops 1000000000 | bytes 5000000 | tf_op jit(solution)/shard_map/prep/pallas_call | solution.py:396
  9.4 1.2 %collective-permute-done.north_hbm = bf16[3,24,4,512]{3,2,1,0:T(4,128)(2,1)S(1)} collective-permute-done((bf16[3,24,4,512]{3,2,1,0:T(4,128)(2,1)S(1)}, bf16[3,24,4,512]{3,2,1,0:T(4,128)(2,1)S(1)}, u32[]{:S(2)}, u32[]{:S(2)}) %collective-permute-start) | collective-permute-done | bytes 294944 | tf_op jit(solution)/shard_map/ppermute | solution.py:383
  10.6 0.1 fusion.2
  10.6 5.4 %collective-permute-done.1.south_hbm = bf16[3,24,4,512]{3,2,1,0:T(4,128)(2,1)S(1)} collective-permute-done((bf16[3,24,4,512]{3,2,1,0:T(4,128)(2,1)S(1)}, bf16[3,24,4,512]{3,2,1,0:T(4,128)(2,1)S(1)}, u32[]{:S(2)}, u32[]{:S(2)}) %collective-permute-start.1) | collective-permute-done | bytes 294944 | tf_op jit(solution)/shard_map/ppermute | solution.py:383
  16.1 0.1 fusion.3
  16.1 0.7 pad_maximum_fusion
  16.9 2.6 %collective-permute-start.2 = (bf16[42,6,4,512]{3,2,1,0:T(4,128)(2,1)S(1)}, bf16[42,6,4,512]{3,2,1,0:T(4,128)(2,1)S(1)}, u32[]{:S(2)}, u32[]{:S(2)}) collective-permute-start(bf16[42,6,4,512]{3,2,1,0:T(4,128)(2,1)S(1)} %pad_maximum_fusion), channel_id=1, source_target_pairs={{120,0},{0,8},{8,16},{16,24},{24,32},{32,40},{40,48},{48,56},{56,6... | collective-permute-start | bytes 3096584 | tf_op jit(solution)/shard_map/ppermute | solution.py:383
  19.4 0.7 pad_maximum_fusion.1
  20.2 0.3 collective-permute-start.3
  20.4 0.0 copy-done
  20.4 0.0 copy-done.1
  20.4 0.0 copy-done.2
  20.4 0.0 copy-done.3
  20.5 0.0 copy-done.6
  20.5 0.0 copy-done.7
  20.5 0.0 copy-done.8
  20.5 0.0 copy-done.9
  20.5 19.0 %inner.1.part_hbm = bf16[36,24,4,512]{3,2,1,0:T(4,128)(2,1)} custom-call(bf16[36,24,4,512]{3,2,1,0:T(4,128)(2,1)} %tok_hbm.3, bf16[512,1536]{1,0:T(8,128)(2,1)S(1)} %copy-done.2, f32[8,144,144]{2,1,0:T(8,128)S(1)} %get-tuple-element.8.bias_hbm.bias1_hbm, bf16[512,512]{1,0:T(8,128)(2,1)S(1)} %copy-done.3, bf16[512,2048]{1,0:T(8,128)(2,1)S(1)} %copy-done, ...), custom_call_target="tpu_custom_call" | custom-call | flops 12000000000 | bytes 12000000 | tf_op jit(solution)/shard_map/inner/pallas_call | solution.py:419
  39.5 2.5 %collective-permute-done.2.west_hbm = bf16[42,6,4,512]{3,2,1,0:T(4,128)(2,1)S(1)} collective-permute-done((bf16[42,6,4,512]{3,2,1,0:T(4,128)(2,1)S(1)}, bf16[42,6,4,512]{3,2,1,0:T(4,128)(2,1)S(1)}, u32[]{:S(2)}, u32[]{:S(2)}) %collective-permute-start.2) | collective-permute-done | bytes 1032224 | tf_op jit(solution)/shard_map/ppermute | solution.py:383
  42.0 3.3 %collective-permute-done.3.east_hbm = bf16[42,6,4,512]{3,2,1,0:T(4,128)(2,1)S(1)} collective-permute-done((bf16[42,6,4,512]{3,2,1,0:T(4,128)(2,1)S(1)}, bf16[42,6,4,512]{3,2,1,0:T(4,128)(2,1)S(1)}, u32[]{:S(2)}, u32[]{:S(2)}) %collective-permute-start.3) | collective-permute-done | bytes 1032224 | tf_op jit(solution)/shard_map/ppermute | solution.py:383
  45.3 32.4 %edge.1 = bf16[36,24,4,512]{3,2,1,0:T(4,128)(2,1)} custom-call(bf16[36,24,4,512]{3,2,1,0:T(4,128)(2,1)} %inner.1.part_hbm, bf16[36,24,4,512]{3,2,1,0:T(4,128)(2,1)} %tok_hbm.3, bf16[42,6,4,512]{3,2,1,0:T(4,128)(2,1)S(1)} %collective-permute-done.2.west_hbm, ...), custom_call_target="tpu_custom_call", output_to_operand_aliasing={{}: (0, {})} | custom-call | flops 16000000000 | bytes 16000000 | tf_op jit(solution)/shard_map/edge/pallas_call | solution.py:436
Async XLA Ops:
  0.0 7.0 %copy-start.4 = (s32[288,384]{1,0:T(8,128)S(1)}, s32[288,384]{1,0:T(8,128)}, u32[]{:S(2)}) copy-start(s32[288,384]{1,0:T(8,128)} %mask_ref.1) | copy-start | bytes 1327108
  0.0 7.0 %copy-start.5 = (f32[8,759]{1,0:T(8,128)S(1)}, f32[8,759]{1,0:T(8,128)}, u32[]{:S(2)}) copy-start(f32[8,759]{1,0:T(8,128)} %table_ref.1) | copy-start | bytes 72868
  1.3 9.3 %collective-permute-start = (bf16[3,24,4,512]{3,2,1,0:T(4,128)(2,1)S(1)}, bf16[3,24,4,512]{3,2,1,0:T(4,128)(2,1)S(1)}, u32[]{:S(2)}, u32[]{:S(2)}) collective-permute-start(bf16[3,24,4,512]{3,2,1,0:T(4,128)(2,1)S(1)} %get-tuple-element.13), channel_id=1, source_target_pairs={{7,0},{0,1},{1,2},{2,3},{3,4},{4,5},{5,6},{6,7},{15,8},{8,9},{9,10... | collective-permute-start | bytes 884744 | tf_op jit(solution)/shard_map/ppermute | solution.py:383
  4.9 11.2 %collective-permute-start.1 = (bf16[3,24,4,512]{3,2,1,0:T(4,128)(2,1)S(1)}, bf16[3,24,4,512]{3,2,1,0:T(4,128)(2,1)S(1)}, u32[]{:S(2)}, u32[]{:S(2)}) collective-permute-start(bf16[3,24,4,512]{3,2,1,0:T(4,128)(2,1)S(1)} %get-tuple-element.14), channel_id=1, source_target_pairs={{1,0},{2,1},{3,2},{4,3},{5,4},{6,5},{7,6},{0,7},{9,8},{10,9},{11,1... | collective-permute-start | bytes 884744 | tf_op jit(solution)/shard_map/ppermute | solution.py:383
  7.0 13.4 %copy-start = (bf16[512,2048]{1,0:T(8,128)(2,1)S(1)}, bf16[512,2048]{1,0:T(8,128)(2,1)}, u32[]{:S(2)}) copy-start(bf16[512,2048]{1,0:T(8,128)(2,1)} %fc1_hbm.3) | copy-start | bytes 6291460
  7.0 13.4 %copy-start.1 = (bf16[2048,512]{1,0:T(8,128)(2,1)S(1)}, bf16[2048,512]{1,0:T(8,128)(2,1)}, u32[]{:S(2)}) copy-start(bf16[2048,512]{1,0:T(8,128)(2,1)} %fc2_hbm.3) | copy-start | bytes 6291460
  7.0 13.4 %copy-start.2 = (bf16[512,1536]{1,0:T(8,128)(2,1)S(1)}, bf16[512,1536]{1,0:T(8,128)(2,1)}, u32[]{:S(2)}) copy-start(bf16[512,1536]{1,0:T(8,128)(2,1)} %qkv_hbm.3) | copy-start | bytes 4718596
  7.0 13.4 %copy-start.3 = (bf16[512,512]{1,0:T(8,128)(2,1)S(1)}, bf16[512,512]{1,0:T(8,128)(2,1)}, u32[]{:S(2)}) copy-start(bf16[512,512]{1,0:T(8,128)(2,1)} %proj_hbm.3) | copy-start | bytes 1572868
  7.0 13.4 %copy-start.6 = (f32[512]{0:T(512)S(1)}, f32[512]{0:T(512)}, u32[]{:S(2)}) copy-start(f32[512]{0:T(512)} %param.12) | copy-start | bytes 6148
  7.0 13.4 %copy-start.7 = (f32[512]{0:T(512)S(1)}, f32[512]{0:T(512)}, u32[]{:S(2)}) copy-start(f32[512]{0:T(512)} %param.13) | copy-start | bytes 6148
  7.0 13.4 %copy-start.8 = (f32[512]{0:T(512)S(1)}, f32[512]{0:T(512)}, u32[]{:S(2)}) copy-start(f32[512]{0:T(512)} %param.18) | copy-start | bytes 6148
  7.1 13.4 %copy-start.9 = (f32[512]{0:T(512)S(1)}, f32[512]{0:T(512)}, u32[]{:S(2)}) copy-start(f32[512]{0:T(512)} %param.19) | copy-start | bytes 6148
  16.9 25.2 %collective-permute-start.2 = (bf16[42,6,4,512]{3,2,1,0:T(4,128)(2,1)S(1)}, bf16[42,6,4,512]{3,2,1,0:T(4,128)(2,1)S(1)}, u32[]{:S(2)}, u32[]{:S(2)}) collective-permute-start(bf16[42,6,4,512]{3,2,1,0:T(4,128)(2,1)S(1)} %pad_maximum_fusion), channel_id=1, source_target_pairs={{120,0},{0,8},{8,16},{16,24},{24,32},{32,40},{40,48},{48,56},{56,6... | collective-permute-start | bytes 3096584 | tf_op jit(solution)/shard_map/ppermute | solution.py:383
  20.2 25.2 %collective-permute-start.3 = (bf16[42,6,4,512]{3,2,1,0:T(4,128)(2,1)S(1)}, bf16[42,6,4,512]{3,2,1,0:T(4,128)(2,1)S(1)}, u32[]{:S(2)}, u32[]{:S(2)}) collective-permute-start(bf16[42,6,4,512]{3,2,1,0:T(4,128)(2,1)S(1)} %pad_maximum_fusion.1), channel_id=1, source_target_pairs={{8,0},{16,8},{24,16},{32,24},{40,32},{48,40},{56,48},{64,56},{72,6... | collective-permute-start | bytes 3096584 | tf_op jit(solution)/shard_map/ppermute | solution.py:383

commit v5 on v4

--- a/solution.py
+++ b/solution.py
@@ -251,7 +251,7 @@
         out_copy(i).wait()
 
 
-def edge_kernel(part_hbm, tok_hbm, west_hbm, east_hbm, north_hbm, south_hbm, qkv_hbm, bias1_hbm, bias2_hbm, proj_hbm,
+def edge_kernel(part_hbm, tok_hbm, west_hbm, east_hbm, north_hbm, south_hbm, west_ends_hbm, east_ends_hbm, qkv_hbm, bias1_hbm, bias2_hbm, proj_hbm,
                 fc1_hbm, fc2_hbm, g1_ref, b1_ref, valid_ref, g2_ref, b2_ref, out_hbm,
                 own_ref, strip_ref, west_ref, east_ref, north_ref, south_ref, qkv_ref, bias1_ref, bias2_ref, proj_ref,
                 fc1_ref, fc2_ref, xs_ref, q_ref, kv_ref, ctx_ref, mid_ref, sem, out_sem):
@@ -263,8 +263,10 @@
     places = [(own_ref.at[side], side_at[side]) for side in range(2)]
     places += [(strip_ref.at[which], strip_at[which]) for which in range(2)]
     copies = start_copies([(tok_hbm.at[at], here) for here, at in places[:2]] + [
-        (west_hbm, west_ref), (east_hbm, east_ref), (qkv_hbm, qkv_ref), (bias1_hbm, bias1_ref)] + [
+        (west_hbm, west_ref.at[pl.ds(SLAT, rows)]), (east_hbm, east_ref.at[pl.ds(SLAT, rows)]), (qkv_hbm, qkv_ref), (bias1_hbm, bias1_ref)] + [
         (tok_hbm.at[at], here) for here, at in places[2:]] + [
+        (ends.at[pl.ds(SLAT * n, SLAT)], ref.at[pl.ds(at, SLAT)])
+        for ends, ref in ((west_ends_hbm, west_ref), (east_ends_hbm, east_ref)) for n, at in ((0, 0), (1, rows + SLAT))] + [
         (north_hbm, north_ref), (south_hbm, south_ref), (bias2_hbm, bias2_ref), (proj_hbm, proj_ref),
         (fc1_hbm, fc1_ref), (fc2_hbm, fc2_ref)], sem)
     big = 2 * WIN
@@ -301,7 +303,7 @@
 
     for i in range(steps):
         sides(i)
-    for copy in copies[6:11]:
+    for copy in copies[6:15]:
         copy.wait()
 
     for which in range(2):
@@ -336,7 +338,7 @@
         ctx_ref[at : at + big, :] = jnp.concatenate(
             [contexts[1, 0], contexts[1, 1]] + [jnp.where(east_cell, contexts[2, pair], contexts[0, pair])
                                                 for pair in range(2)], axis=0).astype(BF)
-    for copy in copies[11:]:
+    for copy in copies[15:]:
         copy.wait()
     part = big * (steps + 2) // 3
 
@@ -388,6 +390,8 @@
     rows, cols = tokens.shape[:2]
     north = passed_along(tokens[rows - SLAT :], "lat", 1)
     south = passed_along(tokens[:SLAT], "lat", -1)
+    west = passed_along(tokens[:, cols - SLON :], "lon", 1)
+    east = passed_along(tokens[:, :SLON], "lon", -1)
 
     vmem = pl.BlockSpec(memory_space=pltpu.VMEM)
     any_space = pl.BlockSpec(memory_space=pl.ANY)
@@ -404,11 +408,11 @@
         name="prep",
     )(rel_bias, key_mask)
 
-    def column(at):
-        return jnp.concatenate([north[:, at], tokens[:, at], south[:, at]], axis=0)
-
-    west = passed_along(column(slice(cols - SLON, cols)), "lon", 1)
-    east = passed_along(column(slice(0, SLON)), "lon", -1)
+    def ends(at):
+        return jnp.concatenate([north[:, at], south[:, at]], axis=0)
+
+    west_ends = passed_along(ends(slice(cols - SLON, cols)), "lon", 1)
+    east_ends = passed_along(ends(slice(0, SLON)), "lon", -1)
 
     g1, b1 = norm1_gain.reshape(1, C), norm1_bias.reshape(1, C)
     g2, b2 = norm2_gain.reshape(1, C), norm2_bias.reshape(1, C)
@@ -436,19 +440,19 @@
     return pl.pallas_call(
         edge_kernel,
         out_shape=jax.ShapeDtypeStruct(tokens.shape, BF),
-        in_specs=[any_space] * 12 + [vmem] * 5,
+        in_specs=[any_space] * 14 + [vmem] * 5,
         out_specs=any_space,
         scratch_shapes=[pltpu.VMEM((2, rows - 2 * SLAT, SLON, LEV, C), BF), pltpu.VMEM((2, *strip), BF),
                         pltpu.VMEM(halo, BF), pltpu.VMEM(halo, BF), pltpu.VMEM(strip, BF), pltpu.VMEM(strip, BF),
                         pltpu.VMEM((C, 3 * C), BF), table_shape, table_shape, *weights,
                         pltpu.VMEM((8 * WIN, C), F32), pltpu.VMEM((4 * WIN, C), F32), pltpu.VMEM((8 * WIN, 2 * C), BF),
                         pltpu.VMEM((own, C), BF), pltpu.VMEM((own, C), F32),
-                        pltpu.SemaphoreType.DMA((14,)), pltpu.SemaphoreType.DMA((own // WIN,))],
+                        pltpu.SemaphoreType.DMA((18,)), pltpu.SemaphoreType.DMA((own // WIN,))],
         input_output_aliases={0: 0},
         compiler_params=params,
         cost_estimate=pl.CostEstimate(flops=16 * 10**9, bytes_accessed=16 * 10**6, transcendentals=0),
         name="edge",
-    )(part, tokens, west, east, north, south, qkv_weight, bias1, bias2, proj_weight, fc1_weight, fc2_weight,
+    )(part, tokens, west, east, north, south, west_ends, east_ends, qkv_weight, bias1, bias2, proj_weight, fc1_weight, fc2_weight,
       g1, b1, valid, g2, b2)
 
 

time: 78.1 us -> 80.4 us (1.029)
  the two profiles are of different devices: /device:TPU:7 before, /device:TPU:0 now
where the time goes in v5:
time: 80.4 us; the launch traced here: 80.3 us
  Pallas kernels  53.8 us (67%)
  starting transfers between devices  13.2 us (16%)
  waiting for transfers between devices  9.08 us (11%)
  local copies, waits for them, and re-layouts  3.67 us (5%)
    pallas_call x1, Pallas kernels, per_device(): pl.pallas_call(edge_kernel, out_shape=jax.ShapeDtypeStruct(tokens.shape,...  32.5 us
    pallas_call x1, Pallas kernels, per_device(): pl.pallas_call(inner_kernel, out_shape=jax.ShapeDtypeStruct(tokens.shape,...  19 us
    ppermute x6, starting transfers between devices, passed_along(): lax.ppermute(block, axis, [((i - distance) % size, i) for i in range(size)])  13.2 us
    ppermute x6, waiting for transfers between devices, passed_along(): lax.ppermute(block, axis, [((i - distance) % size, i) for i in range(size)])  9.08 us
    pallas_call x1, Pallas kernels, per_device(): pl.pallas_call(functools.partial(prep_kernel, shape=shape), out_shape=[ja...  2.31 us
    slice x1, local copies, waits for them, and re-layouts, per_device(): east = passed_along(tokens[:, :SLON], 'lon', -1)  2.21 us
  transfers between devices with their start and end apart: 6, of which 1 were waited for; matrix products, arithmetic and copies ran while one was open for 3% of the time, Pallas kernels for 27%

profile of v5, /device:TPU:0, one launch (start us, length us, event | category | flops | bytes accessed | tf_op | source)
XLA Modules:
  0.0 80.3 jit_solution(8698638519548347726)
XLA Ops:
  0.0 0.0 copy-start.4
  0.0 0.0 copy-start.5
  0.0 1.3 %fusion = (bf16[3,24,4,512]{3,2,1,0:T(4,128)(2,1)S(1)}, bf16[3,24,4,512]{3,2,1,0:T(4,128)(2,1)S(1)}) fusion(bf16[36,24,4,512]{3,2,1,0:T(4,128)(2,1)} %tok_hbm.3), kind=kLoop, calls=%fused_computation.2 | loop fusion | bytes 1179648 | tf_op jit(solution)/shard_map/slice | solution.py:392
  1.3 6.2 %collective-permute-start.3 = (bf16[3,24,4,512]{3,2,1,0:T(4,128)(2,1)S(1)}, bf16[3,24,4,512]{3,2,1,0:T(4,128)(2,1)S(1)}, u32[]{:S(2)}, u32[]{:S(2)}) collective-permute-start(bf16[3,24,4,512]{3,2,1,0:T(4,128)(2,1)S(1)} %get-tuple-element.11), channel_id=1, source_target_pairs={{1,0},{2,1},{3,2},{4,3},{5,4},{6,5},{7,6},{0,7},{9,8},{10,9},{11,1... | collective-permute-start | bytes 884744 | tf_op jit(solution)/shard_map/ppermute | solution.py:385
  7.5 0.0 copy-start
  7.5 0.0 copy-start.1
  7.5 0.0 copy-start.2
  7.5 0.0 copy-start.3
  7.5 0.0 copy-start.6
  7.6 0.0 copy-start.7
  7.6 0.0 copy-start.8
  7.6 0.0 copy-start.9
  7.6 0.1 collective-permute-start.2
  7.7 2.2 %fusion.1 = (bf16[36,6,4,512]{3,2,1,0:T(4,128)(2,1)S(1)}, bf16[36,6,4,512]{3,2,1,0:T(4,128)(2,1)S(1)}) fusion(bf16[36,24,4,512]{3,2,1,0:T(4,128)(2,1)} %tok_hbm.3), kind=kLoop, calls=%fused_computation.3 | loop fusion | bytes 3538944 | tf_op jit(solution)/shard_map/slice | solution.py:394
  9.9 2.7 %collective-permute-start.1 = (bf16[36,6,4,512]{3,2,1,0:T(4,128)(2,1)S(1)}, bf16[36,6,4,512]{3,2,1,0:T(4,128)(2,1)S(1)}, u32[]{:S(2)}, u32[]{:S(2)}) collective-permute-start(bf16[36,6,4,512]{3,2,1,0:T(4,128)(2,1)S(1)} %get-tuple-element.13), channel_id=1, source_target_pairs={{8,0},{16,8},{24,16},{32,24},{40,32},{48,40},{56,48},{64,56},{72,6... | collective-permute-start | bytes 2654216 | tf_op jit(solution)/shard_map/ppermute | solution.py:385
  12.6 0.0 collective-permute-start
  12.6 0.0 copy-done.4
  12.6 0.0 copy-done.5
  12.6 2.3 %prep.1 = (f32[8,144,144]{2,1,0:T(8,128)S(1)}, f32[8,144,144]{2,1,0:T(8,128)S(1)}, f32[21,1,144]{2,1,0:T(1,128)S(1)}) custom-call(f32[8,759]{1,0:T(8,128)S(1)} %copy-done.5, s32[288,384]{1,0:T(8,128)S(1)} %copy-done.4), custom_call_target="tpu_custom_call" | custom-call | flops 1000000000 | bytes 5000000 | tf_op jit(solution)/shard_map/prep/pallas_call | solution.py:400
  14.9 0.0 collective-permute-done.3.south_hbm
  14.9 0.1 fusion.3
  15.0 9.1 %collective-permute-done.2.north_hbm = bf16[3,24,4,512]{3,2,1,0:T(4,128)(2,1)S(1)} collective-permute-done((bf16[3,24,4,512]{3,2,1,0:T(4,128)(2,1)S(1)}, bf16[3,24,4,512]{3,2,1,0:T(4,128)(2,1)S(1)}, u32[]{:S(2)}, u32[]{:S(2)}) %collective-permute-start.2) | collective-permute-done | bytes 294944 | tf_op jit(solution)/shard_map/ppermute | solution.py:385
  24.0 0.1 fusion.2
  24.1 0.1 pad_maximum_fusion
  24.2 0.1 collective-permute-start.4
  24.3 0.1 pad_maximum_fusion.1
  24.4 4.1 %collective-permute-start.5 = (bf16[6,6,4,512]{3,2,1,0:T(4,128)(2,1)S(1)}, bf16[6,6,4,512]{3,2,1,0:T(4,128)(2,1)S(1)}, u32[]{:S(2)}, u32[]{:S(2)}) collective-permute-start(bf16[6,6,4,512]{3,2,1,0:T(4,128)(2,1)S(1)} %pad_maximum_fusion.1), channel_id=1, source_target_pairs={{8,0},{16,8},{24,16},{32,24},{40,32},{48,40},{56,48},{64,56},{72,6... | collective-permute-start | bytes 442376 | tf_op jit(solution)/shard_map/ppermute | solution.py:385
  28.5 0.0 copy-done
  28.5 0.0 copy-done.1
  28.5 0.0 copy-done.2
  28.5 0.0 copy-done.3
  28.5 0.0 copy-done.6
  28.5 0.0 copy-done.7
  28.5 0.0 copy-done.8
  28.5 0.0 copy-done.9
  28.5 19.0 %inner.1.part_hbm = bf16[36,24,4,512]{3,2,1,0:T(4,128)(2,1)} custom-call(bf16[36,24,4,512]{3,2,1,0:T(4,128)(2,1)} %tok_hbm.3, bf16[512,1536]{1,0:T(8,128)(2,1)S(1)} %copy-done.2, f32[8,144,144]{2,1,0:T(8,128)S(1)} %get-tuple-element.8.bias_hbm.bias1_hbm, bf16[512,512]{1,0:T(8,128)(2,1)S(1)} %copy-done.3, bf16[512,2048]{1,0:T(8,128)(2,1)S(1)} %copy-done, ...), custom_call_target="tpu_custom_call" | custom-call | flops 12000000000 | bytes 12000000 | tf_op jit(solution)/shard_map/inner/pallas_call | solution.py:423
  47.6 0.0 collective-permute-done.4.west_ends_hbm
  47.6 0.0 collective-permute-done.5.east_ends_hbm
  47.6 0.0 collective-permute-done.1.east_hbm
  47.6 0.0 collective-permute-done.west_hbm
  47.6 32.5 %edge.1 = bf16[36,24,4,512]{3,2,1,0:T(4,128)(2,1)} custom-call(bf16[36,24,4,512]{3,2,1,0:T(4,128)(2,1)} %inner.1.part_hbm, bf16[36,24,4,512]{3,2,1,0:T(4,128)(2,1)} %tok_hbm.3, bf16[36,6,4,512]{3,2,1,0:T(4,128)(2,1)S(1)} %collective-permute-done.west_hbm, ...), custom_call_target="tpu_custom_call", output_to_operand_aliasing={{}: (0, {})} | custom-call | flops 16000000000 | bytes 16000000 | tf_op jit(solution)/shard_map/edge/pallas_call | solution.py:440
Async XLA Ops:
  0.0 12.6 %copy-start.4 = (s32[288,384]{1,0:T(8,128)S(1)}, s32[288,384]{1,0:T(8,128)}, u32[]{:S(2)}) copy-start(s32[288,384]{1,0:T(8,128)} %mask_ref.1) | copy-start | bytes 1327108
  0.0 12.6 %copy-start.5 = (f32[8,759]{1,0:T(8,128)S(1)}, f32[8,759]{1,0:T(8,128)}, u32[]{:S(2)}) copy-start(f32[8,759]{1,0:T(8,128)} %table_ref.1) | copy-start | bytes 72868
  1.3 13.6 %collective-permute-start.3 = (bf16[3,24,4,512]{3,2,1,0:T(4,128)(2,1)S(1)}, bf16[3,24,4,512]{3,2,1,0:T(4,128)(2,1)S(1)}, u32[]{:S(2)}, u32[]{:S(2)}) collective-permute-start(bf16[3,24,4,512]{3,2,1,0:T(4,128)(2,1)S(1)} %get-tuple-element.11), channel_id=1, source_target_pairs={{1,0},{2,1},{3,2},{4,3},{5,4},{6,5},{7,6},{0,7},{9,8},{10,9},{11,1... | collective-permute-start | bytes 884744 | tf_op jit(solution)/shard_map/ppermute | solution.py:385
  7.5 20.9 %copy-start = (bf16[512,2048]{1,0:T(8,128)(2,1)S(1)}, bf16[512,2048]{1,0:T(8,128)(2,1)}, u32[]{:S(2)}) copy-start(bf16[512,2048]{1,0:T(8,128)(2,1)} %fc1_hbm.3) | copy-start | bytes 6291460
  7.5 20.9 %copy-start.1 = (bf16[2048,512]{1,0:T(8,128)(2,1)S(1)}, bf16[2048,512]{1,0:T(8,128)(2,1)}, u32[]{:S(2)}) copy-start(bf16[2048,512]{1,0:T(8,128)(2,1)} %fc2_hbm.3) | copy-start | bytes 6291460
  7.5 20.9 %copy-start.2 = (bf16[512,1536]{1,0:T(8,128)(2,1)S(1)}, bf16[512,1536]{1,0:T(8,128)(2,1)}, u32[]{:S(2)}) copy-start(bf16[512,1536]{1,0:T(8,128)(2,1)} %qkv_hbm.3) | copy-start | bytes 4718596
  7.5 20.9 %copy-start.3 = (bf16[512,512]{1,0:T(8,128)(2,1)S(1)}, bf16[512,512]{1,0:T(8,128)(2,1)}, u32[]{:S(2)}) copy-start(bf16[512,512]{1,0:T(8,128)(2,1)} %proj_hbm.3) | copy-start | bytes 1572868
  7.5 20.9 %copy-start.6 = (f32[512]{0:T(512)S(1)}, f32[512]{0:T(512)}, u32[]{:S(2)}) copy-start(f32[512]{0:T(512)} %param.12) | copy-start | bytes 6148
  7.6 20.9 %copy-start.7 = (f32[512]{0:T(512)S(1)}, f32[512]{0:T(512)}, u32[]{:S(2)}) copy-start(f32[512]{0:T(512)} %param.13) | copy-start | bytes 6148
  7.6 20.9 %copy-start.8 = (f32[512]{0:T(512)S(1)}, f32[512]{0:T(512)}, u32[]{:S(2)}) copy-start(f32[512]{0:T(512)} %param.18) | copy-start | bytes 6148
  7.6 20.9 %copy-start.9 = (f32[512]{0:T(512)S(1)}, f32[512]{0:T(512)}, u32[]{:S(2)}) copy-start(f32[512]{0:T(512)} %param.19) | copy-start | bytes 6148
  7.6 16.4 %collective-permute-start.2 = (bf16[3,24,4,512]{3,2,1,0:T(4,128)(2,1)S(1)}, bf16[3,24,4,512]{3,2,1,0:T(4,128)(2,1)S(1)}, u32[]{:S(2)}, u32[]{:S(2)}) collective-permute-start(bf16[3,24,4,512]{3,2,1,0:T(4,128)(2,1)S(1)} %get-tuple-element.12), channel_id=1, source_target_pairs={{7,0},{0,1},{1,2},{2,3},{3,4},{4,5},{5,6},{6,7},{15,8},{8,9},{9,10... | collective-permute-start | bytes 884744 | tf_op jit(solution)/shard_map/ppermute | solution.py:385
  9.9 37.7 %collective-permute-start.1 = (bf16[36,6,4,512]{3,2,1,0:T(4,128)(2,1)S(1)}, bf16[36,6,4,512]{3,2,1,0:T(4,128)(2,1)S(1)}, u32[]{:S(2)}, u32[]{:S(2)}) collective-permute-start(bf16[36,6,4,512]{3,2,1,0:T(4,128)(2,1)S(1)} %get-tuple-element.13), channel_id=1, source_target_pairs={{8,0},{16,8},{24,16},{32,24},{40,32},{48,40},{56,48},{64,56},{72,6... | collective-permute-start | bytes 2654216 | tf_op jit(solution)/shard_map/ppermute | solution.py:385
  12.6 35.0 %collective-permute-start = (bf16[36,6,4,512]{3,2,1,0:T(4,128)(2,1)S(1)}, bf16[36,6,4,512]{3,2,1,0:T(4,128)(2,1)S(1)}, u32[]{:S(2)}, u32[]{:S(2)}) collective-permute-start(bf16[36,6,4,512]{3,2,1,0:T(4,128)(2,1)S(1)} %get-tuple-element.14), channel_id=1, source_target_pairs={{120,0},{0,8},{8,16},{16,24},{24,32},{32,40},{40,48},{48,56},{56,6... | collective-permute-start | bytes 2654216 | tf_op jit(solution)/shard_map/ppermute | solution.py:385
  24.2 23.4 %collective-permute-start.4 = (bf16[6,6,4,512]{3,2,1,0:T(4,128)(2,1)S(1)}, bf16[6,6,4,512]{3,2,1,0:T(4,128)(2,1)S(1)}, u32[]{:S(2)}, u32[]{:S(2)}) collective-permute-start(bf16[6,6,4,512]{3,2,1,0:T(4,128)(2,1)S(1)} %pad_maximum_fusion), channel_id=1, source_target_pairs={{120,0},{0,8},{8,16},{16,24},{24,32},{32,40},{40,48},{48,56},{56,6... | collective-permute-start | bytes 442376 | tf_op jit(solution)/shard_map/ppermute | solution.py:385
  24.4 23.2 %collective-permute-start.5 = (bf16[6,6,4,512]{3,2,1,0:T(4,128)(2,1)S(1)}, bf16[6,6,4,512]{3,2,1,0:T(4,128)(2,1)S(1)}, u32[]{:S(2)}, u32[]{:S(2)}) collective-permute-start(bf16[6,6,4,512]{3,2,1,0:T(4,128)(2,1)S(1)} %pad_maximum_fusion.1), channel_id=1, source_target_pairs={{8,0},{16,8},{24,16},{32,24},{40,32},{48,40},{56,48},{64,56},{72,6... | collective-permute-start | bytes 442376 | tf_op jit(solution)/shard_map/ppermute | solution.py:385

commit v6 on v5

--- a/solution.py
+++ b/solution.py
@@ -251,7 +251,7 @@
         out_copy(i).wait()
 
 
-def edge_kernel(part_hbm, tok_hbm, west_hbm, east_hbm, north_hbm, south_hbm, west_ends_hbm, east_ends_hbm, qkv_hbm, bias1_hbm, bias2_hbm, proj_hbm,
+def edge_kernel(part_hbm, tok_hbm, west_hbm, east_hbm, north_hbm, south_hbm, nw_hbm, sw_hbm, ne_hbm, se_hbm, qkv_hbm, bias1_hbm, bias2_hbm, proj_hbm,
                 fc1_hbm, fc2_hbm, g1_ref, b1_ref, valid_ref, g2_ref, b2_ref, out_hbm,
                 own_ref, strip_ref, west_ref, east_ref, north_ref, south_ref, qkv_ref, bias1_ref, bias2_ref, proj_ref,
                 fc1_ref, fc2_ref, xs_ref, q_ref, kv_ref, ctx_ref, mid_ref, sem, out_sem):
@@ -265,8 +265,8 @@
     copies = start_copies([(tok_hbm.at[at], here) for here, at in places[:2]] + [
         (west_hbm, west_ref.at[pl.ds(SLAT, rows)]), (east_hbm, east_ref.at[pl.ds(SLAT, rows)]), (qkv_hbm, qkv_ref), (bias1_hbm, bias1_ref)] + [
         (tok_hbm.at[at], here) for here, at in places[2:]] + [
-        (ends.at[pl.ds(SLAT * n, SLAT)], ref.at[pl.ds(at, SLAT)])
-        for ends, ref in ((west_ends_hbm, west_ref), (east_ends_hbm, east_ref)) for n, at in ((0, 0), (1, rows + SLAT))] + [
+        (nw_hbm, west_ref.at[pl.ds(0, SLAT)]), (sw_hbm, west_ref.at[pl.ds(rows + SLAT, SLAT)]),
+        (ne_hbm, east_ref.at[pl.ds(0, SLAT)]), (se_hbm, east_ref.at[pl.ds(rows + SLAT, SLAT)]),
         (north_hbm, north_ref), (south_hbm, south_ref), (bias2_hbm, bias2_ref), (proj_hbm, proj_ref),
         (fc1_hbm, fc1_ref), (fc2_hbm, fc2_ref)], sem)
     big = 2 * WIN
@@ -380,18 +380,29 @@
         copy.wait()
 
 
-def passed_along(block, axis, distance):
-    size = lax.axis_size(axis)
-    return lax.ppermute(block, axis, [((i - distance) % size, i) for i in range(size)])
+def passed_along(block, axes, distance):
+    sizes = [lax.axis_size(a) for a in axes]
+    route = []
+    for i in np.ndindex(*sizes):
+        j = tuple((a - d) % n for a, d, n in zip(i, distance, sizes))
+        route.append((int(np.ravel_multi_index(j, sizes)), int(np.ravel_multi_index(i, sizes))))
+    return lax.ppermute(block, axes if len(axes) > 1 else axes[0], route)
 
 
 def per_device(tokens, norm1_gain, norm1_bias, qkv_weight, rel_bias, key_mask, proj_weight,
                norm2_gain, norm2_bias, fc1_weight, fc2_weight):
     rows, cols = tokens.shape[:2]
-    north = passed_along(tokens[rows - SLAT :], "lat", 1)
-    south = passed_along(tokens[:SLAT], "lat", -1)
-    west = passed_along(tokens[:, cols - SLON :], "lon", 1)
-    east = passed_along(tokens[:, :SLON], "lon", -1)
+    first, last = slice(0, SLAT), slice(rows - SLAT, rows)
+    left, right = slice(0, SLON), slice(cols - SLON, cols)
+    north = passed_along(tokens[last], ("lat",), (1,))
+    south = passed_along(tokens[first], ("lat",), (-1,))
+    west = passed_along(tokens[:, right], ("lon",), (1,))
+    east = passed_along(tokens[:, left], ("lon",), (-1,))
+    both = ("lon", "lat")
+    nw = passed_along(tokens[last, right], both, (1, 1))
+    sw = passed_along(tokens[first, right], both, (1, -1))
+    ne = passed_along(tokens[last, left], both, (-1, 1))
+    se = passed_along(tokens[first, left], both, (-1, -1))
 
     vmem = pl.BlockSpec(memory_space=pltpu.VMEM)
     any_space = pl.BlockSpec(memory_space=pl.ANY)
@@ -407,12 +418,6 @@
         cost_estimate=pl.CostEstimate(flops=10**9, bytes_accessed=5 * 10**6, transcendentals=0),
         name="prep",
     )(rel_bias, key_mask)
-
-    def ends(at):
-        return jnp.concatenate([north[:, at], south[:, at]], axis=0)
-
-    west_ends = passed_along(ends(slice(cols - SLON, cols)), "lon", 1)
-    east_ends = passed_along(ends(slice(0, SLON)), "lon", -1)
 
     g1, b1 = norm1_gain.reshape(1, C), norm1_bias.reshape(1, C)
     g2, b2 = norm2_gain.reshape(1, C), norm2_bias.reshape(1, C)
@@ -440,7 +445,7 @@
     return pl.pallas_call(
         edge_kernel,
         out_shape=jax.ShapeDtypeStruct(tokens.shape, BF),
-        in_specs=[any_space] * 14 + [vmem] * 5,
+        in_specs=[any_space] * 16 + [vmem] * 5,
         out_specs=any_space,
         scratch_shapes=[pltpu.VMEM((2, rows - 2 * SLAT, SLON, LEV, C), BF), pltpu.VMEM((2, *strip), BF),
                         pltpu.VMEM(halo, BF), pltpu.VMEM(halo, BF), pltpu.VMEM(strip, BF), pltpu.VMEM(strip, BF),
@@ -452,7 +457,7 @@
         compiler_params=params,
         cost_estimate=pl.CostEstimate(flops=16 * 10**9, bytes_accessed=16 * 10**6, transcendentals=0),
         name="edge",
-    )(part, tokens, west, east, north, south, west_ends, east_ends, qkv_weight, bias1, bias2, proj_weight, fc1_weight, fc2_weight,
+    )(part, tokens, west, east, north, south, nw, sw, ne, se, qkv_weight, bias1, bias2, proj_weight, fc1_weight, fc2_weight,
       g1, b1, valid, g2, b2)
 
 

time: 80.4 us -> 85.3 us (1.061)
  the two profiles are of different devices: /device:TPU:0 before, /device:TPU:25 now
where the time goes in v6:
time: 85.3 us; the launch traced here: 85.1 us
  Pallas kernels  53.8 us (63%)
  starting transfers between devices  19.2 us (23%)
  waiting for transfers between devices  7.17 us (8%)
  local copies, waits for them, and re-layouts  4.51 us (5%)
    pallas_call x1, Pallas kernels, per_device(): pl.pallas_call(edge_kernel, out_shape=jax.ShapeDtypeStruct(tokens.shape,...  32.5 us
    ppermute x8, starting transfers between devices, passed_along(): return lax.ppermute(block, axes if len(axes) > 1 else axes[0], route)  19.2 us
    pallas_call x1, Pallas kernels, per_device(): pl.pallas_call(inner_kernel, out_shape=jax.ShapeDtypeStruct(tokens.shape,...  19 us
    ppermute x8, waiting for transfers between devices, passed_along(): return lax.ppermute(block, axes if len(axes) > 1 else axes[0], route)  7.17 us
    pallas_call x1, Pallas kernels, per_device(): pl.pallas_call(functools.partial(prep_kernel, shape=shape), out_shape=[ja...  2.31 us
    slice x1, local copies, waits for them, and re-layouts, per_device(): east = passed_along(tokens[:, left], ('lon',), (-1,))  2.05 us
  transfers between devices with their start and end apart: 8, of which 1 were waited for; matrix products, arithmetic and copies ran while one was open for 4% of the time, Pallas kernels for 25%

profile of v6, /device:TPU:25, one launch (start us, length us, event | category | flops | bytes accessed | tf_op | source)
XLA Modules:
  0.0 85.1 jit_solution(87855201667184428)
XLA Ops:
  0.0 0.0 copy-start.4
  0.0 0.0 copy-start.5
  0.0 1.1 %fusion = (bf16[3,6,4,512]{3,2,1,0:T(4,128)(2,1)S(1)}, bf16[3,6,4,512]{3,2,1,0:T(4,128)(2,1)S(1)}, bf16[3,6,4,512]{3,2,1,0:T(4,128)(2,1)S(1)}, bf16[3,6,4,512]{3,2,1,0:T(4,128)(2,1)S(1)}) fusion(bf16[36,24,4,512]{3,2,1,0:T(4,128)(2,1)} %tok_hbm.3), kind=kLoop, calls=%fused_computation | loop fusion | bytes 589824 | tf_op jit(solution)/shard_map/slice | solution.py:405
  1.2 6.4 %collective-permute-start.7 = (bf16[3,6,4,512]{3,2,1,0:T(4,128)(2,1)S(1)}, bf16[3,6,4,512]{3,2,1,0:T(4,128)(2,1)S(1)}, u32[]{:S(2)}, u32[]{:S(2)}) collective-permute-start(bf16[3,6,4,512]{3,2,1,0:T(4,128)(2,1)S(1)} %get-tuple-element.11), channel_id=1, source_target_pairs={{9,0},{10,1},{11,2},{12,3},{13,4},{14,5},{15,6},{8,7},{17,8},{18,9... | collective-permute-start | bytes 221192 | tf_op jit(solution)/shard_map/ppermute | solution.py:389
  7.6 0.0 collective-permute-start.6
  7.6 5.1 %collective-permute-start.5 = (bf16[3,6,4,512]{3,2,1,0:T(4,128)(2,1)S(1)}, bf16[3,6,4,512]{3,2,1,0:T(4,128)(2,1)S(1)}, u32[]{:S(2)}, u32[]{:S(2)}) collective-permute-start(bf16[3,6,4,512]{3,2,1,0:T(4,128)(2,1)S(1)} %get-tuple-element.13), channel_id=1, source_target_pairs={{121,0},{122,1},{123,2},{124,3},{125,4},{126,5},{127,6},{120,7},{1... | collective-permute-start | bytes 221192 | tf_op jit(solution)/shard_map/ppermute | solution.py:389
  12.6 0.0 collective-permute-start.4
  12.6 1.3 %fusion.1 = (bf16[3,24,4,512]{3,2,1,0:T(4,128)(2,1)S(1)}, bf16[3,24,4,512]{3,2,1,0:T(4,128)(2,1)S(1)}) fusion(bf16[36,24,4,512]{3,2,1,0:T(4,128)(2,1)} %tok_hbm.3), kind=kLoop, calls=%fused_computation.1 | loop fusion | bytes 1179648 | tf_op jit(solution)/shard_map/slice | solution.py:398
  13.9 0.0 copy-start
  13.9 0.0 copy-start.1
  13.9 0.0 copy-start.2
  13.9 0.0 copy-start.3
  14.0 0.0 copy-start.6
  14.0 0.0 copy-start.7
  14.0 0.0 copy-start.8
  14.0 0.0 copy-start.9
  14.0 3.7 %collective-permute-start.3 = (bf16[3,24,4,512]{3,2,1,0:T(4,128)(2,1)S(1)}, bf16[3,24,4,512]{3,2,1,0:T(4,128)(2,1)S(1)}, u32[]{:S(2)}, u32[]{:S(2)}) collective-permute-start(bf16[3,24,4,512]{3,2,1,0:T(4,128)(2,1)S(1)} %get-tuple-element.15), channel_id=1, source_target_pairs={{1,0},{2,1},{3,2},{4,3},{5,4},{6,5},{7,6},{0,7},{9,8},{10,9},{11,1... | collective-permute-start | bytes 884744 | tf_op jit(solution)/shard_map/ppermute | solution.py:389
  17.7 2.0 %fusion.2 = (bf16[36,6,4,512]{3,2,1,0:T(4,128)(2,1)S(1)}, bf16[36,6,4,512]{3,2,1,0:T(4,128)(2,1)S(1)}) fusion(bf16[36,24,4,512]{3,2,1,0:T(4,128)(2,1)} %tok_hbm.3), kind=kLoop, calls=%fused_computation.2 | loop fusion | bytes 3538944 | tf_op jit(solution)/shard_map/slice | solution.py:400
  19.7 0.0 copy-done.4
  19.7 0.0 copy-done.5
  19.7 2.3 %prep.1 = (f32[8,144,144]{2,1,0:T(8,128)S(1)}, f32[8,144,144]{2,1,0:T(8,128)S(1)}, f32[21,1,144]{2,1,0:T(1,128)S(1)}) custom-call(f32[8,759]{1,0:T(8,128)S(1)} %copy-done.5, s32[288,384]{1,0:T(8,128)S(1)} %copy-done.4), custom_call_target="tpu_custom_call" | custom-call | flops 1000000000 | bytes 5000000 | tf_op jit(solution)/shard_map/prep/pallas_call | solution.py:411
  22.0 0.0 collective-permute-done.7.se_hbm
  22.0 0.1 collective-permute-start.2
  22.1 0.0 collective-permute-done.6.ne_hbm
  22.1 2.2 %collective-permute-start.1 = (bf16[36,6,4,512]{3,2,1,0:T(4,128)(2,1)S(1)}, bf16[36,6,4,512]{3,2,1,0:T(4,128)(2,1)S(1)}, u32[]{:S(2)}, u32[]{:S(2)}) collective-permute-start(bf16[36,6,4,512]{3,2,1,0:T(4,128)(2,1)S(1)} %get-tuple-element.17), channel_id=1, source_target_pairs={{8,0},{16,8},{24,16},{32,24},{40,32},{48,40},{56,48},{64,56},{72,6... | collective-permute-start | bytes 2654216 | tf_op jit(solution)/shard_map/ppermute | solution.py:389
  24.4 0.0 collective-permute-done.5.sw_hbm
  24.4 1.8 %collective-permute-start = (bf16[36,6,4,512]{3,2,1,0:T(4,128)(2,1)S(1)}, bf16[36,6,4,512]{3,2,1,0:T(4,128)(2,1)S(1)}, u32[]{:S(2)}, u32[]{:S(2)}) collective-permute-start(bf16[36,6,4,512]{3,2,1,0:T(4,128)(2,1)S(1)} %get-tuple-element.18), channel_id=1, source_target_pairs={{120,0},{0,8},{8,16},{16,24},{24,32},{32,40},{40,48},{48,56},{56,6... | collective-permute-start | bytes 2654216 | tf_op jit(solution)/shard_map/ppermute | solution.py:389
  26.2 0.0 copy-done
  26.2 0.0 copy-done.1
  26.2 0.0 copy-done.2
  26.2 0.0 copy-done.3
  26.2 0.0 copy-done.6
  26.2 0.0 copy-done.7
  26.2 0.0 copy-done.8
  26.2 0.0 copy-done.9
  26.2 19.0 %inner.1.part_hbm = bf16[36,24,4,512]{3,2,1,0:T(4,128)(2,1)} custom-call(bf16[36,24,4,512]{3,2,1,0:T(4,128)(2,1)} %tok_hbm.3, bf16[512,1536]{1,0:T(8,128)(2,1)S(1)} %copy-done.2, f32[8,144,144]{2,1,0:T(8,128)S(1)} %get-tuple-element.8.bias_hbm.bias1_hbm, bf16[512,512]{1,0:T(8,128)(2,1)S(1)} %copy-done.3, bf16[512,2048]{1,0:T(8,128)(2,1)S(1)} %copy-done, ...), custom_call_target="tpu_custom_call" | custom-call | flops 12000000000 | bytes 12000000 | tf_op jit(solution)/shard_map/inner/pallas_call | solution.py:428
  45.2 0.0 collective-permute-done.4.nw_hbm
  45.2 0.0 collective-permute-done.3.south_hbm
  45.3 0.0 collective-permute-done.2.north_hbm
  45.3 7.2 %collective-permute-done.1.east_hbm = bf16[36,6,4,512]{3,2,1,0:T(4,128)(2,1)S(1)} collective-permute-done((bf16[36,6,4,512]{3,2,1,0:T(4,128)(2,1)S(1)}, bf16[36,6,4,512]{3,2,1,0:T(4,128)(2,1)S(1)}, u32[]{:S(2)}, u32[]{:S(2)}) %collective-permute-start.1) | collective-permute-done | bytes 884768 | tf_op jit(solution)/shard_map/ppermute | solution.py:389
  52.4 0.0 collective-permute-done.west_hbm
  52.4 32.5 %edge.1 = bf16[36,24,4,512]{3,2,1,0:T(4,128)(2,1)} custom-call(bf16[36,24,4,512]{3,2,1,0:T(4,128)(2,1)} %inner.1.part_hbm, bf16[36,24,4,512]{3,2,1,0:T(4,128)(2,1)} %tok_hbm.3, bf16[36,6,4,512]{3,2,1,0:T(4,128)(2,1)S(1)} %collective-permute-done.west_hbm, ...), custom_call_target="tpu_custom_call", output_to_operand_aliasing={{}: (0, {})} | custom-call | flops 16000000000 | bytes 16000000 | tf_op jit(solution)/shard_map/edge/pallas_call | solution.py:445
Async XLA Ops:
  0.0 19.7 %copy-start.4 = (s32[288,384]{1,0:T(8,128)S(1)}, s32[288,384]{1,0:T(8,128)}, u32[]{:S(2)}) copy-start(s32[288,384]{1,0:T(8,128)} %mask_ref.1) | copy-start | bytes 1327108
  0.0 19.7 %copy-start.5 = (f32[8,759]{1,0:T(8,128)S(1)}, f32[8,759]{1,0:T(8,128)}, u32[]{:S(2)}) copy-start(f32[8,759]{1,0:T(8,128)} %table_ref.1) | copy-start | bytes 72868
  1.2 20.9 %collective-permute-start.7 = (bf16[3,6,4,512]{3,2,1,0:T(4,128)(2,1)S(1)}, bf16[3,6,4,512]{3,2,1,0:T(4,128)(2,1)S(1)}, u32[]{:S(2)}, u32[]{:S(2)}) collective-permute-start(bf16[3,6,4,512]{3,2,1,0:T(4,128)(2,1)S(1)} %get-tuple-element.11), channel_id=1, source_target_pairs={{9,0},{10,1},{11,2},{12,3},{13,4},{14,5},{15,6},{8,7},{17,8},{18,9... | collective-permute-start | bytes 221192 | tf_op jit(solution)/shard_map/ppermute | solution.py:389
  7.6 14.6 %collective-permute-start.6 = (bf16[3,6,4,512]{3,2,1,0:T(4,128)(2,1)S(1)}, bf16[3,6,4,512]{3,2,1,0:T(4,128)(2,1)S(1)}, u32[]{:S(2)}, u32[]{:S(2)}) collective-permute-start(bf16[3,6,4,512]{3,2,1,0:T(4,128)(2,1)S(1)} %get-tuple-element.12), channel_id=1, source_target_pairs={{15,0},{8,1},{9,2},{10,3},{11,4},{12,5},{13,6},{14,7},{23,8},{16,9... | collective-permute-start | bytes 221192 | tf_op jit(solution)/shard_map/ppermute | solution.py:389
  7.6 16.8 %collective-permute-start.5 = (bf16[3,6,4,512]{3,2,1,0:T(4,128)(2,1)S(1)}, bf16[3,6,4,512]{3,2,1,0:T(4,128)(2,1)S(1)}, u32[]{:S(2)}, u32[]{:S(2)}) collective-permute-start(bf16[3,6,4,512]{3,2,1,0:T(4,128)(2,1)S(1)} %get-tuple-element.13), channel_id=1, source_target_pairs={{121,0},{122,1},{123,2},{124,3},{125,4},{126,5},{127,6},{120,7},{1... | collective-permute-start | bytes 221192 | tf_op jit(solution)/shard_map/ppermute | solution.py:389
  12.6 32.6 %collective-permute-start.4 = (bf16[3,6,4,512]{3,2,1,0:T(4,128)(2,1)S(1)}, bf16[3,6,4,512]{3,2,1,0:T(4,128)(2,1)S(1)}, u32[]{:S(2)}, u32[]{:S(2)}) collective-permute-start(bf16[3,6,4,512]{3,2,1,0:T(4,128)(2,1)S(1)} %get-tuple-element.14), channel_id=1, source_target_pairs={{127,0},{120,1},{121,2},{122,3},{123,4},{124,5},{125,6},{126,7},{7... | collective-permute-start | bytes 221192 | tf_op jit(solution)/shard_map/ppermute | solution.py:389
  13.9 12.3 %copy-start = (bf16[512,2048]{1,0:T(8,128)(2,1)S(1)}, bf16[512,2048]{1,0:T(8,128)(2,1)}, u32[]{:S(2)}) copy-start(bf16[512,2048]{1,0:T(8,128)(2,1)} %fc1_hbm.3) | copy-start | bytes 6291460
  13.9 12.3 %copy-start.1 = (bf16[2048,512]{1,0:T(8,128)(2,1)S(1)}, bf16[2048,512]{1,0:T(8,128)(2,1)}, u32[]{:S(2)}) copy-start(bf16[2048,512]{1,0:T(8,128)(2,1)} %fc2_hbm.3) | copy-start | bytes 6291460
  13.9 12.2 %copy-start.2 = (bf16[512,1536]{1,0:T(8,128)(2,1)S(1)}, bf16[512,1536]{1,0:T(8,128)(2,1)}, u32[]{:S(2)}) copy-start(bf16[512,1536]{1,0:T(8,128)(2,1)} %qkv_hbm.3) | copy-start | bytes 4718596
  13.9 12.2 %copy-start.3 = (bf16[512,512]{1,0:T(8,128)(2,1)S(1)}, bf16[512,512]{1,0:T(8,128)(2,1)}, u32[]{:S(2)}) copy-start(bf16[512,512]{1,0:T(8,128)(2,1)} %proj_hbm.3) | copy-start | bytes 1572868
  14.0 12.2 %copy-start.6 = (f32[512]{0:T(512)S(1)}, f32[512]{0:T(512)}, u32[]{:S(2)}) copy-start(f32[512]{0:T(512)} %param.12) | copy-start | bytes 6148
  14.0 12.2 %copy-start.7 = (f32[512]{0:T(512)S(1)}, f32[512]{0:T(512)}, u32[]{:S(2)}) copy-start(f32[512]{0:T(512)} %param.13) | copy-start | bytes 6148
  14.0 12.2 %copy-start.8 = (f32[512]{0:T(512)S(1)}, f32[512]{0:T(512)}, u32[]{:S(2)}) copy-start(f32[512]{0:T(512)} %param.18) | copy-start | bytes 6148
  14.0 12.2 %copy-start.9 = (f32[512]{0:T(512)S(1)}, f32[512]{0:T(512)}, u32[]{:S(2)}) copy-start(f32[512]{0:T(512)} %param.19) | copy-start | bytes 6148
  14.0 31.2 %collective-permute-start.3 = (bf16[3,24,4,512]{3,2,1,0:T(4,128)(2,1)S(1)}, bf16[3,24,4,512]{3,2,1,0:T(4,128)(2,1)S(1)}, u32[]{:S(2)}, u32[]{:S(2)}) collective-permute-start(bf16[3,24,4,512]{3,2,1,0:T(4,128)(2,1)S(1)} %get-tuple-element.15), channel_id=1, source_target_pairs={{1,0},{2,1},{3,2},{4,3},{5,4},{6,5},{7,6},{0,7},{9,8},{10,9},{11,1... | collective-permute-start | bytes 884744 | tf_op jit(solution)/shard_map/ppermute | solution.py:389
  22.0 23.2 %collective-permute-start.2 = (bf16[3,24,4,512]{3,2,1,0:T(4,128)(2,1)S(1)}, bf16[3,24,4,512]{3,2,1,0:T(4,128)(2,1)S(1)}, u32[]{:S(2)}, u32[]{:S(2)}) collective-permute-start(bf16[3,24,4,512]{3,2,1,0:T(4,128)(2,1)S(1)} %get-tuple-element.16), channel_id=1, source_target_pairs={{7,0},{0,1},{1,2},{2,3},{3,4},{4,5},{5,6},{6,7},{15,8},{8,9},{9,10... | collective-permute-start | bytes 884744 | tf_op jit(solution)/shard_map/ppermute | solution.py:389
  22.1 30.3 %collective-permute-start.1 = (bf16[36,6,4,512]{3,2,1,0:T(4,128)(2,1)S(1)}, bf16[36,6,4,512]{3,2,1,0:T(4,128)(2,1)S(1)}, u32[]{:S(2)}, u32[]{:S(2)}) collective-permute-start(bf16[36,6,4,512]{3,2,1,0:T(4,128)(2,1)S(1)} %get-tuple-element.17), channel_id=1, source_target_pairs={{8,0},{16,8},{24,16},{32,24},{40,32},{48,40},{56,48},{64,56},{72,6... | collective-permute-start | bytes 2654216 | tf_op jit(solution)/shard_map/ppermute | solution.py:389
  24.4 28.0 %collective-permute-start = (bf16[36,6,4,512]{3,2,1,0:T(4,128)(2,1)S(1)}, bf16[36,6,4,512]{3,2,1,0:T(4,128)(2,1)S(1)}, u32[]{:S(2)}, u32[]{:S(2)}) collective-permute-start(bf16[36,6,4,512]{3,2,1,0:T(4,128)(2,1)S(1)} %get-tuple-element.18), channel_id=1, source_target_pairs={{120,0},{0,8},{8,16},{16,24},{24,32},{32,40},{40,48},{48,56},{56,6... | collective-permute-start | bytes 2654216 | tf_op jit(solution)/shard_map/ppermute | solution.py:389
